TPU v7x, 512 devices: a whole 4x8x8 slice. The times are simulated.
512 devices in a mesh: leaf: 512 (over z, x, y, core).
Axes of the slice: x: 4, y: 8, z: 8, core: 2. Of those that a mesh axis runs over, the one named last changes fastest.
Arguments:
- rhs: bfloat16 [256, 1048576], P(None, 'leaf'), may hold values from -6 to 6
- bases: bfloat16 [5, 128, 1048576], P(None, None, 'leaf'), may hold values from -13 to 13
- coupling: bfloat16 [5, 512, 128, 256], P(None, 'leaf'), may hold values from -1 to 1, as said below
Outputs:
- whitened: bfloat16 [256, 1048576], P(None, 'leaf')
Inputs may be any that keep to these rules, and one draw needn't show every extreme that they name: coupling[l, d] is the same for all devices d of one child block at level l, the aligned blocks of 512 // 2**(l+1) devices.
All inputs are finite; a program needn't handle non-finite values.
Results may differ from a plain program's by a relative error of at most 0.029.
Values may be sent and summed in bfloat16 or wider, within the bound.
No kernel may reach another device: no remote copies, remote signals or barrier semaphores. Data moves between devices by JAX's collectives and lax.ppermute only.
A program may use at most 64 MiB of HBM per device.

v0:
```python
import jax
import jax.numpy as jnp
from jax import lax
from jax.sharding import PartitionSpec as P

LEVELS = 5


def from_partner(block, axis, apart):
    count = lax.axis_size(axis)
    route = []
    for low in range(count):
        high = low | 1 << apart
        if high != low and high < count:
            route += [(low, high), (high, low)]
    return lax.ppermute(block, axis, route)


def on_device(rhs, bases, coupling):
    state = rhs.astype(jnp.float32)
    devices = lax.axis_size("leaf")
    myself = lax.axis_index("leaf")
    for level in reversed(range(LEVELS)):
        count = 2 ** (level + 1)
        group = devices // count
        depth = group.bit_length() - 1
        rounded = state.astype(jnp.bfloat16)
        basis = bases[level]
        local = lax.dot_general(
            rounded, basis, (((1,), (1,)), ((), ())), preferred_element_type=jnp.float32
        )
        child = myself >> depth
        bit_list = list(range(depth))
        total = local
        for bit in bit_list:
            total = total + from_partner(total.astype(jnp.bfloat16), "leaf", bit).astype(
                total.dtype
            )
        own_part = total.astype(jnp.bfloat16)
        sibling = from_partner(own_part, "leaf", depth)
        is_left = child & 1 == 0
        first_half = jnp.where(is_left, own_part, sibling)
        second_half = jnp.where(is_left, sibling, own_part)
        pair = jnp.concatenate([first_half, second_half], axis=1)
        corr = lax.dot_general(
            pair, coupling[level, 0], (((1,), (1,)), ((), ())), preferred_element_type=jnp.float32
        )
        corr = corr.astype(jnp.bfloat16)
        state = state - jnp.dot(corr, basis, preferred_element_type=jnp.float32)
    return state.astype(jnp.bfloat16)


def solution(mesh):
    return jax.shard_map(
        on_device,
        mesh=mesh,
        in_specs=(P(None, "leaf"), P(None, None, "leaf"), P(None, "leaf", None, None)),
        out_specs=P(None, "leaf"),
        check_vma=False,
    )
```

profile of v0, /device:TPU:6, one launch (start us, length us, event | category | flops | bytes accessed | tf_op | source)
XLA Modules:
  0.0 269.6 jit_solution(14116669417236732103)
XLA Ops:
  5.1 3.5 %collective-permute-start.1 = (bf16[256,128]{0,1:T(8,128)(2,1)S(1)}, bf16[256,128]{0,1:T(8,128)(2,1)S(1)}, u32[]{:S(2)}, u32[]{:S(2)}) collective-permute-start(bf16[256,128]{0,1:T(8,128)(2,1)S(1)} %fusion.60), channel_id=1, source_target_pairs={{0,2},{2,0},{1,3},{3,1},{4,6},{6,4},{5,7},{7,5},{8,10},{10,8},{9,1... | collective-permute-start | bytes 196616 | tf_op jit(solution)/shard_map/ppermute | solution.py:16
  11.3 4.5 %collective-permute-start.2 = (bf16[256,128]{0,1:T(8,128)(2,1)S(1)}, bf16[256,128]{0,1:T(8,128)(2,1)S(1)}, u32[]{:S(2)}, u32[]{:S(2)}) collective-permute-start(bf16[256,128]{0,1:T(8,128)(2,1)S(1)} %fusion.106), channel_id=1, source_target_pairs={{0,4},{4,0},{1,5},{5,1},{2,6},{6,2},{3,7},{7,3},{8,12},{12,8},{9,1... | collective-permute-start | bytes 196616 | tf_op jit(solution)/shard_map/ppermute | solution.py:16
  18.4 8.4 %collective-permute-start.3 = (bf16[256,128]{0,1:T(8,128)(2,1)S(1)}, bf16[256,128]{0,1:T(8,128)(2,1)S(1)}, u32[]{:S(2)}, u32[]{:S(2)}) collective-permute-start(bf16[256,128]{0,1:T(8,128)(2,1)S(1)} %fusion.61), channel_id=1, source_target_pairs={{0,8},{8,0},{1,9},{9,1},{2,10},{10,2},{3,11},{11,3},{4,12},{12,4},... | collective-permute-start | bytes 196616 | tf_op jit(solution)/shard_map/ppermute | solution.py:16
  32.6 3.4 %collective-permute-done.4 = bf16[256,128]{0,1:T(8,128)(2,1)S(1)} collective-permute-done((bf16[256,128]{0,1:T(8,128)(2,1)S(1)}, bf16[256,128]{0,1:T(8,128)(2,1)S(1)}, u32[]{:S(2)}, u32[]{:S(2)}) %collective-permute-start.4) | collective-permute-done | bytes 65568 | tf_op jit(solution)/shard_map/ppermute | solution.py:16
  45.9 3.6 %collective-permute-done.6 = bf16[256,128]{0,1:T(8,128)(2,1)S(1)} collective-permute-done((bf16[256,128]{0,1:T(8,128)(2,1)S(1)}, bf16[256,128]{0,1:T(8,128)(2,1)S(1)}, u32[]{:S(2)}, u32[]{:S(2)}) %collective-permute-start.6) | collective-permute-done | bytes 65568 | tf_op jit(solution)/shard_map/ppermute | solution.py:16
  49.6 3.5 %collective-permute-start.7 = (bf16[256,128]{0,1:T(8,128)(2,1)S(1)}, bf16[256,128]{0,1:T(8,128)(2,1)S(1)}, u32[]{:S(2)}, u32[]{:S(2)}) collective-permute-start(bf16[256,128]{0,1:T(8,128)(2,1)S(1)} %get-tuple-element.11), channel_id=1, source_target_pairs={{0,4},{4,0},{1,5},{5,1},{2,6},{6,2},{3,7},{7,3},{8,12},{12,8},{9,1... | collective-permute-start | bytes 196616 | tf_op jit(solution)/shard_map/ppermute | solution.py:16
  53.2 4.2 %collective-permute-done.7 = bf16[256,128]{0,1:T(8,128)(2,1)S(1)} collective-permute-done((bf16[256,128]{0,1:T(8,128)(2,1)S(1)}, bf16[256,128]{0,1:T(8,128)(2,1)S(1)}, u32[]{:S(2)}, u32[]{:S(2)}) %collective-permute-start.7) | collective-permute-done | bytes 65568 | tf_op jit(solution)/shard_map/ppermute | solution.py:16
  57.4 7.2 %collective-permute-start.8 = (bf16[256,128]{0,1:T(8,128)(2,1)S(1)}, bf16[256,128]{0,1:T(8,128)(2,1)S(1)}, u32[]{:S(2)}, u32[]{:S(2)}) collective-permute-start(bf16[256,128]{0,1:T(8,128)(2,1)S(1)} %fusion.63), channel_id=1, source_target_pairs={{0,8},{8,0},{1,9},{9,1},{2,10},{10,2},{3,11},{11,3},{4,12},{12,4},... | collective-permute-start | bytes 196616 | tf_op jit(solution)/shard_map/ppermute | solution.py:16
  70.2 3.4 %collective-permute-done.9 = bf16[256,128]{0,1:T(8,128)(2,1)S(1)} collective-permute-done((bf16[256,128]{0,1:T(8,128)(2,1)S(1)}, bf16[256,128]{0,1:T(8,128)(2,1)S(1)}, u32[]{:S(2)}, u32[]{:S(2)}) %collective-permute-start.9) | collective-permute-done | bytes 65568 | tf_op jit(solution)/shard_map/ppermute | solution.py:16
  73.7 6.1 %collective-permute-start.10 = (bf16[256,128]{0,1:T(8,128)(2,1)S(1)}, bf16[256,128]{0,1:T(8,128)(2,1)S(1)}, u32[]{:S(2)}, u32[]{:S(2)}) collective-permute-start(bf16[256,128]{0,1:T(8,128)(2,1)S(1)} %add_convert_fusion.3), channel_id=1, source_target_pairs={{0,32},{32,0},{1,33},{33,1},{2,34},{34,2},{3,35},{35,3},{4,36},{36... | collective-permute-start | bytes 196616 | tf_op jit(solution)/shard_map/ppermute | solution.py:16
  91.7 4.0 %collective-permute-done.12 = bf16[256,128]{0,1:T(8,128)(2,1)S(1)} collective-permute-done((bf16[256,128]{0,1:T(8,128)(2,1)S(1)}, bf16[256,128]{0,1:T(8,128)(2,1)S(1)}, u32[]{:S(2)}, u32[]{:S(2)}) %collective-permute-start.12) | collective-permute-done | bytes 65568 | tf_op jit(solution)/shard_map/ppermute | solution.py:16
  98.3 4.9 %collective-permute-done.13 = bf16[256,128]{0,1:T(8,128)(2,1)S(1)} collective-permute-done((bf16[256,128]{0,1:T(8,128)(2,1)S(1)}, bf16[256,128]{0,1:T(8,128)(2,1)S(1)}, u32[]{:S(2)}, u32[]{:S(2)}) %collective-permute-start.13) | collective-permute-done | bytes 65568 | tf_op jit(solution)/shard_map/ppermute | solution.py:16
  103.2 6.7 %collective-permute-start.14 = (bf16[256,128]{0,1:T(8,128)(2,1)S(1)}, bf16[256,128]{0,1:T(8,128)(2,1)S(1)}, u32[]{:S(2)}, u32[]{:S(2)}) collective-permute-start(bf16[256,128]{0,1:T(8,128)(2,1)S(1)} %fusion.65), channel_id=1, source_target_pairs={{0,8},{8,0},{1,9},{9,1},{2,10},{10,2},{3,11},{11,3},{4,12},{12,4},... | collective-permute-start | bytes 196616 | tf_op jit(solution)/shard_map/ppermute | solution.py:16
  109.9 3.4 %collective-permute-done.14 = bf16[256,128]{0,1:T(8,128)(2,1)S(1)} collective-permute-done((bf16[256,128]{0,1:T(8,128)(2,1)S(1)}, bf16[256,128]{0,1:T(8,128)(2,1)S(1)}, u32[]{:S(2)}, u32[]{:S(2)}) %collective-permute-start.14) | collective-permute-done | bytes 65568 | tf_op jit(solution)/shard_map/ppermute | solution.py:16
  113.3 3.7 %collective-permute-start.15 = (bf16[256,128]{0,1:T(8,128)(2,1)S(1)}, bf16[256,128]{0,1:T(8,128)(2,1)S(1)}, u32[]{:S(2)}, u32[]{:S(2)}) collective-permute-start(bf16[256,128]{0,1:T(8,128)(2,1)S(1)} %get-tuple-element.9), channel_id=1, source_target_pairs={{0,16},{16,0},{1,17},{17,1},{2,18},{18,2},{3,19},{19,3},{4,20},{20... | collective-permute-start | bytes 196616 | tf_op jit(solution)/shard_map/ppermute | solution.py:16
  119.5 5.8 %collective-permute-start.16 = (bf16[256,128]{0,1:T(8,128)(2,1)S(1)}, bf16[256,128]{0,1:T(8,128)(2,1)S(1)}, u32[]{:S(2)}, u32[]{:S(2)}) collective-permute-start(bf16[256,128]{0,1:T(8,128)(2,1)S(1)} %fusion.66), channel_id=1, source_target_pairs={{0,32},{32,0},{1,33},{33,1},{2,34},{34,2},{3,35},{35,3},{4,36},{36... | collective-permute-start | bytes 196616 | tf_op jit(solution)/shard_map/ppermute | solution.py:16
  127.6 4.3 %collective-permute-start.17 = (bf16[256,128]{0,1:T(8,128)(2,1)S(1)}, bf16[256,128]{0,1:T(8,128)(2,1)S(1)}, u32[]{:S(2)}, u32[]{:S(2)}) collective-permute-start(bf16[256,128]{0,1:T(8,128)(2,1)S(1)} %add_convert_fusion.2), channel_id=1, source_target_pairs={{0,64},{64,0},{1,65},{65,1},{2,66},{66,2},{3,67},{67,3},{4,68},{68... | collective-permute-start | bytes 196616 | tf_op jit(solution)/shard_map/ppermute | solution.py:16
  143.2 4.2 %collective-permute-done.19 = bf16[256,128]{0,1:T(8,128)(2,1)S(1)} collective-permute-done((bf16[256,128]{0,1:T(8,128)(2,1)S(1)}, bf16[256,128]{0,1:T(8,128)(2,1)S(1)}, u32[]{:S(2)}, u32[]{:S(2)}) %collective-permute-start.19) | collective-permute-done | bytes 65568 | tf_op jit(solution)/shard_map/ppermute | solution.py:16
  150.2 4.7 %collective-permute-done.20 = bf16[256,128]{0,1:T(8,128)(2,1)S(1)} collective-permute-done((bf16[256,128]{0,1:T(8,128)(2,1)S(1)}, bf16[256,128]{0,1:T(8,128)(2,1)S(1)}, u32[]{:S(2)}, u32[]{:S(2)}) %collective-permute-start.20) | collective-permute-done | bytes 65568 | tf_op jit(solution)/shard_map/ppermute | solution.py:16
  154.9 7.0 %collective-permute-start.21 = (bf16[256,128]{0,1:T(8,128)(2,1)S(1)}, bf16[256,128]{0,1:T(8,128)(2,1)S(1)}, u32[]{:S(2)}, u32[]{:S(2)}) collective-permute-start(bf16[256,128]{0,1:T(8,128)(2,1)S(1)} %fusion.68), channel_id=1, source_target_pairs={{0,8},{8,0},{1,9},{9,1},{2,10},{10,2},{3,11},{11,3},{4,12},{12,4},... | collective-permute-start | bytes 196616 | tf_op jit(solution)/shard_map/ppermute | solution.py:16
  168.1 3.3 %collective-permute-done.22 = bf16[256,128]{0,1:T(8,128)(2,1)S(1)} collective-permute-done((bf16[256,128]{0,1:T(8,128)(2,1)S(1)}, bf16[256,128]{0,1:T(8,128)(2,1)S(1)}, u32[]{:S(2)}, u32[]{:S(2)}) %collective-permute-start.22) | collective-permute-done | bytes 65568 | tf_op jit(solution)/shard_map/ppermute | solution.py:16
  171.4 5.2 %collective-permute-start.23 = (bf16[256,128]{0,1:T(8,128)(2,1)S(1)}, bf16[256,128]{0,1:T(8,128)(2,1)S(1)}, u32[]{:S(2)}, u32[]{:S(2)}) collective-permute-start(bf16[256,128]{0,1:T(8,128)(2,1)S(1)} %fusion.69), channel_id=1, source_target_pairs={{0,32},{32,0},{1,33},{33,1},{2,34},{34,2},{3,35},{35,3},{4,36},{36... | collective-permute-start | bytes 196616 | tf_op jit(solution)/shard_map/ppermute | solution.py:16
  179.1 3.9 %collective-permute-start.24 = (bf16[256,128]{0,1:T(8,128)(2,1)S(1)}, bf16[256,128]{0,1:T(8,128)(2,1)S(1)}, u32[]{:S(2)}, u32[]{:S(2)}) collective-permute-start(bf16[256,128]{0,1:T(8,128)(2,1)S(1)} %fusion.95), channel_id=1, source_target_pairs={{0,64},{64,0},{1,65},{65,1},{2,66},{66,2},{3,67},{67,3},{4,68},{68... | collective-permute-start | bytes 196616 | tf_op jit(solution)/shard_map/ppermute | solution.py:16
  185.3 6.5 %collective-permute-start.25 = (bf16[256,128]{0,1:T(8,128)(2,1)S(1)}, bf16[256,128]{0,1:T(8,128)(2,1)S(1)}, u32[]{:S(2)}, u32[]{:S(2)}) collective-permute-start(bf16[256,128]{0,1:T(8,128)(2,1)S(1)} %add_convert_fusion.1), channel_id=1, source_target_pairs={{0,128},{128,0},{1,129},{129,1},{2,130},{130,2},{3,131},{131,3},{4... | collective-permute-start | bytes 196616 | tf_op jit(solution)/shard_map/ppermute | solution.py:16
  204.7 4.0 %collective-permute-done.27 = bf16[256,128]{0,1:T(8,128)(2,1)S(1)} collective-permute-done((bf16[256,128]{0,1:T(8,128)(2,1)S(1)}, bf16[256,128]{0,1:T(8,128)(2,1)S(1)}, u32[]{:S(2)}, u32[]{:S(2)}) %collective-permute-start.27) | collective-permute-done | bytes 65568 | tf_op jit(solution)/shard_map/ppermute | solution.py:16
  212.0 4.2 %collective-permute-done.28 = bf16[256,128]{0,1:T(8,128)(2,1)S(1)} collective-permute-done((bf16[256,128]{0,1:T(8,128)(2,1)S(1)}, bf16[256,128]{0,1:T(8,128)(2,1)S(1)}, u32[]{:S(2)}, u32[]{:S(2)}) %collective-permute-start.28) | collective-permute-done | bytes 65568 | tf_op jit(solution)/shard_map/ppermute | solution.py:16
  216.3 7.0 %collective-permute-start.29 = (bf16[256,128]{0,1:T(8,128)(2,1)S(1)}, bf16[256,128]{0,1:T(8,128)(2,1)S(1)}, u32[]{:S(2)}, u32[]{:S(2)}) collective-permute-start(bf16[256,128]{0,1:T(8,128)(2,1)S(1)} %fusion.71), channel_id=1, source_target_pairs={{0,8},{8,0},{1,9},{9,1},{2,10},{10,2},{3,11},{11,3},{4,12},{12,4},... | collective-permute-start | bytes 196616 | tf_op jit(solution)/shard_map/ppermute | solution.py:16
  228.8 3.9 %collective-permute-done.30 = bf16[256,128]{0,1:T(8,128)(2,1)S(1)} collective-permute-done((bf16[256,128]{0,1:T(8,128)(2,1)S(1)}, bf16[256,128]{0,1:T(8,128)(2,1)S(1)}, u32[]{:S(2)}, u32[]{:S(2)}) %collective-permute-start.30) | collective-permute-done | bytes 65568 | tf_op jit(solution)/shard_map/ppermute | solution.py:16
  232.7 4.7 %collective-permute-start.31 = (bf16[256,128]{0,1:T(8,128)(2,1)S(1)}, bf16[256,128]{0,1:T(8,128)(2,1)S(1)}, u32[]{:S(2)}, u32[]{:S(2)}) collective-permute-start(bf16[256,128]{0,1:T(8,128)(2,1)S(1)} %fusion.72), channel_id=1, source_target_pairs={{0,32},{32,0},{1,33},{33,1},{2,34},{34,2},{3,35},{35,3},{4,36},{36... | collective-permute-start | bytes 196616 | tf_op jit(solution)/shard_map/ppermute | solution.py:16
  240.4 5.0 %collective-permute-start.32 = (bf16[256,128]{0,1:T(8,128)(2,1)S(1)}, bf16[256,128]{0,1:T(8,128)(2,1)S(1)}, u32[]{:S(2)}, u32[]{:S(2)}) collective-permute-start(bf16[256,128]{0,1:T(8,128)(2,1)S(1)} %fusion.110), channel_id=1, source_target_pairs={{0,64},{64,0},{1,65},{65,1},{2,66},{66,2},{3,67},{67,3},{4,68},{68... | collective-permute-start | bytes 196616 | tf_op jit(solution)/shard_map/ppermute | solution.py:16
  247.8 4.2 %collective-permute-start.33 = (bf16[256,128]{0,1:T(8,128)(2,1)S(1)}, bf16[256,128]{0,1:T(8,128)(2,1)S(1)}, u32[]{:S(2)}, u32[]{:S(2)}) collective-permute-start(bf16[256,128]{0,1:T(8,128)(2,1)S(1)} %fusion.73), channel_id=1, source_target_pairs={{0,128},{128,0},{1,129},{129,1},{2,130},{130,2},{3,131},{131,3},{4... | collective-permute-start | bytes 196616 | tf_op jit(solution)/shard_map/ppermute | solution.py:16
  254.9 9.7 %collective-permute-start.34 = (bf16[256,128]{0,1:T(8,128)(2,1)S(1)}, bf16[256,128]{0,1:T(8,128)(2,1)S(1)}, u32[]{:S(2)}, u32[]{:S(2)}) collective-permute-start(bf16[256,128]{0,1:T(8,128)(2,1)S(1)} %add_convert_fusion), channel_id=1, source_target_pairs={{0,256},{256,0},{1,257},{257,1},{2,258},{258,2},{3,259},{259,3},{4... | collective-permute-start | bytes 196616 | tf_op jit(solution)/shard_map/ppermute | solution.py:16
  (93 shorter events, 110.7 us)
Async XLA Ops:
  2.0 3.1 %collective-permute-start = (bf16[256,128]{0,1:T(8,128)(2,1)S(1)}, bf16[256,128]{0,1:T(8,128)(2,1)S(1)}, u32[]{:S(2)}, u32[]{:S(2)}) collective-permute-start(bf16[256,128]{0,1:T(8,128)(2,1)S(1)} %get-tuple-element.23), channel_id=1, source_target_pairs={{0,1},{1,0},{2,3},{3,2},{4,5},{5,4},{6,7},{7,6},{8,9},{9,8},{10,11... | collective-permute-start | bytes 196616 | tf_op jit(solution)/shard_map/ppermute | solution.py:16
  5.1 6.2 %collective-permute-start.1 = (bf16[256,128]{0,1:T(8,128)(2,1)S(1)}, bf16[256,128]{0,1:T(8,128)(2,1)S(1)}, u32[]{:S(2)}, u32[]{:S(2)}) collective-permute-start(bf16[256,128]{0,1:T(8,128)(2,1)S(1)} %fusion.60), channel_id=1, source_target_pairs={{0,2},{2,0},{1,3},{3,1},{4,6},{6,4},{5,7},{7,5},{8,10},{10,8},{9,1... | collective-permute-start | bytes 196616 | tf_op jit(solution)/shard_map/ppermute | solution.py:16
  11.3 7.1 %collective-permute-start.2 = (bf16[256,128]{0,1:T(8,128)(2,1)S(1)}, bf16[256,128]{0,1:T(8,128)(2,1)S(1)}, u32[]{:S(2)}, u32[]{:S(2)}) collective-permute-start(bf16[256,128]{0,1:T(8,128)(2,1)S(1)} %fusion.106), channel_id=1, source_target_pairs={{0,4},{4,0},{1,5},{5,1},{2,6},{6,2},{3,7},{7,3},{8,12},{12,8},{9,1... | collective-permute-start | bytes 196616 | tf_op jit(solution)/shard_map/ppermute | solution.py:16
  18.4 11.3 %collective-permute-start.3 = (bf16[256,128]{0,1:T(8,128)(2,1)S(1)}, bf16[256,128]{0,1:T(8,128)(2,1)S(1)}, u32[]{:S(2)}, u32[]{:S(2)}) collective-permute-start(bf16[256,128]{0,1:T(8,128)(2,1)S(1)} %fusion.61), channel_id=1, source_target_pairs={{0,8},{8,0},{1,9},{9,1},{2,10},{10,2},{3,11},{11,3},{4,12},{12,4},... | collective-permute-start | bytes 196616 | tf_op jit(solution)/shard_map/ppermute | solution.py:16
  29.8 6.2 %collective-permute-start.4 = (bf16[256,128]{0,1:T(8,128)(2,1)S(1)}, bf16[256,128]{0,1:T(8,128)(2,1)S(1)}, u32[]{:S(2)}, u32[]{:S(2)}) collective-permute-start(bf16[256,128]{0,1:T(8,128)(2,1)S(1)} %add_convert_fusion.4), channel_id=1, source_target_pairs={{0,16},{16,0},{1,17},{17,1},{2,18},{18,2},{3,19},{19,3},{4,20},{20... | collective-permute-start | bytes 196616 | tf_op jit(solution)/shard_map/ppermute | solution.py:16
  43.4 6.2 %collective-permute-start.6 = (bf16[256,128]{0,1:T(8,128)(2,1)S(1)}, bf16[256,128]{0,1:T(8,128)(2,1)S(1)}, u32[]{:S(2)}, u32[]{:S(2)}) collective-permute-start(bf16[256,128]{0,1:T(8,128)(2,1)S(1)} %fusion.62), channel_id=1, source_target_pairs={{0,2},{2,0},{1,3},{3,1},{4,6},{6,4},{5,7},{7,5},{8,10},{10,8},{9,1... | collective-permute-start | bytes 196616 | tf_op jit(solution)/shard_map/ppermute | solution.py:16
  49.6 7.8 %collective-permute-start.7 = (bf16[256,128]{0,1:T(8,128)(2,1)S(1)}, bf16[256,128]{0,1:T(8,128)(2,1)S(1)}, u32[]{:S(2)}, u32[]{:S(2)}) collective-permute-start(bf16[256,128]{0,1:T(8,128)(2,1)S(1)} %get-tuple-element.11), channel_id=1, source_target_pairs={{0,4},{4,0},{1,5},{5,1},{2,6},{6,2},{3,7},{7,3},{8,12},{12,8},{9,1... | collective-permute-start | bytes 196616 | tf_op jit(solution)/shard_map/ppermute | solution.py:16
  57.4 10.1 %collective-permute-start.8 = (bf16[256,128]{0,1:T(8,128)(2,1)S(1)}, bf16[256,128]{0,1:T(8,128)(2,1)S(1)}, u32[]{:S(2)}, u32[]{:S(2)}) collective-permute-start(bf16[256,128]{0,1:T(8,128)(2,1)S(1)} %fusion.63), channel_id=1, source_target_pairs={{0,8},{8,0},{1,9},{9,1},{2,10},{10,2},{3,11},{11,3},{4,12},{12,4},... | collective-permute-start | bytes 196616 | tf_op jit(solution)/shard_map/ppermute | solution.py:16
  67.5 6.2 %collective-permute-start.9 = (bf16[256,128]{0,1:T(8,128)(2,1)S(1)}, bf16[256,128]{0,1:T(8,128)(2,1)S(1)}, u32[]{:S(2)}, u32[]{:S(2)}) collective-permute-start(bf16[256,128]{0,1:T(8,128)(2,1)S(1)} %fusion.94), channel_id=1, source_target_pairs={{0,16},{16,0},{1,17},{17,1},{2,18},{18,2},{3,19},{19,3},{4,20},{20... | collective-permute-start | bytes 196616 | tf_op jit(solution)/shard_map/ppermute | solution.py:16
  73.7 8.3 %collective-permute-start.10 = (bf16[256,128]{0,1:T(8,128)(2,1)S(1)}, bf16[256,128]{0,1:T(8,128)(2,1)S(1)}, u32[]{:S(2)}, u32[]{:S(2)}) collective-permute-start(bf16[256,128]{0,1:T(8,128)(2,1)S(1)} %add_convert_fusion.3), channel_id=1, source_target_pairs={{0,32},{32,0},{1,33},{33,1},{2,34},{34,2},{3,35},{35,3},{4,36},{36... | collective-permute-start | bytes 196616 | tf_op jit(solution)/shard_map/ppermute | solution.py:16
  89.5 6.2 %collective-permute-start.12 = (bf16[256,128]{0,1:T(8,128)(2,1)S(1)}, bf16[256,128]{0,1:T(8,128)(2,1)S(1)}, u32[]{:S(2)}, u32[]{:S(2)}) collective-permute-start(bf16[256,128]{0,1:T(8,128)(2,1)S(1)} %fusion.64), channel_id=1, source_target_pairs={{0,2},{2,0},{1,3},{3,1},{4,6},{6,4},{5,7},{7,5},{8,10},{10,8},{9,1... | collective-permute-start | bytes 196616 | tf_op jit(solution)/shard_map/ppermute | solution.py:16
  95.7 7.4 %collective-permute-start.13 = (bf16[256,128]{0,1:T(8,128)(2,1)S(1)}, bf16[256,128]{0,1:T(8,128)(2,1)S(1)}, u32[]{:S(2)}, u32[]{:S(2)}) collective-permute-start(bf16[256,128]{0,1:T(8,128)(2,1)S(1)} %fusion.107), channel_id=1, source_target_pairs={{0,4},{4,0},{1,5},{5,1},{2,6},{6,2},{3,7},{7,3},{8,12},{12,8},{9,1... | collective-permute-start | bytes 196616 | tf_op jit(solution)/shard_map/ppermute | solution.py:16
  103.2 10.1 %collective-permute-start.14 = (bf16[256,128]{0,1:T(8,128)(2,1)S(1)}, bf16[256,128]{0,1:T(8,128)(2,1)S(1)}, u32[]{:S(2)}, u32[]{:S(2)}) collective-permute-start(bf16[256,128]{0,1:T(8,128)(2,1)S(1)} %fusion.65), channel_id=1, source_target_pairs={{0,8},{8,0},{1,9},{9,1},{2,10},{10,2},{3,11},{11,3},{4,12},{12,4},... | collective-permute-start | bytes 196616 | tf_op jit(solution)/shard_map/ppermute | solution.py:16
  113.3 6.2 %collective-permute-start.15 = (bf16[256,128]{0,1:T(8,128)(2,1)S(1)}, bf16[256,128]{0,1:T(8,128)(2,1)S(1)}, u32[]{:S(2)}, u32[]{:S(2)}) collective-permute-start(bf16[256,128]{0,1:T(8,128)(2,1)S(1)} %get-tuple-element.9), channel_id=1, source_target_pairs={{0,16},{16,0},{1,17},{17,1},{2,18},{18,2},{3,19},{19,3},{4,20},{20... | collective-permute-start | bytes 196616 | tf_op jit(solution)/shard_map/ppermute | solution.py:16
  119.5 8.1 %collective-permute-start.16 = (bf16[256,128]{0,1:T(8,128)(2,1)S(1)}, bf16[256,128]{0,1:T(8,128)(2,1)S(1)}, u32[]{:S(2)}, u32[]{:S(2)}) collective-permute-start(bf16[256,128]{0,1:T(8,128)(2,1)S(1)} %fusion.66), channel_id=1, source_target_pairs={{0,32},{32,0},{1,33},{33,1},{2,34},{34,2},{3,35},{35,3},{4,36},{36... | collective-permute-start | bytes 196616 | tf_op jit(solution)/shard_map/ppermute | solution.py:16
  127.6 6.6 %collective-permute-start.17 = (bf16[256,128]{0,1:T(8,128)(2,1)S(1)}, bf16[256,128]{0,1:T(8,128)(2,1)S(1)}, u32[]{:S(2)}, u32[]{:S(2)}) collective-permute-start(bf16[256,128]{0,1:T(8,128)(2,1)S(1)} %add_convert_fusion.2), channel_id=1, source_target_pairs={{0,64},{64,0},{1,65},{65,1},{2,66},{66,2},{3,67},{67,3},{4,68},{68... | collective-permute-start | bytes 196616 | tf_op jit(solution)/shard_map/ppermute | solution.py:16
  141.3 6.2 %collective-permute-start.19 = (bf16[256,128]{0,1:T(8,128)(2,1)S(1)}, bf16[256,128]{0,1:T(8,128)(2,1)S(1)}, u32[]{:S(2)}, u32[]{:S(2)}) collective-permute-start(bf16[256,128]{0,1:T(8,128)(2,1)S(1)} %fusion.67), channel_id=1, source_target_pairs={{0,2},{2,0},{1,3},{3,1},{4,6},{6,4},{5,7},{7,5},{8,10},{10,8},{9,1... | collective-permute-start | bytes 196616 | tf_op jit(solution)/shard_map/ppermute | solution.py:16
  147.5 7.4 %collective-permute-start.20 = (bf16[256,128]{0,1:T(8,128)(2,1)S(1)}, bf16[256,128]{0,1:T(8,128)(2,1)S(1)}, u32[]{:S(2)}, u32[]{:S(2)}) collective-permute-start(bf16[256,128]{0,1:T(8,128)(2,1)S(1)} %fusion.108), channel_id=1, source_target_pairs={{0,4},{4,0},{1,5},{5,1},{2,6},{6,2},{3,7},{7,3},{8,12},{12,8},{9,1... | collective-permute-start | bytes 196616 | tf_op jit(solution)/shard_map/ppermute | solution.py:16
  154.9 10.3 %collective-permute-start.21 = (bf16[256,128]{0,1:T(8,128)(2,1)S(1)}, bf16[256,128]{0,1:T(8,128)(2,1)S(1)}, u32[]{:S(2)}, u32[]{:S(2)}) collective-permute-start(bf16[256,128]{0,1:T(8,128)(2,1)S(1)} %fusion.68), channel_id=1, source_target_pairs={{0,8},{8,0},{1,9},{9,1},{2,10},{10,2},{3,11},{11,3},{4,12},{12,4},... | collective-permute-start | bytes 196616 | tf_op jit(solution)/shard_map/ppermute | solution.py:16
  165.3 6.2 %collective-permute-start.22 = (bf16[256,128]{0,1:T(8,128)(2,1)S(1)}, bf16[256,128]{0,1:T(8,128)(2,1)S(1)}, u32[]{:S(2)}, u32[]{:S(2)}) collective-permute-start(bf16[256,128]{0,1:T(8,128)(2,1)S(1)} %get-tuple-element.7), channel_id=1, source_target_pairs={{0,16},{16,0},{1,17},{17,1},{2,18},{18,2},{3,19},{19,3},{4,20},{20... | collective-permute-start | bytes 196616 | tf_op jit(solution)/shard_map/ppermute | solution.py:16
  171.4 7.7 %collective-permute-start.23 = (bf16[256,128]{0,1:T(8,128)(2,1)S(1)}, bf16[256,128]{0,1:T(8,128)(2,1)S(1)}, u32[]{:S(2)}, u32[]{:S(2)}) collective-permute-start(bf16[256,128]{0,1:T(8,128)(2,1)S(1)} %fusion.69), channel_id=1, source_target_pairs={{0,32},{32,0},{1,33},{33,1},{2,34},{34,2},{3,35},{35,3},{4,36},{36... | collective-permute-start | bytes 196616 | tf_op jit(solution)/shard_map/ppermute | solution.py:16
  179.1 6.2 %collective-permute-start.24 = (bf16[256,128]{0,1:T(8,128)(2,1)S(1)}, bf16[256,128]{0,1:T(8,128)(2,1)S(1)}, u32[]{:S(2)}, u32[]{:S(2)}) collective-permute-start(bf16[256,128]{0,1:T(8,128)(2,1)S(1)} %fusion.95), channel_id=1, source_target_pairs={{0,64},{64,0},{1,65},{65,1},{2,66},{66,2},{3,67},{67,3},{4,68},{68... | collective-permute-start | bytes 196616 | tf_op jit(solution)/shard_map/ppermute | solution.py:16
  185.3 8.8 %collective-permute-start.25 = (bf16[256,128]{0,1:T(8,128)(2,1)S(1)}, bf16[256,128]{0,1:T(8,128)(2,1)S(1)}, u32[]{:S(2)}, u32[]{:S(2)}) collective-permute-start(bf16[256,128]{0,1:T(8,128)(2,1)S(1)} %add_convert_fusion.1), channel_id=1, source_target_pairs={{0,128},{128,0},{1,129},{129,1},{2,130},{130,2},{3,131},{131,3},{4... | collective-permute-start | bytes 196616 | tf_op jit(solution)/shard_map/ppermute | solution.py:16
  199.3 3.3 %collective-permute-start.26 = (bf16[256,128]{0,1:T(8,128)(2,1)S(1)}, bf16[256,128]{0,1:T(8,128)(2,1)S(1)}, u32[]{:S(2)}, u32[]{:S(2)}) collective-permute-start(bf16[256,128]{0,1:T(8,128)(2,1)S(1)} %get-tuple-element.31), channel_id=1, source_target_pairs={{0,1},{1,0},{2,3},{3,2},{4,5},{5,4},{6,7},{7,6},{8,9},{9,8},{10,11... | collective-permute-start | bytes 196616 | tf_op jit(solution)/shard_map/ppermute | solution.py:16
  202.6 6.2 %collective-permute-start.27 = (bf16[256,128]{0,1:T(8,128)(2,1)S(1)}, bf16[256,128]{0,1:T(8,128)(2,1)S(1)}, u32[]{:S(2)}, u32[]{:S(2)}) collective-permute-start(bf16[256,128]{0,1:T(8,128)(2,1)S(1)} %fusion.70), channel_id=1, source_target_pairs={{0,2},{2,0},{1,3},{3,1},{4,6},{6,4},{5,7},{7,5},{8,10},{10,8},{9,1... | collective-permute-start | bytes 196616 | tf_op jit(solution)/shard_map/ppermute | solution.py:16
  208.8 7.5 %collective-permute-start.28 = (bf16[256,128]{0,1:T(8,128)(2,1)S(1)}, bf16[256,128]{0,1:T(8,128)(2,1)S(1)}, u32[]{:S(2)}, u32[]{:S(2)}) collective-permute-start(bf16[256,128]{0,1:T(8,128)(2,1)S(1)} %fusion.109), channel_id=1, source_target_pairs={{0,4},{4,0},{1,5},{5,1},{2,6},{6,2},{3,7},{7,3},{8,12},{12,8},{9,1... | collective-permute-start | bytes 196616 | tf_op jit(solution)/shard_map/ppermute | solution.py:16
  216.3 10.2 %collective-permute-start.29 = (bf16[256,128]{0,1:T(8,128)(2,1)S(1)}, bf16[256,128]{0,1:T(8,128)(2,1)S(1)}, u32[]{:S(2)}, u32[]{:S(2)}) collective-permute-start(bf16[256,128]{0,1:T(8,128)(2,1)S(1)} %fusion.71), channel_id=1, source_target_pairs={{0,8},{8,0},{1,9},{9,1},{2,10},{10,2},{3,11},{11,3},{4,12},{12,4},... | collective-permute-start | bytes 196616 | tf_op jit(solution)/shard_map/ppermute | solution.py:16
  226.6 6.2 %collective-permute-start.30 = (bf16[256,128]{0,1:T(8,128)(2,1)S(1)}, bf16[256,128]{0,1:T(8,128)(2,1)S(1)}, u32[]{:S(2)}, u32[]{:S(2)}) collective-permute-start(bf16[256,128]{0,1:T(8,128)(2,1)S(1)} %get-tuple-element.5), channel_id=1, source_target_pairs={{0,16},{16,0},{1,17},{17,1},{2,18},{18,2},{3,19},{19,3},{4,20},{20... | collective-permute-start | bytes 196616 | tf_op jit(solution)/shard_map/ppermute | solution.py:16
  232.7 7.7 %collective-permute-start.31 = (bf16[256,128]{0,1:T(8,128)(2,1)S(1)}, bf16[256,128]{0,1:T(8,128)(2,1)S(1)}, u32[]{:S(2)}, u32[]{:S(2)}) collective-permute-start(bf16[256,128]{0,1:T(8,128)(2,1)S(1)} %fusion.72), channel_id=1, source_target_pairs={{0,32},{32,0},{1,33},{33,1},{2,34},{34,2},{3,35},{35,3},{4,36},{36... | collective-permute-start | bytes 196616 | tf_op jit(solution)/shard_map/ppermute | solution.py:16
  240.4 7.4 %collective-permute-start.32 = (bf16[256,128]{0,1:T(8,128)(2,1)S(1)}, bf16[256,128]{0,1:T(8,128)(2,1)S(1)}, u32[]{:S(2)}, u32[]{:S(2)}) collective-permute-start(bf16[256,128]{0,1:T(8,128)(2,1)S(1)} %fusion.110), channel_id=1, source_target_pairs={{0,64},{64,0},{1,65},{65,1},{2,66},{66,2},{3,67},{67,3},{4,68},{68... | collective-permute-start | bytes 196616 | tf_op jit(solution)/shard_map/ppermute | solution.py:16
  247.8 7.1 %collective-permute-start.33 = (bf16[256,128]{0,1:T(8,128)(2,1)S(1)}, bf16[256,128]{0,1:T(8,128)(2,1)S(1)}, u32[]{:S(2)}, u32[]{:S(2)}) collective-permute-start(bf16[256,128]{0,1:T(8,128)(2,1)S(1)} %fusion.73), channel_id=1, source_target_pairs={{0,128},{128,0},{1,129},{129,1},{2,130},{130,2},{3,131},{131,3},{4... | collective-permute-start | bytes 196616 | tf_op jit(solution)/shard_map/ppermute | solution.py:16
  254.9 12.0 %collective-permute-start.34 = (bf16[256,128]{0,1:T(8,128)(2,1)S(1)}, bf16[256,128]{0,1:T(8,128)(2,1)S(1)}, u32[]{:S(2)}, u32[]{:S(2)}) collective-permute-start(bf16[256,128]{0,1:T(8,128)(2,1)S(1)} %add_convert_fusion), channel_id=1, source_target_pairs={{0,256},{256,0},{1,257},{257,1},{2,258},{258,2},{3,259},{259,3},{4... | collective-permute-start | bytes 196616 | tf_op jit(solution)/shard_map/ppermute | solution.py:16
  (8 other events, 214.6 us)
where the time goes:
time: 271 us; the launch traced here: 270 us
  starting transfers between devices  144 us (53%)
  waiting for transfers between devices  101 us (37%)
  matrix products  21.7 us (8%)
    ppermute x35, starting transfers between devices, from_partner(): return lax.ppermute(block, axis, route)  144 us
    ppermute x35, waiting for transfers between devices, from_partner(): return lax.ppermute(block, axis, route)  101 us
    dot_general x5, matrix products, on_device(): state = state - jnp.dot(corr, basis, preferred_element_type=jnp.float32)  12.2 us
    dot_general x5, matrix products, on_device(): lax.dot_general(rounded, basis, (((1,), (1,)), ((), ())), preferred_eleme...  9.46 us
  transfers between devices with their start and end apart: 35, of which 35 were waited for; matrix products, arithmetic and copies ran while one was open for 0% of the time, Pallas kernels for 0%

commit v1 on v0

v1 whole, which is shorter than its diff:
```python
import functools

import jax
import jax.numpy as jnp
from jax import lax
from jax.experimental import pallas as pl
from jax.experimental.pallas import tpu as pltpu
from jax.sharding import Mesh
from jax.sharding import PartitionSpec as P


ROWS = 16
PIECES = 5
R = 128
STEPS = 4
F32 = jnp.float32
BF16 = jnp.bfloat16
VMEM_LIMIT = 40 * 1024 * 1024


def dot_t(a, b):
    return lax.dot_general(a, b, (((1,), (1,)), ((), ())), preferred_element_type=F32)


def dot(a, b):
    return jnp.dot(a, b, preferred_element_type=F32)


def project_kernel(rhs, bases, out, acc_p, acc_a, acc_b, acc_c, acc_d):
    step = pl.program_id(0)

    @pl.when(step == 0)
    def _():
        for acc in (acc_p, acc_a, acc_b, acc_c, acc_d):
            acc[...] = jnp.zeros_like(acc)

    width = rhs.shape[1]
    everything = bases[...].reshape(5 * R, width)
    acc_p[...] += dot_t(rhs[...], everything)
    acc_a[...] += dot_t(everything[: 3 * R], everything[3 * R :])
    acc_b[...] += dot_t(everything[:R], everything[R : 3 * R])
    acc_c[...] += dot_t(everything[3 * R : 4 * R], everything[4 * R :])
    acc_d[...] += dot_t(everything[R : 2 * R], everything[2 * R : 3 * R])

    @pl.when(step == STEPS - 1)
    def _():
        def put(position, value):
            out[:, ROWS * position : ROWS * (position + 1), :] = value.astype(BF16).reshape(16, ROWS, R)

        for level in range(5):
            put(level, acc_p[:, R * level : R * (level + 1)])
        put(5, acc_a[: 2 * R, R:])
        put(6, jnp.concatenate([acc_a[2 * R :, R:], acc_c[...]], axis=0))
        put(7, acc_a[: 2 * R, :R])
        put(8, jnp.concatenate([acc_b[:, R:], acc_d[...]], axis=0))
        put(9, jnp.concatenate([acc_a[2 * R :, :R], acc_b[:, :R]], axis=0))


def project(rhs, bases):
    width = rhs.shape[1] // STEPS
    return pl.pallas_call(
        project_kernel,
        grid=(STEPS,),
        in_specs=[
            pl.BlockSpec((256, width), lambda i: (0, i)),
            pl.BlockSpec((5, R, width), lambda i: (0, 0, i)),
        ],
        out_specs=pl.BlockSpec((16, 10 * ROWS, R), lambda i: (0, 0, 0)),
        out_shape=jax.ShapeDtypeStruct((16, 10 * ROWS, R), BF16),
        scratch_shapes=[
            pltpu.VMEM((256, 5 * R), F32),
            pltpu.VMEM((3 * R, 2 * R), F32),
            pltpu.VMEM((R, 2 * R), F32),
            pltpu.VMEM((R, R), F32),
            pltpu.VMEM((R, R), F32),
        ],
        compiler_params=pltpu.CompilerParams(vmem_limit_bytes=VMEM_LIMIT),
    )(rhs, bases)


def local_call(kernel, place, shape, *arrays):
    whole = pl.BlockSpec(memory_space=pltpu.VMEM)
    return pl.pallas_call(
        kernel,
        in_specs=[pl.BlockSpec(memory_space=pltpu.SMEM)] + [whole] * len(arrays),
        out_specs=whole,
        out_shape=jax.ShapeDtypeStruct(shape, BF16),
        compiler_params=pltpu.CompilerParams(vmem_limit_bytes=VMEM_LIMIT),
    )(place, *arrays)


def couple_kernel(place, parts, coupling, out):
    total = parts[0].astype(F32)
    for source in range(1, 16):
        total += parts[source].astype(F32)
    total = total.astype(BF16)
    proj, gram = total[: 5 * ROWS], total[5 * ROWS :]
    first = dot(gram[: 2 * ROWS], coupling[4, 0])
    second = dot(gram[2 * ROWS : 3 * ROWS], coupling[3, 0])
    third = dot(gram[3 * ROWS : 4 * ROWS], coupling[2, 0])
    last = gram[4 * ROWS :]
    fourth = jnp.where(place[3] < 8, dot(last, coupling[3, 0]), dot(last, coupling[1, 0]))
    mixed = [first[:ROWS], first[ROWS:], second, third, fourth]
    halves = [m[:, R * half : R * (half + 1)].astype(BF16) for m in mixed for half in (0, 1)]
    whole = jnp.concatenate([proj] + halves, axis=0)
    for copy in range(4):
        out[copy] = whole


def piece(ref, position, lead=()):
    return ref[lead + (slice(ROWS * position, ROWS * (position + 1)), slice(None))].astype(F32)


def plane_kernel(place, quarters, out):
    rows = slice(ROWS * 11, ROWS * 15)
    total = quarters[0, rows].astype(F32)
    for x in range(1, 4):
        total += quarters[x, rows].astype(F32)
    total = total.astype(BF16)
    for copy in range(8):
        out[copy] = total


def nodes_kernel(place, quarters, planes, own_planes, out):
    def put(position, value):
        count = value.shape[0] // ROWS
        out[ROWS * position : ROWS * (position + count)] = value.astype(BF16)

    def quarter(x, start, stop):
        return quarters[x, ROWS * start : ROWS * stop].astype(F32)

    def plane(z, start, stop):
        return planes[z, ROWS * start : ROWS * stop].astype(F32)

    for node in range(2):
        put(4 * node, quarter(2 * node, 5, 9) + quarter(2 * node + 1, 5, 9))
    put(8, quarter(0, 9, 11) + quarter(1, 9, 11) + quarter(2, 9, 11) + quarter(3, 9, 11))
    for node in range(4):
        put(10 + 2 * node, plane(2 * node, 0, 2) + plane(2 * node + 1, 0, 2))
    for node in range(2):
        summed = plane(4 * node, 2, 4) + plane(4 * node + 1, 2, 4)
        summed += plane(4 * node + 2, 2, 4) + plane(4 * node + 3, 2, 4)
        mine = own_planes[0, 2 * ROWS :].astype(F32)
        put(18 + 2 * node, jnp.where(place[3] < 8, mine, summed))


def gathered(ref, position):
    return ref[:, ROWS * position : ROWS * (position + 1), :].reshape(16 * ROWS, R)


def level43_kernel(place, quarters, mixed, coupling, out, keep):
    def proj(x, level):
        return quarters[x, ROWS * level : ROWS * (level + 1)]

    sums = []
    for node in range(2):
        left, right = proj(2 * node, 4), proj(2 * node + 1, 4)
        base = 4 * node
        updates = []
        for part in range(2):
            both = dot_t(left, gathered(mixed, base + 2 * part)) + dot_t(right, gathered(mixed, base + 2 * part + 1))
            updates += [both[:, :R], both[:, R:]]
        sums.append(
            [
                proj(2 * node, l).astype(F32) + proj(2 * node + 1, l).astype(F32) - updates[l]
                for l in range(4)
            ]
        )
    left, right = sums[0][3].astype(BF16), sums[1][3].astype(BF16)
    both = dot_t(left, gathered(mixed, 8)) + dot_t(right, gathered(mixed, 9))
    last = dot_t(left, gathered(mixed, 18)[:R]) + dot_t(right, gathered(mixed, 19)[:R])
    updates = [both[:, :R], both[:, R:], last]
    result = [(sums[0][l] + sums[1][l] - updates[l]).astype(BF16) for l in range(3)]
    result = jnp.concatenate(result, axis=0)
    for copy in range(8):
        out[copy] = result
    x = place[1]
    node = x // 2
    four = dot_t(proj(2 * node, 4), coupling[4, 0][:, :R]) + dot_t(proj(2 * node + 1, 4), coupling[4, 0][:, R:])
    three = dot_t(left, coupling[3, 0][:, :R]) + dot_t(right, coupling[3, 0][:, R:])
    keep[:ROWS] = four.astype(BF16)
    keep[ROWS:] = three.astype(BF16)


def level210_kernel(place, planes, mixed, coupling, keep, out):
    z = place[0]

    def proj(plane, level):
        return planes[plane, ROWS * level : ROWS * (level + 1)]

    def apart(left, right, level):
        return dot_t(left, coupling[level, 0][:, :R]) + dot_t(right, coupling[level, 0][:, R:])

    ones, zeros = [], []
    for node in range(4):
        left, right = proj(2 * node, 2), proj(2 * node + 1, 2)
        both = dot_t(left, gathered(mixed, 10 + 2 * node)) + dot_t(right, gathered(mixed, 11 + 2 * node))
        zeros.append(proj(2 * node, 0).astype(F32) + proj(2 * node + 1, 0).astype(F32) - both[:, :R])
        ones.append(proj(2 * node, 1).astype(F32) + proj(2 * node + 1, 1).astype(F32) - both[:, R:])
    ones = [value.astype(BF16) for value in ones]
    ends = []
    for node in range(2):
        left, right = ones[2 * node], ones[2 * node + 1]
        update = dot_t(left, gathered(mixed, 18 + 2 * node)[R:]) + dot_t(right, gathered(mixed, 19 + 2 * node)[R:])
        ends.append((zeros[2 * node] + zeros[2 * node + 1] - update).astype(BF16))
    pair = 2 * (z // 2)
    two = apart(proj(pair, 2), proj(pair + 1, 2), 2)
    one = jnp.where(z < 4, apart(ones[0], ones[1], 1), apart(ones[2], ones[3], 1))
    zero = apart(ends[0], ends[1], 0)
    out[: 3 * ROWS] = jnp.concatenate([zero, one, two], axis=0).astype(BF16)
    out[3 * ROWS : 4 * ROWS] = keep[ROWS:]
    out[4 * ROWS :] = keep[:ROWS]


def apply_kernel(rhs, bases, corr, out, lhs):
    @pl.when(pl.program_id(0) == 0)
    def _():
        for level in range(5):
            lhs[:, R * level : R * (level + 1)] = gathered(corr, level)

    update = dot(lhs[...], bases[...].reshape(5 * R, bases.shape[2]))
    out[...] = (rhs[...].astype(F32) - update).astype(BF16)


def apply_levels(rhs, bases, corr):
    width = rhs.shape[1] // STEPS
    return pl.pallas_call(
        apply_kernel,
        grid=(STEPS,),
        in_specs=[
            pl.BlockSpec((256, width), lambda i: (0, i)),
            pl.BlockSpec((5, R, width), lambda i: (0, 0, i)),
            pl.BlockSpec((16, 5 * ROWS, R), lambda i: (0, 0, 0)),
        ],
        out_specs=pl.BlockSpec((256, width), lambda i: (0, i)),
        out_shape=jax.ShapeDtypeStruct(rhs.shape, BF16),
        scratch_shapes=[pltpu.VMEM((256, 5 * R), BF16)],
        compiler_params=pltpu.CompilerParams(vmem_limit_bytes=VMEM_LIMIT),
    )(rhs, bases, corr)


def on_device(rhs, bases, coupling):
    group = ("y", "c")
    member = lax.axis_index("y") * 2 + lax.axis_index("c")
    place = jnp.stack([lax.axis_index("z"), lax.axis_index("x"), member * 0, member]).astype(jnp.int32)
    exchange = functools.partial(lax.all_to_all, split_axis=0, concat_axis=0)

    parts = exchange(project(rhs, bases), group)
    quarters = local_call(couple_kernel, place, (4, 15 * ROWS, R), parts, coupling)
    quarters = exchange(quarters, "x")
    own_planes = local_call(plane_kernel, place, (8, 4 * ROWS, R), quarters)
    planes = exchange(own_planes, "z")
    mixed = local_call(nodes_kernel, place, (22 * ROWS, R), quarters, planes, own_planes)
    mixed = lax.all_gather(mixed, group)
    whole = pl.BlockSpec(memory_space=pltpu.VMEM)
    sums, keep = pl.pallas_call(
        level43_kernel,
        in_specs=[pl.BlockSpec(memory_space=pltpu.SMEM)] + [whole] * 3,
        out_specs=[whole, whole],
        out_shape=[
            jax.ShapeDtypeStruct((8, 3 * ROWS, R), BF16),
            jax.ShapeDtypeStruct((2 * ROWS, R), BF16),
        ],
        compiler_params=pltpu.CompilerParams(vmem_limit_bytes=VMEM_LIMIT),
    )(place, quarters, mixed, coupling)
    sums = exchange(sums, "z")
    corr = local_call(level210_kernel, place, (5 * ROWS, R), sums, mixed, coupling, keep)
    corr = lax.all_gather(corr, group)
    return apply_levels(rhs, bases, corr)


def solution(mesh):
    names = ("z", "x", "y", "c")
    split = Mesh(mesh.devices.reshape(8, 4, 8, 2), names)
    return jax.shard_map(
        on_device,
        mesh=split,
        in_specs=(P(None, names), P(None, None, names), P(None, names, None, None)),
        out_specs=P(None, names),
        check_vma=False,
    )
```

time: 271 us -> 154 us (0.57)
  the two profiles are of different devices: /device:TPU:6 before, /device:TPU:1 now
where the time goes in v1:
time: 154 us; the launch traced here: 153 us
  blocking collectives  59.2 us (38%)
  waiting for transfers between devices  53.2 us (35%)
  between operations  13.4 us (9%)
  Pallas kernels  11.2 us (7%)
  starting transfers between devices  10.3 us (7%)
  local copies, waits for them, and re-layouts  5.7 us (4%)
    all_gather x1, waiting for transfers between devices, on_device(): mixed = lax.all_gather(mixed, group)  33.3 us
    all_to_all x1, waiting for transfers between devices, on_device(): parts = exchange(project(rhs, bases), group)  19.9 us
    all_to_all x1, blocking collectives, on_device(): planes = exchange(own_planes, 'z')  18.5 us
    all_gather x1, blocking collectives, on_device(): corr = lax.all_gather(corr, group)  18.2 us
    all_to_all x1, blocking collectives, on_device(): sums = exchange(sums, 'z')  14.4 us
    all_to_all x1, starting transfers between devices, on_device(): parts = exchange(project(rhs, bases), group)  10.3 us
    all_to_all x1, blocking collectives, on_device(): quarters = exchange(quarters, 'x')  8.06 us
    unnamed x14, local copies, waits for them, and re-layouts  5.7 us
  transfers between devices with their start and end apart: 2, of which 2 were waited for; matrix products, arithmetic and copies ran while one was open for 0% of the time, Pallas kernels for 0%

profile of v1, /device:TPU:1, one launch (start us, length us, event | category | flops | bytes accessed | tf_op | source)
XLA Modules:
  0.0 153.1 jit_solution(16100133242180008145)
XLA Ops:
  6.5 0.0 copy-start
  6.5 1.7 %copy-done = bf16[5,128,2048]{2,1,0:T(8,128)(2,1)S(1)} copy-done((bf16[5,128,2048]{2,1,0:T(8,128)(2,1)S(1)}, bf16[5,128,2048]{2,1,0:T(8,128)(2,1)}, u32[]{:S(2)}) %copy-start) | copy-done | bytes 2621464
  8.3 0.0 copy-start.4
  8.3 1.2 copy-done.4
  9.5 0.0 copy-start.6
  9.5 3.8 %shard_map.37 = bf16[16,160,128]{2,1,0:T(8,128)(2,1)} custom-call(bf16[256,2048]{1,0:T(8,128)(2,1)S(1)} %copy-done.4, bf16[5,128,2048]{2,1,0:T(8,128)(2,1)S(1)} %copy-done), custom_call_target="tpu_custom_call" | custom-call | tf_op jit(solution)/shard_map/pallas_call | solution.py:61
  13.3 10.3 %all-to-all-start = ((bf16[16,160,128]{2,1,0:T(8,128)(2,1)}), bf16[16,160,128]{2,1,0:T(8,128)(2,1)S(1)}, u32[]{:S(2)}, u32[]{:S(2)}) async-start(bf16[16,160,128]{2,1,0:T(8,128)(2,1)} %shard_map.37), calls=%async_computation | async-start | bytes 1310720 | tf_op jit(solution)/shard_map/all_to_all | solution.py:248
  23.6 0.0 all-gather.4.cloned.1.call-start
  23.6 0.1 pad_add_fusion.place
  23.7 19.9 %all-to-all-done.parts = bf16[16,160,128]{2,1,0:T(8,128)(2,1)S(1)} async-done(((bf16[16,160,128]{2,1,0:T(8,128)(2,1)}), bf16[16,160,128]{2,1,0:T(8,128)(2,1)S(1)}, u32[]{:S(2)}, u32[]{:S(2)}) %all-to-all-start) | async-done | bytes 655392 | tf_op jit(solution)/shard_map/all_to_all | solution.py:248
  43.6 0.0 copy-done.6
  43.6 0.7 shard_map.38
  44.3 8.1 %all_to_all.20.quarters = bf16[4,240,128]{2,1,0:T(8,128)(2,1)S(1)} all-to-all(bf16[4,240,128]{2,1,0:T(8,128)(2,1)S(1)} %shard_map.38), channel_id=1, replica_groups=mesh['z'=8,'x'=4,'y'=8,'c'=2] {'x'}, dimensions={0} | all-to-all | bytes 491520 | tf_op jit(solution)/shard_map/all_to_all | solution.py:250
  52.4 0.6 shard_map.39.own_planes
  53.0 18.5 %all_to_all.21.planes = bf16[8,64,128]{2,1,0:T(8,128)(2,1)S(1)} all-to-all(bf16[8,64,128]{2,1,0:T(8,128)(2,1)S(1)} %shard_map.39.own_planes), channel_id=1, replica_groups=mesh['z'=8,'x'=4,'y'=8,'c'=2] {'z'}, dimensions={0} | all-to-all | bytes 262144 | tf_op jit(solution)/shard_map/all_to_all | solution.py:252
  71.4 0.0 copy-start.1
  71.4 1.2 shard_map.40
  72.6 0.0 all-gather.4.cloned.1.call-update
  72.7 33.3 %all-gather.4.cloned.1.call-done = bf16[5632,128]{1,0:T(8,128)(2,1)} async-done(((bf16[352,128]{1,0:T(8,128)(2,1)}), bf16[5632,128]{1,0:T(8,128)(2,1)}) %all-gather.4.cloned.1.call-update) | async-done | bytes 1441808 | tf_op jit(solution)/shard_map/all_gather | solution.py:254
  105.9 0.0 copy-start.2
  105.9 1.4 copy-done.2
  107.3 1.0 shard_map.41
  108.3 14.4 %all_to_all.22.planes = bf16[8,48,128]{2,1,0:T(8,128)(2,1)S(1)} all-to-all(bf16[8,48,128]{2,1,0:T(8,128)(2,1)S(1)} %get-tuple-element.7), channel_id=1, replica_groups=mesh['z'=8,'x'=4,'y'=8,'c'=2] {'z'}, dimensions={0} | all-to-all | bytes 196608 | tf_op jit(solution)/shard_map/all_to_all | solution.py:266
  122.7 0.0 copy-start.3
  122.7 1.4 copy-done.3
  124.1 0.0 copy-start.5
  124.1 1.1 shard_map.42
  125.1 18.2 %all-gather.1 = bf16[1280,128]{1,0:T(8,128)(2,1)S(1)} all-gather(bf16[80,128]{1,0:T(8,128)(2,1)S(1)} %shard_map.42), channel_id=3, replica_groups=mesh['z'=8,'x'=4,'y'=8,'c'=2] {'y','c'}, dimensions={0}, use_global_device_ids=true | all-gather | bytes 348160 | tf_op jit(solution)/shard_map/all_gather | solution.py:268
  143.4 0.0 copy-done.1
  143.4 0.0 copy-done.5
  143.4 2.8 %shard_map.43 = bf16[256,2048]{1,0:T(8,128)(2,1)} custom-call(bf16[256,2048]{1,0:T(8,128)(2,1)S(1)} %copy-done.5, bf16[5,128,2048]{2,1,0:T(8,128)(2,1)S(1)} %copy-done.1, bf16[16,80,128]{2,1,0:T(8,128)(2,1)S(1)} %bitcast.7), custom_call_target="tpu_custom_call" | custom-call | tf_op jit(solution)/shard_map/pallas_call | solution.py:227
Async XLA Ops:
  6.5 1.7 %copy-start = (bf16[5,128,2048]{2,1,0:T(8,128)(2,1)S(1)}, bf16[5,128,2048]{2,1,0:T(8,128)(2,1)}, u32[]{:S(2)}) copy-start(bf16[5,128,2048]{2,1,0:T(8,128)(2,1)} %bases.3) | copy-start | bytes 7864324
  8.3 1.2 copy-start.4
  9.5 34.1 %copy-start.6 = (bf16[5,1,128,256]{3,2,1,0:T(8,128)(2,1)S(1)}, bf16[5,1,128,256]{3,2,1,0:T(8,128)(2,1)}, u32[]{:S(2)}) copy-start(bf16[5,1,128,256]{3,2,1,0:T(8,128)(2,1)} %coupling.5) | copy-start | bytes 983044
  13.3 30.3 %all-to-all-start = ((bf16[16,160,128]{2,1,0:T(8,128)(2,1)}), bf16[16,160,128]{2,1,0:T(8,128)(2,1)S(1)}, u32[]{:S(2)}, u32[]{:S(2)}) async-start(bf16[16,160,128]{2,1,0:T(8,128)(2,1)} %shard_map.37), calls=%async_computation | async-start | bytes 1310720 | tf_op jit(solution)/shard_map/all_to_all | solution.py:248
  23.6 82.4 %all-gather.4.cloned.1.call-start = ((), (), s32[]{:S(2)}) async-start(), calls=%async_computation.4 | async-start | bytes 1531904 | tf_op jit(solution)/shard_map/all_gather | solution.py:254
  71.4 72.0 %copy-start.1 = (bf16[5,128,2048]{2,1,0:T(8,128)(2,1)S(1)}, bf16[5,128,2048]{2,1,0:T(8,128)(2,1)}, u32[]{:S(2)}) copy-start(bf16[5,128,2048]{2,1,0:T(8,128)(2,1)} %bases.3) | copy-start | bytes 7864324
  105.9 1.4 copy-start.2
  122.7 1.4 copy-start.3
  124.1 19.3 %copy-start.5 = (bf16[256,2048]{1,0:T(8,128)(2,1)S(1)}, bf16[256,2048]{1,0:T(8,128)(2,1)}, u32[]{:S(2)}) copy-start(bf16[256,2048]{1,0:T(8,128)(2,1)} %rhs.3) | copy-start | bytes 3145732
Sparse Core Ops, SparseCore 0:
  72.8 33.1 all-gather.3

commit v2 on v1

--- a/solution.py
+++ b/solution.py
@@ -78,13 +78,13 @@
     )(rhs, bases)
 
 
-def local_call(kernel, place, shape, *arrays):
+def local_call(kernel, place, shapes, *arrays):
     whole = pl.BlockSpec(memory_space=pltpu.VMEM)
     return pl.pallas_call(
         kernel,
         in_specs=[pl.BlockSpec(memory_space=pltpu.SMEM)] + [whole] * len(arrays),
-        out_specs=whole,
-        out_shape=jax.ShapeDtypeStruct(shape, BF16),
+        out_specs=[whole] * len(shapes),
+        out_shape=[jax.ShapeDtypeStruct(shape, dtype) for shape, dtype in shapes],
         compiler_params=pltpu.CompilerParams(vmem_limit_bytes=VMEM_LIMIT),
     )(place, *arrays)
 
@@ -107,21 +107,7 @@
         out[copy] = whole
 
 
-def piece(ref, position, lead=()):
-    return ref[lead + (slice(ROWS * position, ROWS * (position + 1)), slice(None))].astype(F32)
-
-
-def plane_kernel(place, quarters, out):
-    rows = slice(ROWS * 11, ROWS * 15)
-    total = quarters[0, rows].astype(F32)
-    for x in range(1, 4):
-        total += quarters[x, rows].astype(F32)
-    total = total.astype(BF16)
-    for copy in range(8):
-        out[copy] = total
-
-
-def nodes_kernel(place, quarters, planes, own_planes, out):
+def nodes_kernel(place, quarters, out):
     def put(position, value):
         count = value.shape[0] // ROWS
         out[ROWS * position : ROWS * (position + count)] = value.astype(BF16)
@@ -129,26 +115,20 @@
     def quarter(x, start, stop):
         return quarters[x, ROWS * start : ROWS * stop].astype(F32)
 
-    def plane(z, start, stop):
-        return planes[z, ROWS * start : ROWS * stop].astype(F32)
-
     for node in range(2):
         put(4 * node, quarter(2 * node, 5, 9) + quarter(2 * node + 1, 5, 9))
-    put(8, quarter(0, 9, 11) + quarter(1, 9, 11) + quarter(2, 9, 11) + quarter(3, 9, 11))
-    for node in range(4):
-        put(10 + 2 * node, plane(2 * node, 0, 2) + plane(2 * node + 1, 0, 2))
-    for node in range(2):
-        summed = plane(4 * node, 2, 4) + plane(4 * node + 1, 2, 4)
-        summed += plane(4 * node + 2, 2, 4) + plane(4 * node + 3, 2, 4)
-        mine = own_planes[0, 2 * ROWS :].astype(F32)
-        put(18 + 2 * node, jnp.where(place[3] < 8, mine, summed))
+    put(8, quarter(0, 9, 15) + quarter(1, 9, 15) + quarter(2, 9, 15) + quarter(3, 9, 15))
 
 
 def gathered(ref, position):
     return ref[:, ROWS * position : ROWS * (position + 1), :].reshape(16 * ROWS, R)
 
 
-def level43_kernel(place, quarters, mixed, coupling, out, keep):
+def apart(left, right, coupling, level):
+    return dot_t(left, coupling[level, 0][:, :R]) + dot_t(right, coupling[level, 0][:, R:])
+
+
+def level43_kernel(place, quarters, mixed, coupling, two, rest, keep):
     def proj(x, level):
         return quarters[x, ROWS * level : ROWS * (level + 1)]
 
@@ -168,46 +148,44 @@
         )
     left, right = sums[0][3].astype(BF16), sums[1][3].astype(BF16)
     both = dot_t(left, gathered(mixed, 8)) + dot_t(right, gathered(mixed, 9))
-    last = dot_t(left, gathered(mixed, 18)[:R]) + dot_t(right, gathered(mixed, 19)[:R])
-    updates = [both[:, :R], both[:, R:], last]
-    result = [(sums[0][l] + sums[1][l] - updates[l]).astype(BF16) for l in range(3)]
-    result = jnp.concatenate(result, axis=0)
+    last = dot_t(left, gathered(mixed, 12)[:R]) + dot_t(right, gathered(mixed, 13)[:R])
+    two[...] = (sums[0][2] + sums[1][2] - last).astype(BF16)
+    rest[:ROWS] = sums[0][1] + sums[1][1] - both[:, R:]
+    rest[ROWS:] = sums[0][0] + sums[1][0] - both[:, :R]
+    node = place[1] // 2
+    four = apart(proj(2 * node, 4), proj(2 * node + 1, 4), coupling, 4)
+    keep[:ROWS] = four.astype(BF16)
+    keep[ROWS:] = apart(left, right, coupling, 3).astype(BF16)
+
+
+def level2_kernel(place, mine, other, rest, mixed, coupling, one, zero, corr):
+    first = place[0] % 2 == 0
+    left = jnp.where(first, mine[...], other[...])
+    right = jnp.where(first, other[...], mine[...])
+    both = dot_t(left, gathered(mixed, 10)) + dot_t(right, gathered(mixed, 11))
+    value = (rest[:ROWS] - both[:, R:]).astype(BF16)
+    for copy in range(4):
+        one[copy] = value
+    zero[...] = rest[ROWS:] - both[:, :R]
+    corr[...] = apart(left, right, coupling, 2).astype(BF16)
+
+
+def level1_kernel(place, ones, rest, mixed, coupling, zero, corr):
+    ones = [ones[plane].astype(F32) for plane in range(4)]
+    left, right = (ones[0] + ones[1]).astype(BF16), (ones[2] + ones[3]).astype(BF16)
+    update = dot_t(left, gathered(mixed, 12)[R:]) + dot_t(right, gathered(mixed, 13)[R:])
+    value = (rest[...] - update).astype(BF16)
     for copy in range(8):
-        out[copy] = result
-    x = place[1]
-    node = x // 2
-    four = dot_t(proj(2 * node, 4), coupling[4, 0][:, :R]) + dot_t(proj(2 * node + 1, 4), coupling[4, 0][:, R:])
-    three = dot_t(left, coupling[3, 0][:, :R]) + dot_t(right, coupling[3, 0][:, R:])
-    keep[:ROWS] = four.astype(BF16)
-    keep[ROWS:] = three.astype(BF16)
-
-
-def level210_kernel(place, planes, mixed, coupling, keep, out):
-    z = place[0]
-
-    def proj(plane, level):
-        return planes[plane, ROWS * level : ROWS * (level + 1)]
-
-    def apart(left, right, level):
-        return dot_t(left, coupling[level, 0][:, :R]) + dot_t(right, coupling[level, 0][:, R:])
-
-    ones, zeros = [], []
-    for node in range(4):
-        left, right = proj(2 * node, 2), proj(2 * node + 1, 2)
-        both = dot_t(left, gathered(mixed, 10 + 2 * node)) + dot_t(right, gathered(mixed, 11 + 2 * node))
-        zeros.append(proj(2 * node, 0).astype(F32) + proj(2 * node + 1, 0).astype(F32) - both[:, :R])
-        ones.append(proj(2 * node, 1).astype(F32) + proj(2 * node + 1, 1).astype(F32) - both[:, R:])
-    ones = [value.astype(BF16) for value in ones]
-    ends = []
-    for node in range(2):
-        left, right = ones[2 * node], ones[2 * node + 1]
-        update = dot_t(left, gathered(mixed, 18 + 2 * node)[R:]) + dot_t(right, gathered(mixed, 19 + 2 * node)[R:])
-        ends.append((zeros[2 * node] + zeros[2 * node + 1] - update).astype(BF16))
-    pair = 2 * (z // 2)
-    two = apart(proj(pair, 2), proj(pair + 1, 2), 2)
-    one = jnp.where(z < 4, apart(ones[0], ones[1], 1), apart(ones[2], ones[3], 1))
-    zero = apart(ends[0], ends[1], 0)
-    out[: 3 * ROWS] = jnp.concatenate([zero, one, two], axis=0).astype(BF16)
+        zero[copy] = value
+    corr[...] = apart(left, right, coupling, 1).astype(BF16)
+
+
+def level0_kernel(place, zeros, coupling, keep, two, one, out):
+    zeros = [zeros[plane].astype(F32) for plane in range(8)]
+    left, right = sum(zeros[1:4], zeros[0]).astype(BF16), sum(zeros[5:], zeros[4]).astype(BF16)
+    out[:ROWS] = apart(left, right, coupling, 0).astype(BF16)
+    out[ROWS : 2 * ROWS] = one[...]
+    out[2 * ROWS : 3 * ROWS] = two[...]
     out[3 * ROWS : 4 * ROWS] = keep[ROWS:]
     out[4 * ROWS :] = keep[:ROWS]
 
@@ -242,36 +220,50 @@
 def on_device(rhs, bases, coupling):
     group = ("y", "c")
     member = lax.axis_index("y") * 2 + lax.axis_index("c")
-    place = jnp.stack([lax.axis_index("z"), lax.axis_index("x"), member * 0, member]).astype(jnp.int32)
+    z = lax.axis_index("zh") * 4 + lax.axis_index("zl")
+    place = jnp.stack([z, lax.axis_index("x"), member * 0, member]).astype(jnp.int32)
     exchange = functools.partial(lax.all_to_all, split_axis=0, concat_axis=0)
+    block = (ROWS, R)
 
     parts = exchange(project(rhs, bases), group)
-    quarters = local_call(couple_kernel, place, (4, 15 * ROWS, R), parts, coupling)
+    (quarters,) = local_call(couple_kernel, place, [((4, 15 * ROWS, R), BF16)], parts, coupling)
     quarters = exchange(quarters, "x")
-    own_planes = local_call(plane_kernel, place, (8, 4 * ROWS, R), quarters)
-    planes = exchange(own_planes, "z")
-    mixed = local_call(nodes_kernel, place, (22 * ROWS, R), quarters, planes, own_planes)
+    (mixed,) = local_call(nodes_kernel, place, [((14 * ROWS, R), BF16)], quarters)
     mixed = lax.all_gather(mixed, group)
-    whole = pl.BlockSpec(memory_space=pltpu.VMEM)
-    sums, keep = pl.pallas_call(
+    two, rest, keep = local_call(
         level43_kernel,
-        in_specs=[pl.BlockSpec(memory_space=pltpu.SMEM)] + [whole] * 3,
-        out_specs=[whole, whole],
-        out_shape=[
-            jax.ShapeDtypeStruct((8, 3 * ROWS, R), BF16),
-            jax.ShapeDtypeStruct((2 * ROWS, R), BF16),
-        ],
-        compiler_params=pltpu.CompilerParams(vmem_limit_bytes=VMEM_LIMIT),
-    )(place, quarters, mixed, coupling)
-    sums = exchange(sums, "z")
-    corr = local_call(level210_kernel, place, (5 * ROWS, R), sums, mixed, coupling, keep)
+        place,
+        [(block, BF16), ((2 * ROWS, R), F32), ((2 * ROWS, R), BF16)],
+        quarters,
+        mixed,
+        coupling,
+    )
+    other = lax.ppermute(two, "zl", [(plane, plane ^ 1) for plane in range(4)])
+    ones, rest, corr_2 = local_call(
+        level2_kernel,
+        place,
+        [((4, *block), BF16), (block, F32), (block, BF16)],
+        two,
+        other,
+        rest,
+        mixed,
+        coupling,
+    )
+    ones = exchange(ones, "zl")
+    zeros, corr_1 = local_call(
+        level1_kernel, place, [((8, *block), BF16), (block, BF16)], ones, rest, mixed, coupling
+    )
+    zeros = exchange(zeros, ("zh", "zl"))
+    (corr,) = local_call(
+        level0_kernel, place, [((5 * ROWS, R), BF16)], zeros, coupling, keep, corr_2, corr_1
+    )
     corr = lax.all_gather(corr, group)
     return apply_levels(rhs, bases, corr)
 
 
 def solution(mesh):
-    names = ("z", "x", "y", "c")
-    split = Mesh(mesh.devices.reshape(8, 4, 8, 2), names)
+    names = ("zh", "zl", "x", "y", "c")
+    split = Mesh(mesh.devices.reshape(2, 4, 4, 8, 2), names)
     return jax.shard_map(
         on_device,
         mesh=split,

time: 154 us -> 120 us (0.78)
  waiting for transfers between devices: 53.2 us -> 20.9 us
  between operations: 13.4 us -> 0.03 us
  blocking collectives: 59.2 us -> 70.5 us
  starting transfers between devices: 10.3 us -> 14.2 us
  local copies, waits for them, and re-layouts: 5.7 us -> 2.97 us
    all_gather x1 -> x0, waiting for transfers between devices: 33.3 us -> none  [on_device(): mixed = lax.all_gather(mixed, group)]
    all_gather x0 -> x1, blocking collectives: none -> 17.4 us  [on_device(): mixed = lax.all_gather(mixed, group)]
    all_to_all x2, blocking collectives: 32.9 us -> 24.6 us  [the longest x1 14 us: on_device(): zeros = exchange(zeros, ('zh', 'zl'))]
    ppermute x0 -> x1, starting transfers between devices: none -> 3.98 us  [on_device(): other = lax.ppermute(two, 'zl', [(plane, plane ^ 1) for plane in range(4)])]
    unnamed x14 -> x10, local copies, waits for them, and re-layouts: 5.7 us -> 2.97 us
    all_gather x1, blocking collectives: 18.2 us -> 20.5 us  [on_device(): corr = lax.all_gather(corr, group)]
    pallas_call x4 -> x6, Pallas kernels: 3.54 us -> 4.35 us  [local_call(): pl.pallas_call(kernel, in_specs=[pl.BlockSpec(memory_space=pltpu.SMEM)] +...]
where the time goes in v2:
time: 120 us
  blocking collectives  70.5 us (59%)
  waiting for transfers between devices  20.9 us (17%)
  starting transfers between devices  14.2 us (12%)
  Pallas kernels  11 us (9%)
  local copies, waits for them, and re-layouts  2.97 us (2%)
    all_gather x1, blocking collectives, on_device(): corr = lax.all_gather(corr, group)  20.5 us
    all_to_all x1, waiting for transfers between devices, on_device(): parts = exchange(project(rhs, bases), group)  20 us
    all_gather x1, blocking collectives, on_device(): mixed = lax.all_gather(mixed, group)  17.4 us
    all_to_all x1, blocking collectives, on_device(): zeros = exchange(zeros, ('zh', 'zl'))  14 us
    all_to_all x1, blocking collectives, on_device(): ones = exchange(ones, 'zl')  10.6 us
    all_to_all x1, starting transfers between devices, on_device(): parts = exchange(project(rhs, bases), group)  10.3 us
    all_to_all x1, blocking collectives, on_device(): quarters = exchange(quarters, 'x')  8.06 us
    pallas_call x6, Pallas kernels, local_call(): pl.pallas_call(kernel, in_specs=[pl.BlockSpec(memory_space=pltpu.SMEM)] +...  4.35 us
  transfers between devices with their start and end apart: 2, of which 2 were waited for; matrix products, arithmetic and copies ran while one was open for 0% of the time, Pallas kernels for 0%

profile of v2, /device:TPU:1, one launch (start us, length us, event | category | flops | bytes accessed | tf_op | source)
XLA Modules:
  0.0 119.8 jit_solution(2017520691392665106)
XLA Ops:
  0.0 0.0 copy-start
  0.0 1.7 %copy-done = bf16[5,128,2048]{2,1,0:T(8,128)(2,1)S(1)} copy-done((bf16[5,128,2048]{2,1,0:T(8,128)(2,1)S(1)}, bf16[5,128,2048]{2,1,0:T(8,128)(2,1)}, u32[]{:S(2)}) %copy-start) | copy-done | bytes 2621464
  1.7 0.0 copy-start.3
  1.7 1.2 %copy-done.3 = bf16[256,2048]{1,0:T(8,128)(2,1)S(1)} copy-done((bf16[256,2048]{1,0:T(8,128)(2,1)S(1)}, bf16[256,2048]{1,0:T(8,128)(2,1)}, u32[]{:S(2)}) %copy-start.3) | copy-done | bytes 1048600
  3.0 0.0 copy-start.2
  3.0 3.8 %shard_map.37 = bf16[16,160,128]{2,1,0:T(8,128)(2,1)} custom-call(bf16[256,2048]{1,0:T(8,128)(2,1)S(1)} %copy-done.3, bf16[5,128,2048]{2,1,0:T(8,128)(2,1)S(1)} %copy-done), custom_call_target="tpu_custom_call" | custom-call | tf_op jit(solution)/shard_map/pallas_call | solution.py:61
  6.8 10.3 %all-to-all-start = ((bf16[16,160,128]{2,1,0:T(8,128)(2,1)}), bf16[16,160,128]{2,1,0:T(8,128)(2,1)S(1)}, u32[]{:S(2)}, u32[]{:S(2)}) async-start(bf16[16,160,128]{2,1,0:T(8,128)(2,1)} %shard_map.37), calls=%async_computation | async-start | bytes 1310720 | tf_op jit(solution)/shard_map/all_to_all | solution.py:228
  17.0 0.1 pad_add_fusion.place
  17.1 20.0 %all-to-all-done.parts = bf16[16,160,128]{2,1,0:T(8,128)(2,1)S(1)} async-done(((bf16[16,160,128]{2,1,0:T(8,128)(2,1)}), bf16[16,160,128]{2,1,0:T(8,128)(2,1)S(1)}, u32[]{:S(2)}, u32[]{:S(2)}) %all-to-all-start) | async-done | bytes 655392 | tf_op jit(solution)/shard_map/all_to_all | solution.py:228
  37.1 0.0 copy-done.2
  37.1 0.7 shard_map.38
  37.8 8.1 %all_to_all.20.quarters = bf16[4,240,128]{2,1,0:T(8,128)(2,1)S(1)} all-to-all(bf16[4,240,128]{2,1,0:T(8,128)(2,1)S(1)} %shard_map.38), channel_id=1, replica_groups=mesh['zh'=2,'zl'=4,'x'=4,'y'=8,'c'=2] {'x'}, dimensions={0} | all-to-all | bytes 491520 | tf_op jit(solution)/shard_map/all_to_all | solution.py:230
  45.9 0.6 shard_map.39
  46.4 17.4 %all-gather = bf16[3584,128]{1,0:T(8,128)(2,1)S(1)} all-gather(bf16[224,128]{1,0:T(8,128)(2,1)S(1)} %shard_map.39), channel_id=2, replica_groups=mesh['zh'=2,'zl'=4,'x'=4,'y'=8,'c'=2] {'y','c'}, dimensions={0}, use_global_device_ids=true | all-gather | bytes 974848 | tf_op jit(solution)/shard_map/all_gather | solution.py:232
  63.8 0.0 copy-start.1
  63.8 0.0 copy-start.4
  63.8 1.0 shard_map.40
  64.8 4.0 %collective-permute-start = (bf16[16,128]{1,0:T(8,128)(2,1)S(1)}, bf16[16,128]{1,0:T(8,128)(2,1)S(1)}, u32[]{:S(2)}, u32[]{:S(2)}) collective-permute-start(bf16[16,128]{1,0:T(8,128)(2,1)S(1)} %get-tuple-element.13.mine), channel_id=1, source_target_pairs={{0,64},{64,0},{128,192},{192,128},{1,65},{65,1},{129,193},{193,129... | collective-permute-start | bytes 12296 | tf_op jit(solution)/shard_map/ppermute | solution.py:241
  68.8 1.0 collective-permute-done.other
  69.8 0.7 shard_map.41
  70.5 10.6 %all_to_all.21.ones = bf16[4,16,128]{2,1,0:T(8,128)(2,1)S(1)} all-to-all(bf16[4,16,128]{2,1,0:T(8,128)(2,1)S(1)} %get-tuple-element.15), channel_id=1, replica_groups=mesh['zh'=2,'zl'=4,'x'=4,'y'=8,'c'=2] {'zl'}, dimensions={0} | all-to-all | bytes 32768 | tf_op jit(solution)/shard_map/all_to_all | solution.py:252
  81.1 0.7 shard_map.42
  81.8 14.0 %all_to_all.22.zeros = bf16[8,16,128]{2,1,0:T(8,128)(2,1)S(1)} all-to-all(bf16[8,16,128]{2,1,0:T(8,128)(2,1)S(1)} %get-tuple-element.17), channel_id=1, replica_groups=mesh['zh'=2,'zl'=4,'x'=4,'y'=8,'c'=2] {'zh','zl'}, dimensions={0} | all-to-all | bytes 65536 | tf_op jit(solution)/shard_map/all_to_all | solution.py:256
  95.8 0.7 shard_map.43
  96.5 20.5 %all-gather.1 = bf16[1280,128]{1,0:T(8,128)(2,1)S(1)} all-gather(bf16[80,128]{1,0:T(8,128)(2,1)S(1)} %shard_map.43), channel_id=3, replica_groups=mesh['zh'=2,'zl'=4,'x'=4,'y'=8,'c'=2] {'y','c'}, dimensions={0}, use_global_device_ids=true | all-gather | bytes 348160 | tf_op jit(solution)/shard_map/all_gather | solution.py:260
  116.9 0.0 copy-done.1
  116.9 0.0 copy-done.4
  116.9 2.8 %shard_map.44 = bf16[256,2048]{1,0:T(8,128)(2,1)} custom-call(bf16[256,2048]{1,0:T(8,128)(2,1)S(1)} %copy-done.4, bf16[5,128,2048]{2,1,0:T(8,128)(2,1)S(1)} %copy-done.1, bf16[16,80,128]{2,1,0:T(8,128)(2,1)S(1)} %bitcast.8), custom_call_target="tpu_custom_call" | custom-call | tf_op jit(solution)/shard_map/pallas_call | solution.py:205
Async XLA Ops:
  0.0 1.7 %copy-start = (bf16[5,128,2048]{2,1,0:T(8,128)(2,1)S(1)}, bf16[5,128,2048]{2,1,0:T(8,128)(2,1)}, u32[]{:S(2)}) copy-start(bf16[5,128,2048]{2,1,0:T(8,128)(2,1)} %bases.3) | copy-start | bytes 7864324
  1.7 1.2 %copy-start.3 = (bf16[256,2048]{1,0:T(8,128)(2,1)S(1)}, bf16[256,2048]{1,0:T(8,128)(2,1)}, u32[]{:S(2)}) copy-start(bf16[256,2048]{1,0:T(8,128)(2,1)} %rhs.3) | copy-start | bytes 3145732
  3.0 34.1 %copy-start.2 = (bf16[5,1,128,256]{3,2,1,0:T(8,128)(2,1)S(1)}, bf16[5,1,128,256]{3,2,1,0:T(8,128)(2,1)}, u32[]{:S(2)}) copy-start(bf16[5,1,128,256]{3,2,1,0:T(8,128)(2,1)} %coupling.9) | copy-start | bytes 983044
  6.8 30.3 %all-to-all-start = ((bf16[16,160,128]{2,1,0:T(8,128)(2,1)}), bf16[16,160,128]{2,1,0:T(8,128)(2,1)S(1)}, u32[]{:S(2)}, u32[]{:S(2)}) async-start(bf16[16,160,128]{2,1,0:T(8,128)(2,1)} %shard_map.37), calls=%async_computation | async-start | bytes 1310720 | tf_op jit(solution)/shard_map/all_to_all | solution.py:228
  63.8 53.1 %copy-start.1 = (bf16[5,128,2048]{2,1,0:T(8,128)(2,1)S(1)}, bf16[5,128,2048]{2,1,0:T(8,128)(2,1)}, u32[]{:S(2)}) copy-start(bf16[5,128,2048]{2,1,0:T(8,128)(2,1)} %bases.3) | copy-start | bytes 7864324
  63.8 53.1 %copy-start.4 = (bf16[256,2048]{1,0:T(8,128)(2,1)S(1)}, bf16[256,2048]{1,0:T(8,128)(2,1)}, u32[]{:S(2)}) copy-start(bf16[256,2048]{1,0:T(8,128)(2,1)} %rhs.3) | copy-start | bytes 3145732
  64.8 5.0 %collective-permute-start = (bf16[16,128]{1,0:T(8,128)(2,1)S(1)}, bf16[16,128]{1,0:T(8,128)(2,1)S(1)}, u32[]{:S(2)}, u32[]{:S(2)}) collective-permute-start(bf16[16,128]{1,0:T(8,128)(2,1)S(1)} %get-tuple-element.13.mine), channel_id=1, source_target_pairs={{0,64},{64,0},{128,192},{192,128},{1,65},{65,1},{129,193},{193,129... | collective-permute-start | bytes 12296 | tf_op jit(solution)/shard_map/ppermute | solution.py:241

commit v3 on v2

v3 whole, which is shorter than its diff:
```python
import functools

import jax
import jax.numpy as jnp
from jax import lax
from jax.experimental import pallas as pl
from jax.experimental.pallas import tpu as pltpu
from jax.sharding import Mesh
from jax.sharding import PartitionSpec as P


ROWS = 16
R = 128
CHUNKS = 2
OUT_CHUNKS = 4
HALF = 8
F32 = jnp.float32
BF16 = jnp.bfloat16
VMEM_LIMIT = 40 * 1024 * 1024
PROJECT_VMEM_LIMIT = 53 * 1024 * 1024


def dot_t(a, b):
    return lax.dot_general(a, b, (((1,), (1,)), ((), ())), preferred_element_type=F32)


def dot(a, b):
    return jnp.dot(a, b, preferred_element_type=F32)


def project_kernel(rhs, bases, mine, other, stack, high, middle, low, sems):
    width = rhs.shape[1] // CHUNKS
    copies = []
    for chunk in range(CHUNKS):
        columns = pl.ds(chunk * width, width)
        copies.append([pltpu.make_async_copy(rhs.at[:, columns], stack.at[: 2 * R, columns], sems.at[0, chunk])])
        for level in range(5):
            rows = pl.ds((2 + level) * R, R)
            copies[chunk].append(
                pltpu.make_async_copy(
                    bases.at[level, :, columns], stack.at[rows, columns], sems.at[level + 1, chunk]
                )
            )
        for copy in copies[chunk]:
            copy.start()

    def add(acc, chunk, value):
        if chunk == 0:
            acc[...] = value
        else:
            acc[...] += value

    for chunk in range(CHUNKS):
        columns = slice(chunk * width, (chunk + 1) * width)
        for copy in copies[chunk]:
            copy.wait()
        add(high, chunk, dot_t(stack[: 6 * R, columns], stack[5 * R :, columns]))
        add(middle, chunk, dot_t(stack[: 4 * R, columns], stack[3 * R : 5 * R, columns]))
        add(low, chunk, dot_t(stack[: 2 * R, columns], stack[2 * R : 3 * R, columns]))

    def tile(ref, row, column):
        return ref[row * R : (row + 1) * R, column * R : (column + 1) * R]

    first = lax.axis_index("c") == 0

    def put(position, zero, one):
        rows = slice(ROWS * position, ROWS * (position + 1))
        zero, one = zero.astype(BF16), one.astype(BF16)
        mine[:, rows, :] = jnp.where(first, zero, one).reshape(HALF, ROWS, R)
        other[:, rows, :] = jnp.where(first, one, zero).reshape(HALF, ROWS, R)

    for level, (ref, column) in enumerate([(low, 0), (middle, 0), (middle, 1), (high, 0), (high, 1)]):
        put(level, tile(ref, 0, column), tile(ref, 1, column))
    put(5, tile(high, 2, 1), tile(high, 3, 1))
    put(6, tile(high, 4, 1), tile(high, 5, 1))
    put(7, tile(high, 2, 0), tile(high, 3, 0))
    put(8, tile(middle, 2, 1), tile(middle, 3, 1))
    put(9, tile(high, 4, 0), tile(middle, 2, 0))


def project(rhs, bases):
    hbm = pl.BlockSpec(memory_space=pltpu.HBM)
    whole = pl.BlockSpec(memory_space=pltpu.VMEM)
    return pl.pallas_call(
        project_kernel,
        in_specs=[hbm, hbm],
        out_specs=[whole, whole],
        out_shape=[jax.ShapeDtypeStruct((HALF, 10 * ROWS, R), BF16)] * 2,
        scratch_shapes=[
            pltpu.VMEM((7 * R, rhs.shape[1]), BF16),
            pltpu.VMEM((6 * R, 2 * R), F32),
            pltpu.VMEM((4 * R, 2 * R), F32),
            pltpu.VMEM((2 * R, R), F32),
            pltpu.SemaphoreType.DMA((6, CHUNKS)),
        ],
        compiler_params=pltpu.CompilerParams(vmem_limit_bytes=PROJECT_VMEM_LIMIT),
    )(rhs, bases)


def local_call(kernel, shapes, *arrays):
    whole = pl.BlockSpec(memory_space=pltpu.VMEM)
    return pl.pallas_call(
        kernel,
        in_specs=[whole] * len(arrays),
        out_specs=[whole] * len(shapes),
        out_shape=[jax.ShapeDtypeStruct(shape, dtype) for shape, dtype in shapes],
        compiler_params=pltpu.CompilerParams(vmem_limit_bytes=VMEM_LIMIT),
    )(*arrays)


def chip_kernel(mine, theirs, out):
    out[...] = (mine[...].astype(F32) + theirs[...].astype(F32)).astype(BF16)


def couple_kernel(parts, coupling, out):
    total = parts[0].astype(F32)
    for source in range(1, HALF):
        total += parts[source].astype(F32)
    total = total.astype(BF16)
    proj, gram = total[: 5 * ROWS], total[5 * ROWS :]
    first = dot(gram[: 2 * ROWS], coupling[4, 0])
    second = dot(gram[2 * ROWS : 3 * ROWS], coupling[3, 0])
    third = dot(gram[3 * ROWS : 4 * ROWS], coupling[2, 0])
    last = gram[4 * ROWS :]
    fourth = jnp.where(lax.axis_index("c") == 0, dot(last, coupling[3, 0]), dot(last, coupling[1, 0]))
    mixed = [first[:ROWS], first[ROWS:], second, third, fourth]
    halves = [m[:, R * half : R * (half + 1)].astype(BF16) for m in mixed for half in (0, 1)]
    whole = jnp.concatenate([proj] + halves, axis=0)
    for copy in range(4):
        out[copy] = whole


def nodes_kernel(quarters, out):
    def put(position, value):
        count = value.shape[0] // ROWS
        out[ROWS * position : ROWS * (position + count)] = value.astype(BF16)

    def quarter(x, start, stop):
        return quarters[x, ROWS * start : ROWS * stop].astype(F32)

    for node in range(2):
        put(4 * node, quarter(2 * node, 5, 9) + quarter(2 * node + 1, 5, 9))
    put(8, quarter(0, 9, 15) + quarter(1, 9, 15) + quarter(2, 9, 15) + quarter(3, 9, 15))


def gathered(ref, position):
    rows = slice(ROWS * position, ROWS * (position + 1))
    return jnp.concatenate([ref[2 * y + c, rows] for c in range(2) for y in range(HALF)], axis=0)


def apart(left, right, coupling, level):
    return dot_t(left, coupling[level, 0][:, :R]) + dot_t(right, coupling[level, 0][:, R:])


def level43_kernel(quarters, mixed, coupling, two, rest, keep):
    def proj(x, level):
        return quarters[x, ROWS * level : ROWS * (level + 1)]

    sums = []
    for node in range(2):
        left, right = proj(2 * node, 4), proj(2 * node + 1, 4)
        base = 4 * node
        updates = []
        for part in range(2):
            both = dot_t(left, gathered(mixed, base + 2 * part)) + dot_t(right, gathered(mixed, base + 2 * part + 1))
            updates += [both[:, :R], both[:, R:]]
        sums.append(
            [
                proj(2 * node, l).astype(F32) + proj(2 * node + 1, l).astype(F32) - updates[l]
                for l in range(4)
            ]
        )
    left, right = sums[0][3].astype(BF16), sums[1][3].astype(BF16)
    both = dot_t(left, gathered(mixed, 8)) + dot_t(right, gathered(mixed, 9))
    last = dot_t(left, gathered(mixed, 12)[:R]) + dot_t(right, gathered(mixed, 13)[:R])
    two[...] = (sums[0][2] + sums[1][2] - last).astype(BF16)
    rest[:ROWS] = sums[0][1] + sums[1][1] - both[:, R:]
    rest[ROWS:] = sums[0][0] + sums[1][0] - both[:, :R]
    node = lax.axis_index("x") // 2
    four = apart(proj(2 * node, 4), proj(2 * node + 1, 4), coupling, 4)
    keep[:ROWS] = four.astype(BF16)
    keep[ROWS:] = apart(left, right, coupling, 3).astype(BF16)


def level2_kernel(mine, other, rest, mixed, coupling, one, zero, corr):
    first = lax.axis_index("zl") % 2 == 0
    left = jnp.where(first, mine[...], other[...])
    right = jnp.where(first, other[...], mine[...])
    both = dot_t(left, gathered(mixed, 10)) + dot_t(right, gathered(mixed, 11))
    value = (rest[:ROWS] - both[:, R:]).astype(BF16)
    for copy in range(4):
        one[copy] = value
    zero[...] = rest[ROWS:] - both[:, :R]
    corr[...] = apart(left, right, coupling, 2).astype(BF16)


def level1_kernel(ones, rest, mixed, coupling, zero, corr):
    ones = [ones[plane].astype(F32) for plane in range(4)]
    left, right = (ones[0] + ones[1]).astype(BF16), (ones[2] + ones[3]).astype(BF16)
    update = dot_t(left, gathered(mixed, 12)[R:]) + dot_t(right, gathered(mixed, 13)[R:])
    value = (rest[...] - update).astype(BF16)
    for copy in range(8):
        zero[copy] = value
    corr[...] = apart(left, right, coupling, 1).astype(BF16)


def level0_kernel(zeros, coupling, keep, two, one, out):
    zeros = [zeros[plane].astype(F32) for plane in range(8)]
    left, right = sum(zeros[1:4], zeros[0]).astype(BF16), sum(zeros[5:], zeros[4]).astype(BF16)
    out[:ROWS] = apart(left, right, coupling, 0).astype(BF16)
    out[ROWS : 2 * ROWS] = one[...]
    out[2 * ROWS : 3 * ROWS] = two[...]
    out[3 * ROWS : 4 * ROWS] = keep[ROWS:]
    out[4 * ROWS :] = keep[:ROWS]


def apply_kernel(rhs, bases, corr, out, here, sems):
    everything = jnp.concatenate([gathered(corr, level) for level in range(5)], axis=1)
    width = rhs.shape[1] // OUT_CHUNKS
    copies = []
    for chunk in range(OUT_CHUNKS):
        columns = slice(chunk * width, (chunk + 1) * width)
        update = dot(everything, bases[:, :, columns].reshape(5 * R, width))
        here[:, columns] = (rhs[:, columns].astype(F32) - update).astype(BF16)
        columns = pl.ds(chunk * width, width)
        copies.append(pltpu.make_async_copy(here.at[:, columns], out.at[:, columns], sems.at[chunk]))
        copies[-1].start()
    for copy in copies:
        copy.wait()


def apply_levels(rhs, bases, corr):
    whole = pl.BlockSpec(memory_space=pltpu.VMEM)
    return pl.pallas_call(
        apply_kernel,
        in_specs=[whole, whole, whole],
        out_specs=pl.BlockSpec(memory_space=pltpu.HBM),
        out_shape=jax.ShapeDtypeStruct(rhs.shape, BF16),
        scratch_shapes=[pltpu.VMEM(rhs.shape, BF16), pltpu.SemaphoreType.DMA((OUT_CHUNKS,))],
        compiler_params=pltpu.CompilerParams(vmem_limit_bytes=VMEM_LIMIT),
    )(rhs, bases, corr)


def on_device(rhs, bases, coupling):
    group = ("y", "c")
    exchange = functools.partial(lax.all_to_all, split_axis=0, concat_axis=0)
    block = (ROWS, R)

    mine, other = project(rhs, bases)
    theirs = lax.ppermute(other, "c", [(0, 1), (1, 0)])
    (parts,) = local_call(chip_kernel, [(mine.shape, BF16)], mine, theirs)
    parts = exchange(parts, "y")
    (quarters,) = local_call(couple_kernel, [((4, 15 * ROWS, R), BF16)], parts, coupling)
    quarters = exchange(quarters, "x")
    (mixed,) = local_call(nodes_kernel, [((14 * ROWS, R), BF16)], quarters)
    mixed = lax.all_gather(mixed, group)
    two, rest, keep = local_call(
        level43_kernel,
        [(block, BF16), ((2 * ROWS, R), F32), ((2 * ROWS, R), BF16)],
        quarters,
        mixed,
        coupling,
    )
    other = lax.ppermute(two, "zl", [(plane, plane ^ 1) for plane in range(4)])
    ones, rest, corr_2 = local_call(
        level2_kernel,
        [((4, *block), BF16), (block, F32), (block, BF16)],
        two,
        other,
        rest,
        mixed,
        coupling,
    )
    ones = exchange(ones, "zl")
    zeros, corr_1 = local_call(
        level1_kernel, [((8, *block), BF16), (block, BF16)], ones, rest, mixed, coupling
    )
    zeros = exchange(zeros, ("zh", "zl"))
    (corr,) = local_call(
        level0_kernel, [((5 * ROWS, R), BF16)], zeros, coupling, keep, corr_2, corr_1
    )
    corr = lax.all_gather(corr, group)
    return apply_levels(rhs, bases, corr)


def solution(mesh):
    names = ("zh", "zl", "x", "y", "c")
    split = Mesh(mesh.devices.reshape(2, 4, 4, 8, 2), names)
    return jax.shard_map(
        on_device,
        mesh=split,
        in_specs=(P(None, names), P(None, None, names), P(None, names, None, None)),
        out_specs=P(None, names),
        check_vma=False,
    )
```

time: 120 us -> 110 us (0.917)
  waiting for transfers between devices: 20.9 us -> 2.22 us
  blocking collectives: 70.5 us -> 88.3 us
  Pallas kernels: 11 us -> 6.41 us
  local copies, waits for them, and re-layouts: 2.97 us -> 0.01 us
  starting transfers between devices: 14.2 us -> 12.9 us
    all_to_all x1 -> x0, waiting for transfers between devices: 20 us -> none  [on_device(): parts = exchange(project(rhs, bases), group)]
    all_to_all x0 -> x1, blocking collectives: none -> 16.1 us  [on_device(): parts = exchange(parts, 'y')]
    all_to_all x1 -> x0, starting transfers between devices: 10.3 us -> none  [on_device(): parts = exchange(project(rhs, bases), group)]
    ppermute x0 -> x1, starting transfers between devices: none -> 8.79 us  [on_device(): theirs = lax.ppermute(other, 'c', [(0, 1), (1, 0)])]
    pallas_call x8 -> x9, Pallas kernels: 11 us -> 6.41 us  [the longest x1 3.49 us: project(): pl.pallas_call(project_kernel, in_specs=[hbm, hbm], out_specs=[whole, who...]
    unnamed x10 -> x6, local copies, waits for them, and re-layouts: 2.97 us -> 0.01 us
    all_gather x1, blocking collectives: 17.4 us -> 19.2 us  [on_device(): mixed = lax.all_gather(mixed, group)]
    ppermute x0 -> x1, waiting for transfers between devices: none -> 1.23 us  [on_device(): theirs = lax.ppermute(other, 'c', [(0, 1), (1, 0)])]
where the time goes in v3:
time: 110 us
  blocking collectives  88.3 us (80%)
  starting transfers between devices  12.9 us (12%)
  Pallas kernels  6.41 us (6%)
  waiting for transfers between devices  2.22 us (2%)
    all_gather x1, blocking collectives, on_device(): corr = lax.all_gather(corr, group)  20.5 us
    all_gather x1, blocking collectives, on_device(): mixed = lax.all_gather(mixed, group)  19.2 us
    all_to_all x1, blocking collectives, on_device(): parts = exchange(parts, 'y')  16.1 us
    all_to_all x1, blocking collectives, on_device(): zeros = exchange(zeros, ('zh', 'zl'))  14 us
    all_to_all x1, blocking collectives, on_device(): ones = exchange(ones, 'zl')  10.6 us
    ppermute x1, starting transfers between devices, on_device(): theirs = lax.ppermute(other, 'c', [(0, 1), (1, 0)])  8.79 us
    all_to_all x1, blocking collectives, on_device(): quarters = exchange(quarters, 'x')  7.83 us
    ppermute x1, starting transfers between devices, on_device(): other = lax.ppermute(two, 'zl', [(plane, plane ^ 1) for plane in range(4)])  4.14 us
  transfers between devices with their start and end apart: 2, of which 2 were waited for; matrix products, arithmetic and copies ran while one was open for 0% of the time, Pallas kernels for 0%

profile of v3, /device:TPU:1, one launch (start us, length us, event | category | flops | bytes accessed | tf_op | source)
XLA Modules:
  0.0 109.9 jit_solution(8863592903610282125)
XLA Ops:
  0.0 0.0 copy-start.1
  0.0 3.5 %shard_map.37 = (bf16[8,160,128]{2,1,0:T(8,128)(2,1)S(1)}, bf16[8,160,128]{2,1,0:T(8,128)(2,1)S(1)}) custom-call(bf16[256,2048]{1,0:T(8,128)(2,1)} %rhs.3, bf16[5,128,2048]{2,1,0:T(8,128)(2,1)} %bases.3), custom_call_target="tpu_custom_call" | custom-call | tf_op jit(solution)/shard_map/pallas_call | solution.py:84
  3.5 8.8 %collective-permute-start = (bf16[8,160,128]{2,1,0:T(8,128)(2,1)S(1)}, bf16[8,160,128]{2,1,0:T(8,128)(2,1)S(1)}, u32[]{:S(2)}, u32[]{:S(2)}) collective-permute-start(bf16[8,160,128]{2,1,0:T(8,128)(2,1)S(1)} %get-tuple-element.16), channel_id=1, source_target_pairs={{0,1},{1,0},{2,3},{3,2},{4,5},{5,4},{6,7},{7,6},{8,9},{9,8},{10,11... | collective-permute-start | bytes 983048 | tf_op jit(solution)/shard_map/ppermute | solution.py:250
  12.3 1.2 %collective-permute-done.theirs = bf16[8,160,128]{2,1,0:T(8,128)(2,1)S(1)} collective-permute-done((bf16[8,160,128]{2,1,0:T(8,128)(2,1)S(1)}, bf16[8,160,128]{2,1,0:T(8,128)(2,1)S(1)}, u32[]{:S(2)}, u32[]{:S(2)}) %collective-permute-start) | collective-permute-done | bytes 327712 | tf_op jit(solution)/shard_map/ppermute | solution.py:250
  13.5 0.1 shard_map.38
  13.6 16.1 %all_to_all.20.parts = bf16[8,160,128]{2,1,0:T(8,128)(2,1)S(1)} all-to-all(bf16[8,160,128]{2,1,0:T(8,128)(2,1)S(1)} %shard_map.38), channel_id=1, replica_groups=mesh['zh'=2,'zl'=4,'x'=4,'y'=8,'c'=2] {'y'}, dimensions={0} | all-to-all | bytes 655360 | tf_op jit(solution)/shard_map/all_to_all | solution.py:252
  29.7 0.0 copy-done.1
  29.8 0.2 shard_map.39
  29.9 7.8 %all_to_all.21.quarters = bf16[4,240,128]{2,1,0:T(8,128)(2,1)S(1)} all-to-all(bf16[4,240,128]{2,1,0:T(8,128)(2,1)S(1)} %shard_map.39), channel_id=1, replica_groups=mesh['zh'=2,'zl'=4,'x'=4,'y'=8,'c'=2] {'x'}, dimensions={0} | all-to-all | bytes 491520 | tf_op jit(solution)/shard_map/all_to_all | solution.py:254
  37.8 19.2 %all-gather = bf16[3584,128]{1,0:T(8,128)(2,1)S(1)} all-gather(bf16[224,128]{1,0:T(8,128)(2,1)S(1)} %shard_map.40), channel_id=2, replica_groups=mesh['zh'=2,'zl'=4,'x'=4,'y'=8,'c'=2] {'y','c'}, dimensions={0}, use_global_device_ids=true | all-gather | bytes 974848 | tf_op jit(solution)/shard_map/all_gather | solution.py:256
  57.0 0.0 copy-start
  57.0 0.0 copy-start.2
  57.0 0.5 shard_map.41
  57.5 4.1 %collective-permute-start.1 = (bf16[16,128]{1,0:T(8,128)(2,1)S(1)}, bf16[16,128]{1,0:T(8,128)(2,1)S(1)}, u32[]{:S(2)}, u32[]{:S(2)}) collective-permute-start(bf16[16,128]{1,0:T(8,128)(2,1)S(1)} %get-tuple-element.17.mine), channel_id=1, source_target_pairs={{0,64},{64,0},{128,192},{192,128},{1,65},{65,1},{129,193},{193,129... | collective-permute-start | bytes 12296 | tf_op jit(solution)/shard_map/ppermute | solution.py:264
  61.6 1.0 collective-permute-done.1.other
  62.6 0.2 shard_map.42
  62.8 10.6 %all_to_all.22.ones = bf16[4,16,128]{2,1,0:T(8,128)(2,1)S(1)} all-to-all(bf16[4,16,128]{2,1,0:T(8,128)(2,1)S(1)} %get-tuple-element.19), channel_id=1, replica_groups=mesh['zh'=2,'zl'=4,'x'=4,'y'=8,'c'=2] {'zl'}, dimensions={0} | all-to-all | bytes 32768 | tf_op jit(solution)/shard_map/all_to_all | solution.py:274
  73.4 0.2 shard_map.43
  73.6 14.0 %all_to_all.23.zeros = bf16[8,16,128]{2,1,0:T(8,128)(2,1)S(1)} all-to-all(bf16[8,16,128]{2,1,0:T(8,128)(2,1)S(1)} %get-tuple-element.21), channel_id=1, replica_groups=mesh['zh'=2,'zl'=4,'x'=4,'y'=8,'c'=2] {'zh','zl'}, dimensions={0} | all-to-all | bytes 65536 | tf_op jit(solution)/shard_map/all_to_all | solution.py:278
  87.6 0.1 shard_map.44
  87.7 20.5 %all-gather.1 = bf16[1280,128]{1,0:T(8,128)(2,1)S(1)} all-gather(bf16[80,128]{1,0:T(8,128)(2,1)S(1)} %shard_map.44), channel_id=3, replica_groups=mesh['zh'=2,'zl'=4,'x'=4,'y'=8,'c'=2] {'y','c'}, dimensions={0}, use_global_device_ids=true | all-gather | bytes 348160 | tf_op jit(solution)/shard_map/all_gather | solution.py:282
  108.2 0.0 copy-done
  108.2 0.0 copy-done.2
  108.2 1.7 %shard_map.45 = bf16[256,2048]{1,0:T(8,128)(2,1)} custom-call(bf16[256,2048]{1,0:T(8,128)(2,1)S(1)} %copy-done.2, bf16[5,128,2048]{2,1,0:T(8,128)(2,1)S(1)} %copy-done, bf16[16,80,128]{2,1,0:T(8,128)(2,1)S(1)} %bitcast.5), custom_call_target="tpu_custom_call" | custom-call | tf_op jit(solution)/shard_map/pallas_call | solution.py:234
  (1 shorter events, 0.0 us)
Async XLA Ops:
  0.0 29.7 %copy-start.1 = (bf16[5,1,128,256]{3,2,1,0:T(8,128)(2,1)S(1)}, bf16[5,1,128,256]{3,2,1,0:T(8,128)(2,1)}, u32[]{:S(2)}) copy-start(bf16[5,1,128,256]{3,2,1,0:T(8,128)(2,1)} %coupling.9) | copy-start | bytes 983044
  3.5 10.0 %collective-permute-start = (bf16[8,160,128]{2,1,0:T(8,128)(2,1)S(1)}, bf16[8,160,128]{2,1,0:T(8,128)(2,1)S(1)}, u32[]{:S(2)}, u32[]{:S(2)}) collective-permute-start(bf16[8,160,128]{2,1,0:T(8,128)(2,1)S(1)} %get-tuple-element.16), channel_id=1, source_target_pairs={{0,1},{1,0},{2,3},{3,2},{4,5},{5,4},{6,7},{7,6},{8,9},{9,8},{10,11... | collective-permute-start | bytes 983048 | tf_op jit(solution)/shard_map/ppermute | solution.py:250
  57.0 51.1 %copy-start = (bf16[5,128,2048]{2,1,0:T(8,128)(2,1)S(1)}, bf16[5,128,2048]{2,1,0:T(8,128)(2,1)}, u32[]{:S(2)}) copy-start(bf16[5,128,2048]{2,1,0:T(8,128)(2,1)} %bases.3) | copy-start | bytes 7864324
  57.0 51.1 %copy-start.2 = (bf16[256,2048]{1,0:T(8,128)(2,1)S(1)}, bf16[256,2048]{1,0:T(8,128)(2,1)}, u32[]{:S(2)}) copy-start(bf16[256,2048]{1,0:T(8,128)(2,1)} %rhs.3) | copy-start | bytes 3145732
  57.5 5.1 %collective-permute-start.1 = (bf16[16,128]{1,0:T(8,128)(2,1)S(1)}, bf16[16,128]{1,0:T(8,128)(2,1)S(1)}, u32[]{:S(2)}, u32[]{:S(2)}) collective-permute-start(bf16[16,128]{1,0:T(8,128)(2,1)S(1)} %get-tuple-element.17.mine), channel_id=1, source_target_pairs={{0,64},{64,0},{128,192},{192,128},{1,65},{65,1},{129,193},{193,129... | collective-permute-start | bytes 12296 | tf_op jit(solution)/shard_map/ppermute | solution.py:264

commit v4 on v3

--- a/solution.py
+++ b/solution.py
@@ -130,7 +130,20 @@
         out[copy] = whole
 
 
-def nodes_kernel(quarters, out):
+def quarter_sum(quarters, start, stop):
+    rows = slice(ROWS * start, ROWS * stop)
+    return sum((quarters[x, rows].astype(F32) for x in range(1, 4)), quarters[0, rows].astype(F32))
+
+
+def plane_kernel(quarters, out):
+    total = quarter_sum(quarters, 11, 15).astype(BF16)
+    for plane in range(4):
+        second, first = plane % 2, 2 + plane // 2
+        out[plane, :ROWS] = total[ROWS * second : ROWS * (second + 1)]
+        out[plane, ROWS:] = total[ROWS * first : ROWS * (first + 1)]
+
+
+def nodes_kernel(quarters, planes, out):
     def put(position, value):
         count = value.shape[0] // ROWS
         out[ROWS * position : ROWS * (position + count)] = value.astype(BF16)
@@ -140,7 +153,14 @@
 
     for node in range(2):
         put(4 * node, quarter(2 * node, 5, 9) + quarter(2 * node + 1, 5, 9))
-    put(8, quarter(0, 9, 15) + quarter(1, 9, 15) + quarter(2, 9, 15) + quarter(3, 9, 15))
+    put(8, quarter_sum(quarters, 9, 11))
+    summed = planes[0].astype(F32) + planes[1].astype(F32) + planes[2].astype(F32) + planes[3].astype(F32)
+    last = quarter_sum(quarters, 13, 15)
+    here = lax.axis_index("c") == 0
+    put(10, jnp.where(here, last[:ROWS], summed[ROWS:]))
+    put(11, last[ROWS:])
+    pair = 2 * (lax.axis_index("zl") // 2)
+    put(12, planes[pair, :ROWS].astype(F32) + planes[pair + 1, :ROWS].astype(F32))
 
 
 def gathered(ref, position):
@@ -152,7 +172,7 @@
     return dot_t(left, coupling[level, 0][:, :R]) + dot_t(right, coupling[level, 0][:, R:])
 
 
-def level43_kernel(quarters, mixed, coupling, two, rest, keep):
+def levels_kernel(quarters, mixed, coupling, out, keep):
     def proj(x, level):
         return quarters[x, ROWS * level : ROWS * (level + 1)]
 
@@ -172,44 +192,35 @@
         )
     left, right = sums[0][3].astype(BF16), sums[1][3].astype(BF16)
     both = dot_t(left, gathered(mixed, 8)) + dot_t(right, gathered(mixed, 9))
-    last = dot_t(left, gathered(mixed, 12)[:R]) + dot_t(right, gathered(mixed, 13)[:R])
-    two[...] = (sums[0][2] + sums[1][2] - last).astype(BF16)
-    rest[:ROWS] = sums[0][1] + sums[1][1] - both[:, R:]
-    rest[ROWS:] = sums[0][0] + sums[1][0] - both[:, :R]
+    last = gathered(mixed, 10)
+    update = dot_t(left, last[:R]) + dot_t(right, gathered(mixed, 11)[:R])
+    two = (sums[0][2] + sums[1][2] - update).astype(BF16)
+    lower = dot_t(two, gathered(mixed, 12))
+    one = (sums[0][1] + sums[1][1] - both[:, R:] - lower[:, R:]).astype(BF16)
+    zero = sums[0][0] + sums[1][0] - both[:, :R] - lower[:, :R] - dot_t(one, last[R:])
+    result = jnp.concatenate([zero.astype(BF16), one, two], axis=0)
+    for copy in range(8):
+        out[copy] = result
     node = lax.axis_index("x") // 2
     four = apart(proj(2 * node, 4), proj(2 * node + 1, 4), coupling, 4)
     keep[:ROWS] = four.astype(BF16)
     keep[ROWS:] = apart(left, right, coupling, 3).astype(BF16)
 
 
-def level2_kernel(mine, other, rest, mixed, coupling, one, zero, corr):
-    first = lax.axis_index("zl") % 2 == 0
-    left = jnp.where(first, mine[...], other[...])
-    right = jnp.where(first, other[...], mine[...])
-    both = dot_t(left, gathered(mixed, 10)) + dot_t(right, gathered(mixed, 11))
-    value = (rest[:ROWS] - both[:, R:]).astype(BF16)
-    for copy in range(4):
-        one[copy] = value
-    zero[...] = rest[ROWS:] - both[:, :R]
-    corr[...] = apart(left, right, coupling, 2).astype(BF16)
-
-
-def level1_kernel(ones, rest, mixed, coupling, zero, corr):
-    ones = [ones[plane].astype(F32) for plane in range(4)]
-    left, right = (ones[0] + ones[1]).astype(BF16), (ones[2] + ones[3]).astype(BF16)
-    update = dot_t(left, gathered(mixed, 12)[R:]) + dot_t(right, gathered(mixed, 13)[R:])
-    value = (rest[...] - update).astype(BF16)
-    for copy in range(8):
-        zero[copy] = value
-    corr[...] = apart(left, right, coupling, 1).astype(BF16)
-
-
-def level0_kernel(zeros, coupling, keep, two, one, out):
-    zeros = [zeros[plane].astype(F32) for plane in range(8)]
-    left, right = sum(zeros[1:4], zeros[0]).astype(BF16), sum(zeros[5:], zeros[4]).astype(BF16)
-    out[:ROWS] = apart(left, right, coupling, 0).astype(BF16)
-    out[ROWS : 2 * ROWS] = one[...]
-    out[2 * ROWS : 3 * ROWS] = two[...]
+def corr_kernel(planes, coupling, keep, out):
+    def proj(plane, level):
+        return planes[plane, ROWS * level : ROWS * (level + 1)]
+
+    def over(level, first, count):
+        return sum(
+            (proj(first + plane, level).astype(F32) for plane in range(1, count)), proj(first, level).astype(F32)
+        ).astype(BF16)
+
+    z = lax.axis_index("zh") * 4 + lax.axis_index("zl")
+    pair, quad = 2 * (z // 2), 4 * (z // 4)
+    out[:ROWS] = apart(over(0, 0, 4), over(0, 4, 4), coupling, 0).astype(BF16)
+    out[ROWS : 2 * ROWS] = apart(over(1, quad, 2), over(1, quad + 2, 2), coupling, 1).astype(BF16)
+    out[2 * ROWS : 3 * ROWS] = apart(proj(pair, 2), proj(pair + 1, 2), coupling, 2).astype(BF16)
     out[3 * ROWS : 4 * ROWS] = keep[ROWS:]
     out[4 * ROWS :] = keep[:ROWS]
 
@@ -244,7 +255,6 @@
 def on_device(rhs, bases, coupling):
     group = ("y", "c")
     exchange = functools.partial(lax.all_to_all, split_axis=0, concat_axis=0)
-    block = (ROWS, R)
 
     mine, other = project(rhs, bases)
     theirs = lax.ppermute(other, "c", [(0, 1), (1, 0)])
@@ -252,33 +262,19 @@
     parts = exchange(parts, "y")
     (quarters,) = local_call(couple_kernel, [((4, 15 * ROWS, R), BF16)], parts, coupling)
     quarters = exchange(quarters, "x")
-    (mixed,) = local_call(nodes_kernel, [((14 * ROWS, R), BF16)], quarters)
+    (planes,) = local_call(plane_kernel, [((4, 2 * ROWS, R), BF16)], quarters)
+    planes = exchange(planes, "zl")
+    (mixed,) = local_call(nodes_kernel, [((13 * ROWS, R), BF16)], quarters, planes)
     mixed = lax.all_gather(mixed, group)
-    two, rest, keep = local_call(
-        level43_kernel,
-        [(block, BF16), ((2 * ROWS, R), F32), ((2 * ROWS, R), BF16)],
+    lower, keep = local_call(
+        levels_kernel,
+        [((8, 3 * ROWS, R), BF16), ((2 * ROWS, R), BF16)],
         quarters,
         mixed,
         coupling,
     )
-    other = lax.ppermute(two, "zl", [(plane, plane ^ 1) for plane in range(4)])
-    ones, rest, corr_2 = local_call(
-        level2_kernel,
-        [((4, *block), BF16), (block, F32), (block, BF16)],
-        two,
-        other,
-        rest,
-        mixed,
-        coupling,
-    )
-    ones = exchange(ones, "zl")
-    zeros, corr_1 = local_call(
-        level1_kernel, [((8, *block), BF16), (block, BF16)], ones, rest, mixed, coupling
-    )
-    zeros = exchange(zeros, ("zh", "zl"))
-    (corr,) = local_call(
-        level0_kernel, [((5 * ROWS, R), BF16)], zeros, coupling, keep, corr_2, corr_1
-    )
+    lower = exchange(lower, ("zh", "zl"))
+    (corr,) = local_call(corr_kernel, [((5 * ROWS, R), BF16)], lower, coupling, keep)
     corr = lax.all_gather(corr, group)
     return apply_levels(rhs, bases, corr)
 

time: 110 us -> 105 us (0.955)
  starting transfers between devices: 12.9 us -> 8.79 us
    ppermute x1 -> x0, starting transfers between devices: 4.14 us -> none  [on_device(): other = lax.ppermute(two, 'zl', [(plane, plane ^ 1) for plane in range(4)])]
    all_gather x1, blocking collectives: 20.5 us -> 18.1 us  [on_device(): corr = lax.all_gather(corr, group)]
    all_gather x1, blocking collectives: 19.2 us -> 21.2 us  [on_device(): mixed = lax.all_gather(mixed, group)]
  transfers between devices with their start and end apart: 2 -> 1, of which waited for: 2 -> 1; matrix products, arithmetic and copies ran while one was open for 0% -> 0% of each run, Pallas kernels for 0% -> 0%
where the time goes in v4:
time: 105 us
  blocking collectives  88.8 us (85%)
  starting transfers between devices  8.79 us (8%)
  Pallas kernels  6.38 us (6%)
  waiting for transfers between devices  1.23 us (1%)
    all_gather x1, blocking collectives, on_device(): mixed = lax.all_gather(mixed, group)  21.2 us
    all_gather x1, blocking collectives, on_device(): corr = lax.all_gather(corr, group)  18.1 us
    all_to_all x1, blocking collectives, on_device(): parts = exchange(parts, 'y')  16.1 us
    all_to_all x1, blocking collectives, on_device(): lower = exchange(lower, ('zh', 'zl'))  14.6 us
    all_to_all x1, blocking collectives, on_device(): planes = exchange(planes, 'zl')  10.6 us
    ppermute x1, starting transfers between devices, on_device(): theirs = lax.ppermute(other, 'c', [(0, 1), (1, 0)])  8.79 us
    all_to_all x1, blocking collectives, on_device(): quarters = exchange(quarters, 'x')  8.09 us
    pallas_call x1, Pallas kernels, project(): pl.pallas_call(project_kernel, in_specs=[hbm, hbm], out_specs=[whole, who...  3.49 us
  transfers between devices with their start and end apart: 1, of which 1 were waited for; matrix products, arithmetic and copies ran while one was open for 0% of the time, Pallas kernels for 0%

profile of v4, /device:TPU:1, one launch (start us, length us, event | category | flops | bytes accessed | tf_op | source)
XLA Modules:
  0.0 105.2 jit_solution(12835476318436445386)
XLA Ops:
  0.0 0.0 copy-start.2
  0.0 3.5 %shard_map.37 = (bf16[8,160,128]{2,1,0:T(8,128)(2,1)S(1)}, bf16[8,160,128]{2,1,0:T(8,128)(2,1)S(1)}) custom-call(bf16[256,2048]{1,0:T(8,128)(2,1)} %rhs.3, bf16[5,128,2048]{2,1,0:T(8,128)(2,1)} %bases.3), custom_call_target="tpu_custom_call" | custom-call | tf_op jit(solution)/shard_map/pallas_call | solution.py:84
  3.5 8.8 %collective-permute-start = (bf16[8,160,128]{2,1,0:T(8,128)(2,1)S(1)}, bf16[8,160,128]{2,1,0:T(8,128)(2,1)S(1)}, u32[]{:S(2)}, u32[]{:S(2)}) collective-permute-start(bf16[8,160,128]{2,1,0:T(8,128)(2,1)S(1)} %get-tuple-element.10), channel_id=1, source_target_pairs={{0,1},{1,0},{2,3},{3,2},{4,5},{5,4},{6,7},{7,6},{8,9},{9,8},{10,11... | collective-permute-start | bytes 983048 | tf_op jit(solution)/shard_map/ppermute | solution.py:260
  12.3 1.2 %collective-permute-done.theirs = bf16[8,160,128]{2,1,0:T(8,128)(2,1)S(1)} collective-permute-done((bf16[8,160,128]{2,1,0:T(8,128)(2,1)S(1)}, bf16[8,160,128]{2,1,0:T(8,128)(2,1)S(1)}, u32[]{:S(2)}, u32[]{:S(2)}) %collective-permute-start) | collective-permute-done | bytes 327712 | tf_op jit(solution)/shard_map/ppermute | solution.py:260
  13.5 0.1 shard_map.38
  13.6 16.1 %all_to_all.20.parts = bf16[8,160,128]{2,1,0:T(8,128)(2,1)S(1)} all-to-all(bf16[8,160,128]{2,1,0:T(8,128)(2,1)S(1)} %shard_map.38), channel_id=1, replica_groups=mesh['zh'=2,'zl'=4,'x'=4,'y'=8,'c'=2] {'y'}, dimensions={0} | all-to-all | bytes 655360 | tf_op jit(solution)/shard_map/all_to_all | solution.py:262
  29.7 0.0 copy-done.2
  29.8 0.0 copy-start
  29.8 0.0 copy-start.1
  29.8 0.2 shard_map.39
  29.9 8.1 %all_to_all.21.quarters = bf16[4,240,128]{2,1,0:T(8,128)(2,1)S(1)} all-to-all(bf16[4,240,128]{2,1,0:T(8,128)(2,1)S(1)} %shard_map.39), channel_id=1, replica_groups=mesh['zh'=2,'zl'=4,'x'=4,'y'=8,'c'=2] {'x'}, dimensions={0} | all-to-all | bytes 491520 | tf_op jit(solution)/shard_map/all_to_all | solution.py:264
  38.0 10.6 %all_to_all.22.planes = bf16[4,32,128]{2,1,0:T(8,128)(2,1)S(1)} all-to-all(bf16[4,32,128]{2,1,0:T(8,128)(2,1)S(1)} %shard_map.40), channel_id=1, replica_groups=mesh['zh'=2,'zl'=4,'x'=4,'y'=8,'c'=2] {'zl'}, dimensions={0} | all-to-all | bytes 65536 | tf_op jit(solution)/shard_map/all_to_all | solution.py:266
  48.7 21.2 %all-gather = bf16[3328,128]{1,0:T(8,128)(2,1)S(1)} all-gather(bf16[208,128]{1,0:T(8,128)(2,1)S(1)} %shard_map.41), channel_id=2, replica_groups=mesh['zh'=2,'zl'=4,'x'=4,'y'=8,'c'=2] {'y','c'}, dimensions={0}, use_global_device_ids=true | all-gather | bytes 905216 | tf_op jit(solution)/shard_map/all_gather | solution.py:268
  69.8 0.7 shard_map.42
  70.5 14.6 %all_to_all.23.planes = bf16[8,48,128]{2,1,0:T(8,128)(2,1)S(1)} all-to-all(bf16[8,48,128]{2,1,0:T(8,128)(2,1)S(1)} %get-tuple-element.11), channel_id=1, replica_groups=mesh['zh'=2,'zl'=4,'x'=4,'y'=8,'c'=2] {'zh','zl'}, dimensions={0} | all-to-all | bytes 196608 | tf_op jit(solution)/shard_map/all_to_all | solution.py:276
  85.1 0.2 shard_map.43
  85.3 18.1 %all-gather.1 = bf16[1280,128]{1,0:T(8,128)(2,1)S(1)} all-gather(bf16[80,128]{1,0:T(8,128)(2,1)S(1)} %shard_map.43), channel_id=3, replica_groups=mesh['zh'=2,'zl'=4,'x'=4,'y'=8,'c'=2] {'y','c'}, dimensions={0}, use_global_device_ids=true | all-gather | bytes 348160 | tf_op jit(solution)/shard_map/all_gather | solution.py:278
  103.5 0.0 copy-done
  103.5 0.0 copy-done.1
  103.5 1.7 %shard_map.44 = bf16[256,2048]{1,0:T(8,128)(2,1)} custom-call(bf16[256,2048]{1,0:T(8,128)(2,1)S(1)} %copy-done.1, bf16[5,128,2048]{2,1,0:T(8,128)(2,1)S(1)} %copy-done, bf16[16,80,128]{2,1,0:T(8,128)(2,1)S(1)} %bitcast.3), custom_call_target="tpu_custom_call" | custom-call | tf_op jit(solution)/shard_map/pallas_call | solution.py:245
  (2 shorter events, 0.0 us)
Async XLA Ops:
  0.0 29.7 %copy-start.2 = (bf16[5,1,128,256]{3,2,1,0:T(8,128)(2,1)S(1)}, bf16[5,1,128,256]{3,2,1,0:T(8,128)(2,1)}, u32[]{:S(2)}) copy-start(bf16[5,1,128,256]{3,2,1,0:T(8,128)(2,1)} %coupling.5) | copy-start | bytes 983044
  3.5 10.0 %collective-permute-start = (bf16[8,160,128]{2,1,0:T(8,128)(2,1)S(1)}, bf16[8,160,128]{2,1,0:T(8,128)(2,1)S(1)}, u32[]{:S(2)}, u32[]{:S(2)}) collective-permute-start(bf16[8,160,128]{2,1,0:T(8,128)(2,1)S(1)} %get-tuple-element.10), channel_id=1, source_target_pairs={{0,1},{1,0},{2,3},{3,2},{4,5},{5,4},{6,7},{7,6},{8,9},{9,8},{10,11... | collective-permute-start | bytes 983048 | tf_op jit(solution)/shard_map/ppermute | solution.py:260
  29.8 73.7 %copy-start = (bf16[5,128,2048]{2,1,0:T(8,128)(2,1)S(1)}, bf16[5,128,2048]{2,1,0:T(8,128)(2,1)}, u32[]{:S(2)}) copy-start(bf16[5,128,2048]{2,1,0:T(8,128)(2,1)} %bases.3) | copy-start | bytes 7864324
  29.8 73.7 %copy-start.1 = (bf16[256,2048]{1,0:T(8,128)(2,1)S(1)}, bf16[256,2048]{1,0:T(8,128)(2,1)}, u32[]{:S(2)}) copy-start(bf16[256,2048]{1,0:T(8,128)(2,1)} %rhs.3) | copy-start | bytes 3145732

commit v5 on v4

--- a/solution.py
+++ b/solution.py
@@ -12,7 +12,7 @@
 ROWS = 16
 R = 128
 CHUNKS = 2
-OUT_CHUNKS = 4
+OUT_CHUNKS = 2
 HALF = 8
 F32 = jnp.float32
 BF16 = jnp.bfloat16
@@ -143,7 +143,7 @@
         out[plane, ROWS:] = total[ROWS * first : ROWS * (first + 1)]
 
 
-def nodes_kernel(quarters, planes, out):
+def nodes_kernel(quarters, planes, coupling, out):
     def put(position, value):
         count = value.shape[0] // ROWS
         out[ROWS * position : ROWS * (position + count)] = value.astype(BF16)
@@ -161,6 +161,10 @@
     put(11, last[ROWS:])
     pair = 2 * (lax.axis_index("zl") // 2)
     put(12, planes[pair, :ROWS].astype(F32) + planes[pair + 1, :ROWS].astype(F32))
+    node = lax.axis_index("x") // 2
+    four = ROWS * 4, ROWS * 5
+    left, right = quarters[2 * node, slice(*four)], quarters[2 * node + 1, slice(*four)]
+    put(13, apart(left, right, coupling, 4))
 
 
 def gathered(ref, position):
@@ -201,10 +205,7 @@
     result = jnp.concatenate([zero.astype(BF16), one, two], axis=0)
     for copy in range(8):
         out[copy] = result
-    node = lax.axis_index("x") // 2
-    four = apart(proj(2 * node, 4), proj(2 * node + 1, 4), coupling, 4)
-    keep[:ROWS] = four.astype(BF16)
-    keep[ROWS:] = apart(left, right, coupling, 3).astype(BF16)
+    keep[...] = apart(left, right, coupling, 3).astype(BF16)
 
 
 def corr_kernel(planes, coupling, keep, out):
@@ -218,15 +219,22 @@
 
     z = lax.axis_index("zh") * 4 + lax.axis_index("zl")
     pair, quad = 2 * (z // 2), 4 * (z // 4)
-    out[:ROWS] = apart(over(0, 0, 4), over(0, 4, 4), coupling, 0).astype(BF16)
-    out[ROWS : 2 * ROWS] = apart(over(1, quad, 2), over(1, quad + 2, 2), coupling, 1).astype(BF16)
-    out[2 * ROWS : 3 * ROWS] = apart(proj(pair, 2), proj(pair + 1, 2), coupling, 2).astype(BF16)
-    out[3 * ROWS : 4 * ROWS] = keep[ROWS:]
-    out[4 * ROWS :] = keep[:ROWS]
-
-
-def apply_kernel(rhs, bases, corr, out, here, sems):
-    everything = jnp.concatenate([gathered(corr, level) for level in range(5)], axis=1)
+    zero = apart(over(0, 0, 4), over(0, 4, 4), coupling, 0).astype(BF16)
+    one = apart(over(1, quad, 2), over(1, quad + 2, 2), coupling, 1).astype(BF16)
+    two = apart(proj(pair, 2), proj(pair + 1, 2), coupling, 2).astype(BF16)
+    result = jnp.concatenate([zero, one, two, keep[...]], axis=0)
+    for copy in range(HALF):
+        out[copy] = result
+
+
+def apply_kernel(rhs, bases, mixed, mine, theirs, out, here, sems):
+    first = lax.axis_index("c") == 0
+    levels = []
+    for level in range(4):
+        rows = slice(ROWS * level, ROWS * (level + 1))
+        low, high = mine[:, rows].reshape(R, R), theirs[:, rows].reshape(R, R)
+        levels.append(jnp.concatenate([jnp.where(first, low, high), jnp.where(first, high, low)], axis=0))
+    everything = jnp.concatenate(levels + [gathered(mixed, 13)], axis=1)
     width = rhs.shape[1] // OUT_CHUNKS
     copies = []
     for chunk in range(OUT_CHUNKS):
@@ -240,43 +248,45 @@
         copy.wait()
 
 
-def apply_levels(rhs, bases, corr):
+def apply_levels(rhs, *arrays):
     whole = pl.BlockSpec(memory_space=pltpu.VMEM)
     return pl.pallas_call(
         apply_kernel,
-        in_specs=[whole, whole, whole],
+        in_specs=[whole] * (1 + len(arrays)),
         out_specs=pl.BlockSpec(memory_space=pltpu.HBM),
         out_shape=jax.ShapeDtypeStruct(rhs.shape, BF16),
         scratch_shapes=[pltpu.VMEM(rhs.shape, BF16), pltpu.SemaphoreType.DMA((OUT_CHUNKS,))],
         compiler_params=pltpu.CompilerParams(vmem_limit_bytes=VMEM_LIMIT),
-    )(rhs, bases, corr)
+    )(rhs, *arrays)
 
 
 def on_device(rhs, bases, coupling):
     group = ("y", "c")
+    swap = [(0, 1), (1, 0)]
     exchange = functools.partial(lax.all_to_all, split_axis=0, concat_axis=0)
 
     mine, other = project(rhs, bases)
-    theirs = lax.ppermute(other, "c", [(0, 1), (1, 0)])
+    theirs = lax.ppermute(other, "c", swap)
     (parts,) = local_call(chip_kernel, [(mine.shape, BF16)], mine, theirs)
     parts = exchange(parts, "y")
     (quarters,) = local_call(couple_kernel, [((4, 15 * ROWS, R), BF16)], parts, coupling)
     quarters = exchange(quarters, "x")
     (planes,) = local_call(plane_kernel, [((4, 2 * ROWS, R), BF16)], quarters)
     planes = exchange(planes, "zl")
-    (mixed,) = local_call(nodes_kernel, [((13 * ROWS, R), BF16)], quarters, planes)
+    (mixed,) = local_call(nodes_kernel, [((14 * ROWS, R), BF16)], quarters, planes, coupling)
     mixed = lax.all_gather(mixed, group)
     lower, keep = local_call(
         levels_kernel,
-        [((8, 3 * ROWS, R), BF16), ((2 * ROWS, R), BF16)],
+        [((8, 3 * ROWS, R), BF16), ((ROWS, R), BF16)],
         quarters,
         mixed,
         coupling,
     )
     lower = exchange(lower, ("zh", "zl"))
-    (corr,) = local_call(corr_kernel, [((5 * ROWS, R), BF16)], lower, coupling, keep)
-    corr = lax.all_gather(corr, group)
-    return apply_levels(rhs, bases, corr)
+    (mine,) = local_call(corr_kernel, [((HALF, 4 * ROWS, R), BF16)], lower, coupling, keep)
+    mine = exchange(mine, "y")
+    theirs = lax.ppermute(mine, "c", swap)
+    return apply_levels(rhs, bases, mixed, mine, theirs)
 
 
 def solution(mesh):

time: 105 us -> 105 us (level)
  blocking collectives: 88.8 us -> 82.1 us
  starting transfers between devices: 8.79 us -> 13.8 us
    all_gather x1 -> x0, blocking collectives: 18.1 us -> none  [on_device(): corr = lax.all_gather(corr, group)]
    all_to_all x0 -> x1, blocking collectives: none -> 11.3 us  [on_device(): mine = exchange(mine, 'y')]
    ppermute x1 -> x2, starting transfers between devices: 8.79 us -> 13.8 us  [the longest x1 8.79 us: on_device(): theirs = lax.ppermute(other, 'c', swap)]
    ppermute x1 -> x2, waiting for transfers between devices: 1.23 us -> 2.2 us  [the longest x1 1.23 us: on_device(): theirs = lax.ppermute(other, 'c', swap)]
  transfers between devices with their start and end apart: 1 -> 2, of which waited for: 1 -> 2; matrix products, arithmetic and copies ran while one was open for 0% -> 0% of each run, Pallas kernels for 0% -> 0%
where the time goes in v5:
time: 105 us
  blocking collectives  82.1 us (78%)
  starting transfers between devices  13.8 us (13%)
  Pallas kernels  6.53 us (6%)
  waiting for transfers between devices  2.2 us (2%)
    all_gather x1, blocking collectives, on_device(): mixed = lax.all_gather(mixed, group)  21.3 us
    all_to_all x1, blocking collectives, on_device(): parts = exchange(parts, 'y')  16.1 us
    all_to_all x1, blocking collectives, on_device(): lower = exchange(lower, ('zh', 'zl'))  14.6 us
    all_to_all x1, blocking collectives, on_device(): mine = exchange(mine, 'y')  11.3 us
    all_to_all x1, blocking collectives, on_device(): planes = exchange(planes, 'zl')  10.6 us
    ppermute x1, starting transfers between devices, on_device(): theirs = lax.ppermute(other, 'c', swap)  8.79 us
    all_to_all x1, blocking collectives, on_device(): quarters = exchange(quarters, 'x')  8.09 us
    ppermute x1, starting transfers between devices, on_device(): theirs = lax.ppermute(mine, 'c', swap)  5.06 us
  transfers between devices with their start and end apart: 2, of which 2 were waited for; matrix products, arithmetic and copies ran while one was open for 0% of the time, Pallas kernels for 0%

profile of v5, /device:TPU:1, one launch (start us, length us, event | category | flops | bytes accessed | tf_op | source)
XLA Modules:
  0.0 104.8 jit_solution(12428689283830833262)
XLA Ops:
  0.0 0.0 copy-start.1
  0.0 3.5 %shard_map.37 = (bf16[8,160,128]{2,1,0:T(8,128)(2,1)S(1)}, bf16[8,160,128]{2,1,0:T(8,128)(2,1)S(1)}) custom-call(bf16[256,2048]{1,0:T(8,128)(2,1)} %rhs.3, bf16[5,128,2048]{2,1,0:T(8,128)(2,1)} %bases.3), custom_call_target="tpu_custom_call" | custom-call | tf_op jit(solution)/shard_map/pallas_call | solution.py:84
  3.5 8.8 %collective-permute-start = (bf16[8,160,128]{2,1,0:T(8,128)(2,1)S(1)}, bf16[8,160,128]{2,1,0:T(8,128)(2,1)S(1)}, u32[]{:S(2)}, u32[]{:S(2)}) collective-permute-start(bf16[8,160,128]{2,1,0:T(8,128)(2,1)S(1)} %get-tuple-element.10), channel_id=1, source_target_pairs={{0,1},{1,0},{2,3},{3,2},{4,5},{5,4},{6,7},{7,6},{8,9},{9,8},{10,11... | collective-permute-start | bytes 983048 | tf_op jit(solution)/shard_map/ppermute | solution.py:269
  12.3 1.2 %collective-permute-done.theirs = bf16[8,160,128]{2,1,0:T(8,128)(2,1)S(1)} collective-permute-done((bf16[8,160,128]{2,1,0:T(8,128)(2,1)S(1)}, bf16[8,160,128]{2,1,0:T(8,128)(2,1)S(1)}, u32[]{:S(2)}, u32[]{:S(2)}) %collective-permute-start) | collective-permute-done | bytes 327712 | tf_op jit(solution)/shard_map/ppermute | solution.py:269
  13.5 0.1 shard_map.38
  13.6 16.1 %all_to_all.25.parts = bf16[8,160,128]{2,1,0:T(8,128)(2,1)S(1)} all-to-all(bf16[8,160,128]{2,1,0:T(8,128)(2,1)S(1)} %shard_map.38), channel_id=1, replica_groups=mesh['zh'=2,'zl'=4,'x'=4,'y'=8,'c'=2] {'y'}, dimensions={0} | all-to-all | bytes 655360 | tf_op jit(solution)/shard_map/all_to_all | solution.py:271
  29.7 0.0 copy-done.1
  29.8 0.2 shard_map.39
  29.9 0.0 copy-start
  29.9 0.0 copy-start.2
  29.9 8.1 %all_to_all.26.quarters = bf16[4,240,128]{2,1,0:T(8,128)(2,1)S(1)} all-to-all(bf16[4,240,128]{2,1,0:T(8,128)(2,1)S(1)} %shard_map.39), channel_id=1, replica_groups=mesh['zh'=2,'zl'=4,'x'=4,'y'=8,'c'=2] {'x'}, dimensions={0} | all-to-all | bytes 491520 | tf_op jit(solution)/shard_map/all_to_all | solution.py:273
  38.0 10.6 %all_to_all.27.planes = bf16[4,32,128]{2,1,0:T(8,128)(2,1)S(1)} all-to-all(bf16[4,32,128]{2,1,0:T(8,128)(2,1)S(1)} %shard_map.40), channel_id=1, replica_groups=mesh['zh'=2,'zl'=4,'x'=4,'y'=8,'c'=2] {'zl'}, dimensions={0} | all-to-all | bytes 65536 | tf_op jit(solution)/shard_map/all_to_all | solution.py:275
  48.7 0.1 shard_map.41
  48.8 21.3 %all-gather = bf16[3584,128]{1,0:T(8,128)(2,1)S(1)} all-gather(bf16[224,128]{1,0:T(8,128)(2,1)S(1)} %shard_map.41), channel_id=2, replica_groups=mesh['zh'=2,'zl'=4,'x'=4,'y'=8,'c'=2] {'y','c'}, dimensions={0}, use_global_device_ids=true | all-gather | bytes 974848 | tf_op jit(solution)/shard_map/all_gather | solution.py:277
  70.1 0.6 shard_map.42
  70.8 14.6 %all_to_all.28.planes = bf16[8,48,128]{2,1,0:T(8,128)(2,1)S(1)} all-to-all(bf16[8,48,128]{2,1,0:T(8,128)(2,1)S(1)} %get-tuple-element.11), channel_id=1, replica_groups=mesh['zh'=2,'zl'=4,'x'=4,'y'=8,'c'=2] {'zh','zl'}, dimensions={0} | all-to-all | bytes 196608 | tf_op jit(solution)/shard_map/all_to_all | solution.py:285
  85.4 0.2 shard_map.43
  85.6 11.3 %all_to_all.29.mine = bf16[8,64,128]{2,1,0:T(8,128)(2,1)S(1)} all-to-all(bf16[8,64,128]{2,1,0:T(8,128)(2,1)S(1)} %shard_map.43), channel_id=1, replica_groups=mesh['zh'=2,'zl'=4,'x'=4,'y'=8,'c'=2] {'y'}, dimensions={0} | all-to-all | bytes 262144 | tf_op jit(solution)/shard_map/all_to_all | solution.py:287
  96.9 5.1 %collective-permute-start.1 = (bf16[8,64,128]{2,1,0:T(8,128)(2,1)S(1)}, bf16[8,64,128]{2,1,0:T(8,128)(2,1)S(1)}, u32[]{:S(2)}, u32[]{:S(2)}) collective-permute-start(bf16[8,64,128]{2,1,0:T(8,128)(2,1)S(1)} %all_to_all.29.mine), channel_id=1, source_target_pairs={{0,1},{1,0},{2,3},{3,2},{4,5},{5,4},{6,7},{7,6},{8,9},{9,8},{10,11... | collective-permute-start | bytes 393224 | tf_op jit(solution)/shard_map/ppermute | solution.py:288
  102.0 1.0 collective-permute-done.1.theirs
  103.0 0.0 copy-done
  103.0 0.0 copy-done.2
  103.0 1.8 %shard_map.44 = bf16[256,2048]{1,0:T(8,128)(2,1)} custom-call(bf16[256,2048]{1,0:T(8,128)(2,1)S(1)} %copy-done.2, bf16[5,128,2048]{2,1,0:T(8,128)(2,1)S(1)} %copy-done, bf16[16,224,128]{2,1,0:T(8,128)(2,1)S(1)} %bitcast.2, bf16[8,64,128]{2,1,0:T(8,128)(2,1)S(1)} %all_to_all.29.mine, bf16[8,64,128]{2,1,0:T(8,128)(2,1)S(1)} %collective-permute-done.1.theirs), custom_call_target="tpu_custom_call" | custom-call | tf_op jit(solution)/shard_map/pallas_call | solution.py:253
  (1 shorter events, 0.0 us)
Async XLA Ops:
  0.0 29.7 %copy-start.1 = (bf16[5,1,128,256]{3,2,1,0:T(8,128)(2,1)S(1)}, bf16[5,1,128,256]{3,2,1,0:T(8,128)(2,1)}, u32[]{:S(2)}) copy-start(bf16[5,1,128,256]{3,2,1,0:T(8,128)(2,1)} %coupling.7) | copy-start | bytes 983044
  3.5 10.0 %collective-permute-start = (bf16[8,160,128]{2,1,0:T(8,128)(2,1)S(1)}, bf16[8,160,128]{2,1,0:T(8,128)(2,1)S(1)}, u32[]{:S(2)}, u32[]{:S(2)}) collective-permute-start(bf16[8,160,128]{2,1,0:T(8,128)(2,1)S(1)} %get-tuple-element.10), channel_id=1, source_target_pairs={{0,1},{1,0},{2,3},{3,2},{4,5},{5,4},{6,7},{7,6},{8,9},{9,8},{10,11... | collective-permute-start | bytes 983048 | tf_op jit(solution)/shard_map/ppermute | solution.py:269
  29.9 73.0 %copy-start = (bf16[5,128,2048]{2,1,0:T(8,128)(2,1)S(1)}, bf16[5,128,2048]{2,1,0:T(8,128)(2,1)}, u32[]{:S(2)}) copy-start(bf16[5,128,2048]{2,1,0:T(8,128)(2,1)} %bases.3) | copy-start | bytes 7864324
  29.9 73.0 %copy-start.2 = (bf16[256,2048]{1,0:T(8,128)(2,1)S(1)}, bf16[256,2048]{1,0:T(8,128)(2,1)}, u32[]{:S(2)}) copy-start(bf16[256,2048]{1,0:T(8,128)(2,1)} %rhs.3) | copy-start | bytes 3145732
  96.9 6.0 %collective-permute-start.1 = (bf16[8,64,128]{2,1,0:T(8,128)(2,1)S(1)}, bf16[8,64,128]{2,1,0:T(8,128)(2,1)S(1)}, u32[]{:S(2)}, u32[]{:S(2)}) collective-permute-start(bf16[8,64,128]{2,1,0:T(8,128)(2,1)S(1)} %all_to_all.29.mine), channel_id=1, source_target_pairs={{0,1},{1,0},{2,3},{3,2},{4,5},{5,4},{6,7},{7,6},{8,9},{9,8},{10,11... | collective-permute-start | bytes 393224 | tf_op jit(solution)/shard_map/ppermute | solution.py:288

commit v6 on v5

--- a/solution.py
+++ b/solution.py
@@ -223,18 +223,13 @@
     one = apart(over(1, quad, 2), over(1, quad + 2, 2), coupling, 1).astype(BF16)
     two = apart(proj(pair, 2), proj(pair + 1, 2), coupling, 2).astype(BF16)
     result = jnp.concatenate([zero, one, two, keep[...]], axis=0)
-    for copy in range(HALF):
+    for copy in range(2 * HALF):
         out[copy] = result
 
 
-def apply_kernel(rhs, bases, mixed, mine, theirs, out, here, sems):
-    first = lax.axis_index("c") == 0
-    levels = []
-    for level in range(4):
-        rows = slice(ROWS * level, ROWS * (level + 1))
-        low, high = mine[:, rows].reshape(R, R), theirs[:, rows].reshape(R, R)
-        levels.append(jnp.concatenate([jnp.where(first, low, high), jnp.where(first, high, low)], axis=0))
-    everything = jnp.concatenate(levels + [gathered(mixed, 13)], axis=1)
+def apply_kernel(rhs, bases, mixed, corr, out, here, sems):
+    levels = [gathered(corr, level) for level in range(4)] + [gathered(mixed, 13)]
+    everything = jnp.concatenate(levels, axis=1)
     width = rhs.shape[1] // OUT_CHUNKS
     copies = []
     for chunk in range(OUT_CHUNKS):
@@ -283,10 +278,8 @@
         coupling,
     )
     lower = exchange(lower, ("zh", "zl"))
-    (mine,) = local_call(corr_kernel, [((HALF, 4 * ROWS, R), BF16)], lower, coupling, keep)
-    mine = exchange(mine, "y")
-    theirs = lax.ppermute(mine, "c", swap)
-    return apply_levels(rhs, bases, mixed, mine, theirs)
+    (corr,) = local_call(corr_kernel, [((2 * HALF, 4 * ROWS, R), BF16)], lower, coupling, keep)
+    return apply_levels(rhs, bases, mixed, exchange(corr, group))
 
 
 def solution(mesh):

time: 105 us -> 105 us (level)
  blocking collectives: 82.1 us -> 87.9 us
  starting transfers between devices: 13.8 us -> 8.79 us
    all_to_all x1, blocking collectives: 11.3 us -> 17.1 us  [on_device(): return apply_levels(rhs, bases, mixed, exchange(corr, group))]
    ppermute x1 -> x0, starting transfers between devices: 5.06 us -> none  [on_device(): theirs = lax.ppermute(mine, 'c', swap)]
  transfers between devices with their start and end apart: 2 -> 1, of which waited for: 2 -> 1; matrix products, arithmetic and copies ran while one was open for 0% -> 0% of each run, Pallas kernels for 0% -> 0%
where the time goes in v6:
time: 105 us
  blocking collectives  87.9 us (84%)
  starting transfers between devices  8.79 us (8%)
  Pallas kernels  6.56 us (6%)
  waiting for transfers between devices  1.23 us (1%)
    all_gather x1, blocking collectives, on_device(): mixed = lax.all_gather(mixed, group)  21.3 us
    all_to_all x1, blocking collectives, on_device(): return apply_levels(rhs, bases, mixed, exchange(corr, group))  17.1 us
    all_to_all x1, blocking collectives, on_device(): parts = exchange(parts, 'y')  16.1 us
    all_to_all x1, blocking collectives, on_device(): lower = exchange(lower, ('zh', 'zl'))  14.6 us
    all_to_all x1, blocking collectives, on_device(): planes = exchange(planes, 'zl')  10.6 us
    ppermute x1, starting transfers between devices, on_device(): theirs = lax.ppermute(other, 'c', swap)  8.79 us
    all_to_all x1, blocking collectives, on_device(): quarters = exchange(quarters, 'x')  8.09 us
    pallas_call x1, Pallas kernels, project(): pl.pallas_call(project_kernel, in_specs=[hbm, hbm], out_specs=[whole, who...  3.49 us
  transfers between devices with their start and end apart: 1, of which 1 were waited for; matrix products, arithmetic and copies ran while one was open for 0% of the time, Pallas kernels for 0%

profile of v6, /device:TPU:1, one launch (start us, length us, event | category | flops | bytes accessed | tf_op | source)
XLA Modules:
  0.0 104.6 jit_solution(5430540625600248030)
XLA Ops:
  0.0 0.0 copy-start.1
  0.0 3.5 %shard_map.37 = (bf16[8,160,128]{2,1,0:T(8,128)(2,1)S(1)}, bf16[8,160,128]{2,1,0:T(8,128)(2,1)S(1)}) custom-call(bf16[256,2048]{1,0:T(8,128)(2,1)} %rhs.3, bf16[5,128,2048]{2,1,0:T(8,128)(2,1)} %bases.3), custom_call_target="tpu_custom_call" | custom-call | tf_op jit(solution)/shard_map/pallas_call | solution.py:84
  3.5 8.8 %collective-permute-start = (bf16[8,160,128]{2,1,0:T(8,128)(2,1)S(1)}, bf16[8,160,128]{2,1,0:T(8,128)(2,1)S(1)}, u32[]{:S(2)}, u32[]{:S(2)}) collective-permute-start(bf16[8,160,128]{2,1,0:T(8,128)(2,1)S(1)} %get-tuple-element.10), channel_id=1, source_target_pairs={{0,1},{1,0},{2,3},{3,2},{4,5},{5,4},{6,7},{7,6},{8,9},{9,8},{10,11... | collective-permute-start | bytes 983048 | tf_op jit(solution)/shard_map/ppermute | solution.py:264
  12.3 1.2 %collective-permute-done.theirs = bf16[8,160,128]{2,1,0:T(8,128)(2,1)S(1)} collective-permute-done((bf16[8,160,128]{2,1,0:T(8,128)(2,1)S(1)}, bf16[8,160,128]{2,1,0:T(8,128)(2,1)S(1)}, u32[]{:S(2)}, u32[]{:S(2)}) %collective-permute-start) | collective-permute-done | bytes 327712 | tf_op jit(solution)/shard_map/ppermute | solution.py:264
  13.5 0.1 shard_map.38
  13.6 16.1 %all_to_all.25.parts = bf16[8,160,128]{2,1,0:T(8,128)(2,1)S(1)} all-to-all(bf16[8,160,128]{2,1,0:T(8,128)(2,1)S(1)} %shard_map.38), channel_id=1, replica_groups=mesh['zh'=2,'zl'=4,'x'=4,'y'=8,'c'=2] {'y'}, dimensions={0} | all-to-all | bytes 655360 | tf_op jit(solution)/shard_map/all_to_all | solution.py:266
  29.7 0.0 copy-done.1
  29.8 0.2 shard_map.39
  29.9 0.0 copy-start
  29.9 0.0 copy-start.2
  29.9 8.1 %all_to_all.26.quarters = bf16[4,240,128]{2,1,0:T(8,128)(2,1)S(1)} all-to-all(bf16[4,240,128]{2,1,0:T(8,128)(2,1)S(1)} %shard_map.39), channel_id=1, replica_groups=mesh['zh'=2,'zl'=4,'x'=4,'y'=8,'c'=2] {'x'}, dimensions={0} | all-to-all | bytes 491520 | tf_op jit(solution)/shard_map/all_to_all | solution.py:268
  38.0 10.6 %all_to_all.27.planes = bf16[4,32,128]{2,1,0:T(8,128)(2,1)S(1)} all-to-all(bf16[4,32,128]{2,1,0:T(8,128)(2,1)S(1)} %shard_map.40), channel_id=1, replica_groups=mesh['zh'=2,'zl'=4,'x'=4,'y'=8,'c'=2] {'zl'}, dimensions={0} | all-to-all | bytes 65536 | tf_op jit(solution)/shard_map/all_to_all | solution.py:270
  48.7 0.1 shard_map.41
  48.8 21.3 %all-gather = bf16[3584,128]{1,0:T(8,128)(2,1)S(1)} all-gather(bf16[224,128]{1,0:T(8,128)(2,1)S(1)} %shard_map.41), channel_id=2, replica_groups=mesh['zh'=2,'zl'=4,'x'=4,'y'=8,'c'=2] {'y','c'}, dimensions={0}, use_global_device_ids=true | all-gather | bytes 974848 | tf_op jit(solution)/shard_map/all_gather | solution.py:272
  70.1 0.6 shard_map.42
  70.8 14.6 %all_to_all.28.planes = bf16[8,48,128]{2,1,0:T(8,128)(2,1)S(1)} all-to-all(bf16[8,48,128]{2,1,0:T(8,128)(2,1)S(1)} %get-tuple-element.11), channel_id=1, replica_groups=mesh['zh'=2,'zl'=4,'x'=4,'y'=8,'c'=2] {'zh','zl'}, dimensions={0} | all-to-all | bytes 196608 | tf_op jit(solution)/shard_map/all_to_all | solution.py:280
  85.4 0.2 shard_map.43
  85.6 17.1 %all_to_all.29.corr = bf16[16,64,128]{2,1,0:T(8,128)(2,1)S(1)} all-to-all(bf16[16,64,128]{2,1,0:T(8,128)(2,1)S(1)} %shard_map.43), channel_id=1, replica_groups=mesh['zh'=2,'zl'=4,'x'=4,'y'=8,'c'=2] {'y','c'}, dimensions={0} | all-to-all | bytes 524288 | tf_op jit(solution)/shard_map/all_to_all | solution.py:282
  102.7 0.0 copy-done
  102.8 0.0 copy-done.2
  102.8 1.8 %shard_map.44 = bf16[256,2048]{1,0:T(8,128)(2,1)} custom-call(bf16[256,2048]{1,0:T(8,128)(2,1)S(1)} %copy-done.2, bf16[5,128,2048]{2,1,0:T(8,128)(2,1)S(1)} %copy-done, bf16[16,224,128]{2,1,0:T(8,128)(2,1)S(1)} %bitcast.2, bf16[16,64,128]{2,1,0:T(8,128)(2,1)S(1)} %all_to_all.29.corr), custom_call_target="tpu_custom_call" | custom-call | tf_op jit(solution)/shard_map/pallas_call | solution.py:248
  (1 shorter events, 0.0 us)
Async XLA Ops:
  0.0 29.7 %copy-start.1 = (bf16[5,1,128,256]{3,2,1,0:T(8,128)(2,1)S(1)}, bf16[5,1,128,256]{3,2,1,0:T(8,128)(2,1)}, u32[]{:S(2)}) copy-start(bf16[5,1,128,256]{3,2,1,0:T(8,128)(2,1)} %coupling.7) | copy-start | bytes 983044
  3.5 10.0 %collective-permute-start = (bf16[8,160,128]{2,1,0:T(8,128)(2,1)S(1)}, bf16[8,160,128]{2,1,0:T(8,128)(2,1)S(1)}, u32[]{:S(2)}, u32[]{:S(2)}) collective-permute-start(bf16[8,160,128]{2,1,0:T(8,128)(2,1)S(1)} %get-tuple-element.10), channel_id=1, source_target_pairs={{0,1},{1,0},{2,3},{3,2},{4,5},{5,4},{6,7},{7,6},{8,9},{9,8},{10,11... | collective-permute-start | bytes 983048 | tf_op jit(solution)/shard_map/ppermute | solution.py:264
  29.9 72.8 %copy-start = (bf16[5,128,2048]{2,1,0:T(8,128)(2,1)S(1)}, bf16[5,128,2048]{2,1,0:T(8,128)(2,1)}, u32[]{:S(2)}) copy-start(bf16[5,128,2048]{2,1,0:T(8,128)(2,1)} %bases.3) | copy-start | bytes 7864324
  29.9 72.8 %copy-start.2 = (bf16[256,2048]{1,0:T(8,128)(2,1)S(1)}, bf16[256,2048]{1,0:T(8,128)(2,1)}, u32[]{:S(2)}) copy-start(bf16[256,2048]{1,0:T(8,128)(2,1)} %rhs.3) | copy-start | bytes 3145732

commit v7 on v6

--- a/solution.py
+++ b/solution.py
@@ -71,10 +71,10 @@
 
     for level, (ref, column) in enumerate([(low, 0), (middle, 0), (middle, 1), (high, 0), (high, 1)]):
         put(level, tile(ref, 0, column), tile(ref, 1, column))
-    put(5, tile(high, 2, 1), tile(high, 3, 1))
-    put(6, tile(high, 4, 1), tile(high, 5, 1))
-    put(7, tile(high, 2, 0), tile(high, 3, 0))
-    put(8, tile(middle, 2, 1), tile(middle, 3, 1))
+    put(5, tile(high, 2, 1), tile(high, 4, 1))
+    put(6, tile(high, 3, 1), tile(high, 5, 1))
+    put(7, tile(high, 2, 0), tile(middle, 2, 1))
+    put(8, tile(high, 3, 0), tile(middle, 3, 1))
     put(9, tile(high, 4, 0), tile(middle, 2, 0))
 
 
@@ -118,12 +118,14 @@
         total += parts[source].astype(F32)
     total = total.astype(BF16)
     proj, gram = total[: 5 * ROWS], total[5 * ROWS :]
-    first = dot(gram[: 2 * ROWS], coupling[4, 0])
-    second = dot(gram[2 * ROWS : 3 * ROWS], coupling[3, 0])
-    third = dot(gram[3 * ROWS : 4 * ROWS], coupling[2, 0])
-    last = gram[4 * ROWS :]
-    fourth = jnp.where(lax.axis_index("c") == 0, dot(last, coupling[3, 0]), dot(last, coupling[1, 0]))
-    mixed = [first[:ROWS], first[ROWS:], second, third, fourth]
+    first = lax.axis_index("c") == 0
+    middle, last = gram[2 * ROWS : 4 * ROWS], gram[4 * ROWS :]
+    mixed = [
+        dot(gram[: 2 * ROWS], coupling[4, 0]),
+        jnp.where(first, dot(middle, coupling[3, 0]), dot(middle, coupling[2, 0])),
+        jnp.where(first, dot(last, coupling[3, 0]), dot(last, coupling[1, 0])),
+    ]
+    mixed = [mixed[0][:ROWS], mixed[0][ROWS:], mixed[1][:ROWS], mixed[1][ROWS:], mixed[2]]
     halves = [m[:, R * half : R * (half + 1)].astype(BF16) for m in mixed for half in (0, 1)]
     whole = jnp.concatenate([proj] + halves, axis=0)
     for copy in range(4):
@@ -136,11 +138,10 @@
 
 
 def plane_kernel(quarters, out):
-    total = quarter_sum(quarters, 11, 15).astype(BF16)
+    total = quarter_sum(quarters, 9, 15).astype(BF16)
     for plane in range(4):
-        second, first = plane % 2, 2 + plane // 2
-        out[plane, :ROWS] = total[ROWS * second : ROWS * (second + 1)]
-        out[plane, ROWS:] = total[ROWS * first : ROWS * (first + 1)]
+        for position, block in enumerate((plane % 2, 2 + plane % 2, 4 + plane // 2)):
+            out[plane, ROWS * position : ROWS * (position + 1)] = total[ROWS * block : ROWS * (block + 1)]
 
 
 def nodes_kernel(quarters, planes, coupling, out):
@@ -151,20 +152,26 @@
     def quarter(x, start, stop):
         return quarters[x, ROWS * start : ROWS * stop].astype(F32)
 
+    def over(planes_of, rows):
+        return sum((planes[plane, rows].astype(F32) for plane in planes_of[1:]), planes[planes_of[0], rows].astype(F32))
+
     for node in range(2):
         put(4 * node, quarter(2 * node, 5, 9) + quarter(2 * node + 1, 5, 9))
-    put(8, quarter_sum(quarters, 9, 11))
-    summed = planes[0].astype(F32) + planes[1].astype(F32) + planes[2].astype(F32) + planes[3].astype(F32)
-    last = quarter_sum(quarters, 13, 15)
+    pair = 2 * (lax.axis_index("zl") // 2)
+    second = over([pair, pair + 1], slice(0, 2 * ROWS))
+    first = over([0, 1, 2, 3], slice(2 * ROWS, 3 * ROWS))
+    unused = jnp.zeros((3 * ROWS, R), F32)
     here = lax.axis_index("c") == 0
-    put(10, jnp.where(here, last[:ROWS], summed[ROWS:]))
-    put(11, last[ROWS:])
-    pair = 2 * (lax.axis_index("zl") // 2)
-    put(12, planes[pair, :ROWS].astype(F32) + planes[pair + 1, :ROWS].astype(F32))
+    put(8, jnp.where(here, quarter_sum(quarters, 9, 15), jnp.concatenate([second, first, unused], axis=0)))
     node = lax.axis_index("x") // 2
-    four = ROWS * 4, ROWS * 5
-    left, right = quarters[2 * node, slice(*four)], quarters[2 * node + 1, slice(*four)]
-    put(13, apart(left, right, coupling, 4))
+    four = slice(4 * ROWS, 5 * ROWS)
+    put(14, apart(quarters[2 * node, four], quarters[2 * node + 1, four], coupling, 4))
+
+
+def of_core(ref, core, *positions):
+    return jnp.concatenate(
+        [ref[2 * y + core, ROWS * p : ROWS * (p + 1)] for p in positions for y in range(HALF)], axis=0
+    )
 
 
 def gathered(ref, position):
@@ -185,8 +192,9 @@
         left, right = proj(2 * node, 4), proj(2 * node + 1, 4)
         base = 4 * node
         updates = []
-        for part in range(2):
-            both = dot_t(left, gathered(mixed, base + 2 * part)) + dot_t(right, gathered(mixed, base + 2 * part + 1))
+        for core in range(2):
+            both = dot_t(left, of_core(mixed, core, base, base + 2))
+            both += dot_t(right, of_core(mixed, core, base + 1, base + 3))
             updates += [both[:, :R], both[:, R:]]
         sums.append(
             [
@@ -195,13 +203,12 @@
             ]
         )
     left, right = sums[0][3].astype(BF16), sums[1][3].astype(BF16)
-    both = dot_t(left, gathered(mixed, 8)) + dot_t(right, gathered(mixed, 9))
-    last = gathered(mixed, 10)
-    update = dot_t(left, last[:R]) + dot_t(right, gathered(mixed, 11)[:R])
+    both = dot_t(left, of_core(mixed, 0, 8, 10)) + dot_t(right, of_core(mixed, 0, 9, 11))
+    update = dot_t(left, of_core(mixed, 0, 12)) + dot_t(right, of_core(mixed, 0, 13))
     two = (sums[0][2] + sums[1][2] - update).astype(BF16)
-    lower = dot_t(two, gathered(mixed, 12))
+    lower = dot_t(two, of_core(mixed, 1, 8, 9))
     one = (sums[0][1] + sums[1][1] - both[:, R:] - lower[:, R:]).astype(BF16)
-    zero = sums[0][0] + sums[1][0] - both[:, :R] - lower[:, :R] - dot_t(one, last[R:])
+    zero = sums[0][0] + sums[1][0] - both[:, :R] - lower[:, :R] - dot_t(one, of_core(mixed, 1, 10))
     result = jnp.concatenate([zero.astype(BF16), one, two], axis=0)
     for copy in range(8):
         out[copy] = result
@@ -228,7 +235,7 @@
 
 
 def apply_kernel(rhs, bases, mixed, corr, out, here, sems):
-    levels = [gathered(corr, level) for level in range(4)] + [gathered(mixed, 13)]
+    levels = [gathered(corr, level) for level in range(4)] + [gathered(mixed, 14)]
     everything = jnp.concatenate(levels, axis=1)
     width = rhs.shape[1] // OUT_CHUNKS
     copies = []
@@ -266,9 +273,11 @@
     parts = exchange(parts, "y")
     (quarters,) = local_call(couple_kernel, [((4, 15 * ROWS, R), BF16)], parts, coupling)
     quarters = exchange(quarters, "x")
-    (planes,) = local_call(plane_kernel, [((4, 2 * ROWS, R), BF16)], quarters)
-    planes = exchange(planes, "zl")
-    (mixed,) = local_call(nodes_kernel, [((14 * ROWS, R), BF16)], quarters, planes, coupling)
+    (planes,) = local_call(plane_kernel, [((4, 3 * ROWS, R), BF16)], quarters)
+    planes = lax.cond(
+        lax.axis_index("c") == 1, lambda pieces: exchange(pieces, "zl"), lambda pieces: pieces, planes
+    )
+    (mixed,) = local_call(nodes_kernel, [((15 * ROWS, R), BF16)], quarters, planes, coupling)
     mixed = lax.all_gather(mixed, group)
     lower, keep = local_call(
         levels_kernel,

time: 105 us -> 101 us (0.962)
  blocking collectives: 87.9 us -> 73.6 us
  waiting for transfers between devices: 1.23 us -> 7.02 us
  starting transfers between devices: 8.79 us -> 12.2 us
    all_to_all x2 -> x1, blocking collectives: 18.7 us -> 9.48 us  [on_device(): exchange(pieces, 'zl')]
    all_to_all x0 -> x1, waiting for transfers between devices: none -> 5.78 us  [on_device(): quarters = exchange(quarters, 'x')]
    all_gather x1, blocking collectives: 21.3 us -> 17.3 us  [on_device(): mixed = lax.all_gather(mixed, group)]
    all_to_all x0 -> x1, starting transfers between devices: none -> 3.4 us  [on_device(): quarters = exchange(quarters, 'x')]
  transfers between devices with their start and end apart: 1 -> 2, of which waited for: 1 -> 2; matrix products, arithmetic and copies ran while one was open for 0% -> 0% of each run, Pallas kernels for 0% -> 0%
where the time goes in v7:
time: 101 us; the launch traced here: 100 us
  blocking collectives  73.6 us (73%)
  starting transfers between devices  12.2 us (12%)
  Pallas kernels  7.27 us (7%)
  waiting for transfers between devices  7.02 us (7%)
    all_gather x1, blocking collectives, on_device(): mixed = lax.all_gather(mixed, group)  17.3 us
    all_to_all x1, blocking collectives, on_device(): parts = exchange(parts, 'y')  16.1 us
    all_to_all x1, blocking collectives, on_device(): return apply_levels(rhs, bases, mixed, exchange(corr, group))  16.1 us
    all_to_all x1, blocking collectives, on_device(): lower = exchange(lower, ('zh', 'zl'))  14.6 us
    all_to_all x1, blocking collectives, on_device(): exchange(pieces, 'zl')  9.48 us
    ppermute x1, starting transfers between devices, on_device(): theirs = lax.ppermute(other, 'c', swap)  8.79 us
    all_to_all x1, waiting for transfers between devices, on_device(): quarters = exchange(quarters, 'x')  5.78 us
    pallas_call x1, Pallas kernels, project(): pl.pallas_call(project_kernel, in_specs=[hbm, hbm], out_specs=[whole, who...  3.49 us
  transfers between devices with their start and end apart: 2, of which 2 were waited for; matrix products, arithmetic and copies ran while one was open for 0% of the time, Pallas kernels for 0%

profile of v7, /device:TPU:1, one launch (start us, length us, event | category | flops | bytes accessed | tf_op | source)
XLA Modules:
  0.0 100.2 jit_solution(15031343648081637921)
XLA Ops:
  0.0 0.0 copy-start.1
  0.0 3.5 %shard_map.37 = (bf16[8,160,128]{2,1,0:T(8,128)(2,1)S(1)}, bf16[8,160,128]{2,1,0:T(8,128)(2,1)S(1)}) custom-call(bf16[256,2048]{1,0:T(8,128)(2,1)} %rhs.3, bf16[5,128,2048]{2,1,0:T(8,128)(2,1)} %bases.3), custom_call_target="tpu_custom_call" | custom-call | tf_op jit(solution)/shard_map/pallas_call | solution.py:84
  3.5 8.8 %collective-permute-start = (bf16[8,160,128]{2,1,0:T(8,128)(2,1)S(1)}, bf16[8,160,128]{2,1,0:T(8,128)(2,1)S(1)}, u32[]{:S(2)}, u32[]{:S(2)}) collective-permute-start(bf16[8,160,128]{2,1,0:T(8,128)(2,1)S(1)} %get-tuple-element.15), channel_id=1, source_target_pairs={{0,1},{1,0},{2,3},{3,2},{4,5},{5,4},{6,7},{7,6},{8,9},{9,8},{10,11... | collective-permute-start | bytes 983048 | tf_op jit(solution)/shard_map/ppermute | solution.py:271
  12.3 1.2 %collective-permute-done.theirs = bf16[8,160,128]{2,1,0:T(8,128)(2,1)S(1)} collective-permute-done((bf16[8,160,128]{2,1,0:T(8,128)(2,1)S(1)}, bf16[8,160,128]{2,1,0:T(8,128)(2,1)S(1)}, u32[]{:S(2)}, u32[]{:S(2)}) %collective-permute-start) | collective-permute-done | bytes 327712 | tf_op jit(solution)/shard_map/ppermute | solution.py:271
  13.5 0.1 shard_map.38
  13.6 16.1 %all_to_all.25.parts = bf16[8,160,128]{2,1,0:T(8,128)(2,1)S(1)} all-to-all(bf16[8,160,128]{2,1,0:T(8,128)(2,1)S(1)} %shard_map.38), channel_id=1, replica_groups=mesh['zh'=2,'zl'=4,'x'=4,'y'=8,'c'=2] {'y'}, dimensions={0} | all-to-all | bytes 655360 | tf_op jit(solution)/shard_map/all_to_all | solution.py:273
  29.7 0.0 copy-done.1
  29.8 0.9 shard_map.39
  30.6 3.4 %all-to-all-start.2 = ((bf16[4,240,128]{2,1,0:T(8,128)(2,1)}), bf16[4,240,128]{2,1,0:T(8,128)(2,1)S(1)}, u32[]{:S(2)}, u32[]{:S(2)}) async-start(bf16[4,240,128]{2,1,0:T(8,128)(2,1)} %shard_map.39), calls=%async_computation.2 | async-start | bytes 491520 | tf_op jit(solution)/shard_map/all_to_all | solution.py:275
  34.0 0.0 copy-start
  34.0 5.8 %all-to-all-done.2.quarters = bf16[4,240,128]{2,1,0:T(8,128)(2,1)S(1)} async-done(((bf16[4,240,128]{2,1,0:T(8,128)(2,1)}), bf16[4,240,128]{2,1,0:T(8,128)(2,1)S(1)}, u32[]{:S(2)}, u32[]{:S(2)}) %all-to-all-start.2) | async-done | bytes 245792 | tf_op jit(solution)/shard_map/all_to_all | solution.py:275
  39.8 9.5 %conditional.1 = (bf16[4,48,128]{2,1,0:T(8,128)(2,1)S(1)}) conditional(s32[]{:T(128)} %convert_element_type.3, bf16[4,48,128]{2,1,0:T(8,128)(2,1)S(1)} %shard_map.40, bf16[4,48,128]{2,1,0:T(8,128)(2,1)S(1)} %shard_map.40), branch_computations={%region_0.0_spmd, %region_1.0_spmd} | conditional | bytes 196616 | solution.py:277
  39.9 9.5 %all_to_all.24 = bf16[4,48,128]{2,1,0:T(8,128)(2,1)S(1)} all-to-all(bf16[4,48,128]{2,1,0:T(8,128)(2,1)S(1)} %copy.6), channel_id=1, replica_groups=mesh['zh'=2,'zl'=4,'x'=4,'y'=8,'c'=2] {'zl'}, dimensions={0} | all-to-all | bytes 98304 | tf_op jit(solution)/shard_map/cond/branch_1_fun/all_to_all | solution.py:278
  49.3 0.0 copy-start.2
  49.3 0.1 shard_map.41
  49.5 17.3 %all-gather = bf16[3840,128]{1,0:T(8,128)(2,1)S(1)} all-gather(bf16[240,128]{1,0:T(8,128)(2,1)S(1)} %shard_map.41), channel_id=2, replica_groups=mesh['zh'=2,'zl'=4,'x'=4,'y'=8,'c'=2] {'y','c'}, dimensions={0}, use_global_device_ids=true | all-gather | bytes 1044480 | tf_op jit(solution)/shard_map/all_gather | solution.py:281
  66.8 0.6 shard_map.42
  67.4 14.6 %all_to_all.26.planes = bf16[8,48,128]{2,1,0:T(8,128)(2,1)S(1)} all-to-all(bf16[8,48,128]{2,1,0:T(8,128)(2,1)S(1)} %get-tuple-element.16), channel_id=1, replica_groups=mesh['zh'=2,'zl'=4,'x'=4,'y'=8,'c'=2] {'zh','zl'}, dimensions={0} | all-to-all | bytes 196608 | tf_op jit(solution)/shard_map/all_to_all | solution.py:289
  82.1 0.2 shard_map.43
  82.3 16.1 %all_to_all.27.corr = bf16[16,64,128]{2,1,0:T(8,128)(2,1)S(1)} all-to-all(bf16[16,64,128]{2,1,0:T(8,128)(2,1)S(1)} %shard_map.43), channel_id=1, replica_groups=mesh['zh'=2,'zl'=4,'x'=4,'y'=8,'c'=2] {'y','c'}, dimensions={0} | all-to-all | bytes 524288 | tf_op jit(solution)/shard_map/all_to_all | solution.py:291
  98.4 0.0 copy-done
  98.4 0.0 copy-done.2
  98.4 1.8 %shard_map.44 = bf16[256,2048]{1,0:T(8,128)(2,1)} custom-call(bf16[256,2048]{1,0:T(8,128)(2,1)S(1)} %copy-done.2, bf16[5,128,2048]{2,1,0:T(8,128)(2,1)S(1)} %copy-done, bf16[16,240,128]{2,1,0:T(8,128)(2,1)S(1)} %bitcast.2, bf16[16,64,128]{2,1,0:T(8,128)(2,1)S(1)} %all_to_all.27.corr), custom_call_target="tpu_custom_call" | custom-call | tf_op jit(solution)/shard_map/pallas_call | solution.py:255
  (2 shorter events, 0.0 us)
Async XLA Ops:
  0.0 29.7 %copy-start.1 = (bf16[5,1,128,256]{3,2,1,0:T(8,128)(2,1)S(1)}, bf16[5,1,128,256]{3,2,1,0:T(8,128)(2,1)}, u32[]{:S(2)}) copy-start(bf16[5,1,128,256]{3,2,1,0:T(8,128)(2,1)} %coupling.7) | copy-start | bytes 983044
  3.5 10.0 %collective-permute-start = (bf16[8,160,128]{2,1,0:T(8,128)(2,1)S(1)}, bf16[8,160,128]{2,1,0:T(8,128)(2,1)S(1)}, u32[]{:S(2)}, u32[]{:S(2)}) collective-permute-start(bf16[8,160,128]{2,1,0:T(8,128)(2,1)S(1)} %get-tuple-element.15), channel_id=1, source_target_pairs={{0,1},{1,0},{2,3},{3,2},{4,5},{5,4},{6,7},{7,6},{8,9},{9,8},{10,11... | collective-permute-start | bytes 983048 | tf_op jit(solution)/shard_map/ppermute | solution.py:271
  30.6 9.2 %all-to-all-start.2 = ((bf16[4,240,128]{2,1,0:T(8,128)(2,1)}), bf16[4,240,128]{2,1,0:T(8,128)(2,1)S(1)}, u32[]{:S(2)}, u32[]{:S(2)}) async-start(bf16[4,240,128]{2,1,0:T(8,128)(2,1)} %shard_map.39), calls=%async_computation.2 | async-start | bytes 491520 | tf_op jit(solution)/shard_map/all_to_all | solution.py:275
  34.0 64.4 %copy-start = (bf16[5,128,2048]{2,1,0:T(8,128)(2,1)S(1)}, bf16[5,128,2048]{2,1,0:T(8,128)(2,1)}, u32[]{:S(2)}) copy-start(bf16[5,128,2048]{2,1,0:T(8,128)(2,1)} %bases.3) | copy-start | bytes 7864324
  49.3 49.0 %copy-start.2 = (bf16[256,2048]{1,0:T(8,128)(2,1)S(1)}, bf16[256,2048]{1,0:T(8,128)(2,1)}, u32[]{:S(2)}) copy-start(bf16[256,2048]{1,0:T(8,128)(2,1)} %rhs.3) | copy-start | bytes 3145732

commit v8 on v7

--- a/solution.py
+++ b/solution.py
@@ -1,3 +1,5 @@
+import functools
+
 import functools
 
 import jax
@@ -112,20 +114,14 @@
     out[...] = (mine[...].astype(F32) + theirs[...].astype(F32)).astype(BF16)
 
 
-def couple_kernel(parts, coupling, out):
+def couple_kernel(core, parts, coupling, out):
     total = parts[0].astype(F32)
     for source in range(1, HALF):
         total += parts[source].astype(F32)
     total = total.astype(BF16)
     proj, gram = total[: 5 * ROWS], total[5 * ROWS :]
-    first = lax.axis_index("c") == 0
-    middle, last = gram[2 * ROWS : 4 * ROWS], gram[4 * ROWS :]
-    mixed = [
-        dot(gram[: 2 * ROWS], coupling[4, 0]),
-        jnp.where(first, dot(middle, coupling[3, 0]), dot(middle, coupling[2, 0])),
-        jnp.where(first, dot(last, coupling[3, 0]), dot(last, coupling[1, 0])),
-    ]
-    mixed = [mixed[0][:ROWS], mixed[0][ROWS:], mixed[1][:ROWS], mixed[1][ROWS:], mixed[2]]
+    levels = (4, 4, 2, 2, 1) if core else (4, 4, 3, 3, 3)
+    mixed = [dot(gram[ROWS * p : ROWS * (p + 1)], coupling[level, 0]) for p, level in enumerate(levels)]
     halves = [m[:, R * half : R * (half + 1)].astype(BF16) for m in mixed for half in (0, 1)]
     whole = jnp.concatenate([proj] + halves, axis=0)
     for copy in range(4):
@@ -144,7 +140,10 @@
             out[plane, ROWS * position : ROWS * (position + 1)] = total[ROWS * block : ROWS * (block + 1)]
 
 
-def nodes_kernel(quarters, planes, coupling, out):
+def nodes_kernel(quarters, coupling, *planes_and_out):
+    *planes, proj, out = planes_and_out
+    proj[...] = quarters[:, : 5 * ROWS]
+
     def put(position, value):
         count = value.shape[0] // ROWS
         out[ROWS * position : ROWS * (position + count)] = value.astype(BF16)
@@ -152,17 +151,17 @@
     def quarter(x, start, stop):
         return quarters[x, ROWS * start : ROWS * stop].astype(F32)
 
-    def over(planes_of, rows):
-        return sum((planes[plane, rows].astype(F32) for plane in planes_of[1:]), planes[planes_of[0], rows].astype(F32))
-
     for node in range(2):
         put(4 * node, quarter(2 * node, 5, 9) + quarter(2 * node + 1, 5, 9))
-    pair = 2 * (lax.axis_index("zl") // 2)
-    second = over([pair, pair + 1], slice(0, 2 * ROWS))
-    first = over([0, 1, 2, 3], slice(2 * ROWS, 3 * ROWS))
-    unused = jnp.zeros((3 * ROWS, R), F32)
-    here = lax.axis_index("c") == 0
-    put(8, jnp.where(here, quarter_sum(quarters, 9, 15), jnp.concatenate([second, first, unused], axis=0)))
+    if planes:
+        (planes,) = planes
+        pair = 2 * (lax.axis_index("zl") // 2)
+        second, first = slice(0, 2 * ROWS), slice(2 * ROWS, 3 * ROWS)
+        put(8, planes[pair, second].astype(F32) + planes[pair + 1, second].astype(F32))
+        put(10, sum((planes[plane, first].astype(F32) for plane in range(1, 4)), planes[0, first].astype(F32)))
+        put(11, jnp.zeros((3 * ROWS, R), F32))
+    else:
+        put(8, quarter_sum(quarters, 9, 15))
     node = lax.axis_index("x") // 2
     four = slice(4 * ROWS, 5 * ROWS)
     put(14, apart(quarters[2 * node, four], quarters[2 * node + 1, four], coupling, 4))
@@ -270,19 +269,31 @@
     mine, other = project(rhs, bases)
     theirs = lax.ppermute(other, "c", swap)
     (parts,) = local_call(chip_kernel, [(mine.shape, BF16)], mine, theirs)
-    parts = exchange(parts, "y")
-    (quarters,) = local_call(couple_kernel, [((4, 15 * ROWS, R), BF16)], parts, coupling)
-    quarters = exchange(quarters, "x")
-    (planes,) = local_call(plane_kernel, [((4, 3 * ROWS, R), BF16)], quarters)
-    planes = lax.cond(
-        lax.axis_index("c") == 1, lambda pieces: exchange(pieces, "zl"), lambda pieces: pieces, planes
+
+    def reduce_and_mix(core, parts, coupling):
+        parts = exchange(parts, "y")
+        couple = functools.partial(couple_kernel, core)
+        (quarters,) = local_call(couple, [((4, 15 * ROWS, R), BF16)], parts, coupling)
+        quarters = exchange(quarters, "x")
+        planes = []
+        if core:
+            planes = local_call(plane_kernel, [((4, 3 * ROWS, R), BF16)], quarters)
+            planes = [exchange(planes[0], "zl")]
+        shapes = [((4, 5 * ROWS, R), BF16), ((15 * ROWS, R), BF16)]
+        return local_call(nodes_kernel, shapes, quarters, coupling, *planes)
+
+    proj, mixed = lax.cond(
+        lax.axis_index("c") == 1,
+        functools.partial(reduce_and_mix, 1),
+        functools.partial(reduce_and_mix, 0),
+        parts,
+        coupling,
     )
-    (mixed,) = local_call(nodes_kernel, [((15 * ROWS, R), BF16)], quarters, planes, coupling)
     mixed = lax.all_gather(mixed, group)
     lower, keep = local_call(
         levels_kernel,
         [((8, 3 * ROWS, R), BF16), ((ROWS, R), BF16)],
-        quarters,
+        proj,
         mixed,
         coupling,
     )

time: 101 us -> 99.6 us (0.986)
  blocking collectives: 73.6 us -> 82.6 us
  waiting for transfers between devices: 7.02 us -> 1.23 us
  starting transfers between devices: 12.2 us -> 8.79 us
    all_to_all x2 -> x3, blocking collectives: 25.6 us -> 34.6 us  [the longest x1 16.1 us: reduce_and_mix(): parts = exchange(parts, 'y')]
    all_to_all x1 -> x0, waiting for transfers between devices: 5.78 us -> none  [on_device(): quarters = exchange(quarters, 'x')]
    all_to_all x1 -> x0, starting transfers between devices: 3.4 us -> none  [on_device(): quarters = exchange(quarters, 'x')]
  transfers between devices with their start and end apart: 2 -> 1, of which waited for: 2 -> 1; matrix products, arithmetic and copies ran while one was open for 0% -> 0% of each run, Pallas kernels for 0% -> 0%
where the time goes in v8:
time: 99.6 us; the launch traced here: 99.3 us
  blocking collectives  82.6 us (83%)
  starting transfers between devices  8.79 us (9%)
  Pallas kernels  6.56 us (7%)
  waiting for transfers between devices  1.23 us (1%)
    all_gather x1, blocking collectives, on_device(): mixed = lax.all_gather(mixed, group)  17.3 us
    all_to_all x1, blocking collectives, reduce_and_mix(): parts = exchange(parts, 'y')  16.1 us
    all_to_all x1, blocking collectives, on_device(): return apply_levels(rhs, bases, mixed, exchange(corr, group))  16.1 us
    all_to_all x1, blocking collectives, on_device(): lower = exchange(lower, ('zh', 'zl'))  14.6 us
    all_to_all x1, blocking collectives, reduce_and_mix(): planes = [exchange(planes[0], 'zl')]  10.7 us
    ppermute x1, starting transfers between devices, on_device(): theirs = lax.ppermute(other, 'c', swap)  8.79 us
    all_to_all x1, blocking collectives, reduce_and_mix(): quarters = exchange(quarters, 'x')  7.83 us
    pallas_call x1, Pallas kernels, project(): pl.pallas_call(project_kernel, in_specs=[hbm, hbm], out_specs=[whole, who...  3.49 us
  transfers between devices with their start and end apart: 1, of which 1 were waited for; matrix products, arithmetic and copies ran while one was open for 0% of the time, Pallas kernels for 0%

profile of v8, /device:TPU:1, one launch (start us, length us, event | category | flops | bytes accessed | tf_op | source)
XLA Modules:
  0.0 99.3 jit_solution(12090401691015345664)
XLA Ops:
  0.0 0.0 copy-start.2
  0.0 3.5 %shard_map.37 = (bf16[8,160,128]{2,1,0:T(8,128)(2,1)S(1)}, bf16[8,160,128]{2,1,0:T(8,128)(2,1)S(1)}) custom-call(bf16[256,2048]{1,0:T(8,128)(2,1)} %rhs.3, bf16[5,128,2048]{2,1,0:T(8,128)(2,1)} %bases.3), custom_call_target="tpu_custom_call" | custom-call | tf_op jit(solution)/shard_map/pallas_call | solution.py:86
  3.5 8.8 %collective-permute-start = (bf16[8,160,128]{2,1,0:T(8,128)(2,1)S(1)}, bf16[8,160,128]{2,1,0:T(8,128)(2,1)S(1)}, u32[]{:S(2)}, u32[]{:S(2)}) collective-permute-start(bf16[8,160,128]{2,1,0:T(8,128)(2,1)S(1)} %get-tuple-element.24), channel_id=1, source_target_pairs={{0,1},{1,0},{2,3},{3,2},{4,5},{5,4},{6,7},{7,6},{8,9},{9,8},{10,11... | collective-permute-start | bytes 983048 | tf_op jit(solution)/shard_map/ppermute | solution.py:270
  12.3 1.2 %collective-permute-done.theirs = bf16[8,160,128]{2,1,0:T(8,128)(2,1)S(1)} collective-permute-done((bf16[8,160,128]{2,1,0:T(8,128)(2,1)S(1)}, bf16[8,160,128]{2,1,0:T(8,128)(2,1)S(1)}, u32[]{:S(2)}, u32[]{:S(2)}) %collective-permute-start) | collective-permute-done | bytes 327712 | tf_op jit(solution)/shard_map/ppermute | solution.py:270
  13.5 0.1 shard_map.38
  13.6 0.0 copy-done.2
  13.6 35.0 %conditional.1 = ((bf16[4,80,128]{2,1,0:T(8,128)(2,1)S(1)}, bf16[240,128]{1,0:T(8,128)(2,1)S(1)})) conditional(s32[]{:T(128)} %convert_element_type.3, (bf16[8,160,128]{2,1,0:T(8,128)(2,1)S(1)}, bf16[5,1,128,256]{3,2,1,0:T(8,128)(2,1)S(1)}) %tuple.16, (bf16[8,160,128]{2,1,0:T(8,128)(2,1)S(1)}, bf16[5,1,128,256]{3,2,1,0:T(8,128)(2,1)S(1)}) %tuple.17), branch_computations={%region_0.0_spmd, %region_1.0_spmd} | conditional | bytes 1245192 | solution.py:285
  13.6 16.1 %all_to_all.32.parts = bf16[8,160,128]{2,1,0:T(8,128)(2,1)S(1)} all-to-all(bf16[8,160,128]{2,1,0:T(8,128)(2,1)S(1)} %get-tuple-element.15), channel_id=1, replica_groups=mesh['zh'=2,'zl'=4,'x'=4,'y'=8,'c'=2] {'y'}, dimensions={0} | all-to-all | bytes 655360 | tf_op jit(solution)/shard_map/cond/branch_1_fun/all_to_all | solution.py:274
  29.8 0.2 branch_1_fun.3
  29.9 7.8 %all_to_all.33.quarters = bf16[4,240,128]{2,1,0:T(8,128)(2,1)S(1)} all-to-all(bf16[4,240,128]{2,1,0:T(8,128)(2,1)S(1)} %branch_1_fun.3), channel_id=1, replica_groups=mesh['zh'=2,'zl'=4,'x'=4,'y'=8,'c'=2] {'x'}, dimensions={0} | all-to-all | bytes 491520 | tf_op jit(solution)/shard_map/cond/branch_1_fun/all_to_all | solution.py:277
  37.8 10.7 %all_to_all.34.planes_and_out_0_ = bf16[4,48,128]{2,1,0:T(8,128)(2,1)S(1)} all-to-all(bf16[4,48,128]{2,1,0:T(8,128)(2,1)S(1)} %branch_1_fun.4), channel_id=1, replica_groups=mesh['zh'=2,'zl'=4,'x'=4,'y'=8,'c'=2] {'zl'}, dimensions={0} | all-to-all | bytes 98304 | tf_op jit(solution)/shard_map/cond/branch_1_fun/all_to_all | solution.py:281
  48.5 0.1 branch_1_fun.5
  48.6 0.0 copy-start
  48.6 0.0 copy-start.1
  48.6 17.3 %all-gather = bf16[3840,128]{1,0:T(8,128)(2,1)S(1)} all-gather(bf16[240,128]{1,0:T(8,128)(2,1)S(1)} %get-tuple-element.25), channel_id=2, replica_groups=mesh['zh'=2,'zl'=4,'x'=4,'y'=8,'c'=2] {'y','c'}, dimensions={0}, use_global_device_ids=true | all-gather | bytes 1044480 | tf_op jit(solution)/shard_map/all_gather | solution.py:292
  65.9 0.6 shard_map.39
  66.5 14.6 %all_to_all.35.planes = bf16[8,48,128]{2,1,0:T(8,128)(2,1)S(1)} all-to-all(bf16[8,48,128]{2,1,0:T(8,128)(2,1)S(1)} %get-tuple-element.27), channel_id=1, replica_groups=mesh['zh'=2,'zl'=4,'x'=4,'y'=8,'c'=2] {'zh','zl'}, dimensions={0} | all-to-all | bytes 196608 | tf_op jit(solution)/shard_map/all_to_all | solution.py:300
  81.2 0.2 shard_map.40
  81.4 16.1 %all_to_all.36.corr = bf16[16,64,128]{2,1,0:T(8,128)(2,1)S(1)} all-to-all(bf16[16,64,128]{2,1,0:T(8,128)(2,1)S(1)} %shard_map.40), channel_id=1, replica_groups=mesh['zh'=2,'zl'=4,'x'=4,'y'=8,'c'=2] {'y','c'}, dimensions={0} | all-to-all | bytes 524288 | tf_op jit(solution)/shard_map/all_to_all | solution.py:302
  97.5 0.0 copy-done
  97.5 0.0 copy-done.1
  97.5 1.8 %shard_map.41 = bf16[256,2048]{1,0:T(8,128)(2,1)} custom-call(bf16[256,2048]{1,0:T(8,128)(2,1)S(1)} %copy-done.1, bf16[5,128,2048]{2,1,0:T(8,128)(2,1)S(1)} %copy-done, bf16[16,240,128]{2,1,0:T(8,128)(2,1)S(1)} %bitcast.2, bf16[16,64,128]{2,1,0:T(8,128)(2,1)S(1)} %all_to_all.36.corr), custom_call_target="tpu_custom_call" | custom-call | tf_op jit(solution)/shard_map/pallas_call | solution.py:254
  (1 shorter events, 0.0 us)
Async XLA Ops:
  0.0 13.6 %copy-start.2 = (bf16[5,1,128,256]{3,2,1,0:T(8,128)(2,1)S(1)}, bf16[5,1,128,256]{3,2,1,0:T(8,128)(2,1)}, u32[]{:S(2)}) copy-start(bf16[5,1,128,256]{3,2,1,0:T(8,128)(2,1)} %coupling.3) | copy-start | bytes 983044
  3.5 10.0 %collective-permute-start = (bf16[8,160,128]{2,1,0:T(8,128)(2,1)S(1)}, bf16[8,160,128]{2,1,0:T(8,128)(2,1)S(1)}, u32[]{:S(2)}, u32[]{:S(2)}) collective-permute-start(bf16[8,160,128]{2,1,0:T(8,128)(2,1)S(1)} %get-tuple-element.24), channel_id=1, source_target_pairs={{0,1},{1,0},{2,3},{3,2},{4,5},{5,4},{6,7},{7,6},{8,9},{9,8},{10,11... | collective-permute-start | bytes 983048 | tf_op jit(solution)/shard_map/ppermute | solution.py:270
  48.6 48.9 %copy-start = (bf16[5,128,2048]{2,1,0:T(8,128)(2,1)S(1)}, bf16[5,128,2048]{2,1,0:T(8,128)(2,1)}, u32[]{:S(2)}) copy-start(bf16[5,128,2048]{2,1,0:T(8,128)(2,1)} %bases.3) | copy-start | bytes 7864324
  48.6 48.9 %copy-start.1 = (bf16[256,2048]{1,0:T(8,128)(2,1)S(1)}, bf16[256,2048]{1,0:T(8,128)(2,1)}, u32[]{:S(2)}) copy-start(bf16[256,2048]{1,0:T(8,128)(2,1)} %rhs.3) | copy-start | bytes 3145732

commit v9 on v8

--- a/solution.py
+++ b/solution.py
@@ -30,14 +30,16 @@
     return jnp.dot(a, b, preferred_element_type=F32)
 
 
-def project_kernel(rhs, bases, mine, other, stack, high, middle, low, sems):
+def load(rhs, rhs_rows, bases, stack, sems):
     width = rhs.shape[1] // CHUNKS
     copies = []
     for chunk in range(CHUNKS):
         columns = pl.ds(chunk * width, width)
-        copies.append([pltpu.make_async_copy(rhs.at[:, columns], stack.at[: 2 * R, columns], sems.at[0, chunk])])
+        count = rhs_rows.stop - rhs_rows.start
+        source = rhs.at[pl.ds(rhs_rows.start, count), columns]
+        copies.append([pltpu.make_async_copy(source, stack.at[pl.ds(0, count), columns], sems.at[0, chunk])])
         for level in range(5):
-            rows = pl.ds((2 + level) * R, R)
+            rows = pl.ds(count + level * R, R)
             copies[chunk].append(
                 pltpu.make_async_copy(
                     bases.at[level, :, columns], stack.at[rows, columns], sems.at[level + 1, chunk]
@@ -45,49 +47,97 @@
             )
         for copy in copies[chunk]:
             copy.start()
-
-    def add(acc, chunk, value):
-        if chunk == 0:
-            acc[...] = value
-        else:
-            acc[...] += value
-
+    return copies
+
+
+def multiply(copies, stack, products):
+    width = stack.shape[1] // CHUNKS
     for chunk in range(CHUNKS):
         columns = slice(chunk * width, (chunk + 1) * width)
         for copy in copies[chunk]:
             copy.wait()
-        add(high, chunk, dot_t(stack[: 6 * R, columns], stack[5 * R :, columns]))
-        add(middle, chunk, dot_t(stack[: 4 * R, columns], stack[3 * R : 5 * R, columns]))
-        add(low, chunk, dot_t(stack[: 2 * R, columns], stack[2 * R : 3 * R, columns]))
-
-    def tile(ref, row, column):
-        return ref[row * R : (row + 1) * R, column * R : (column + 1) * R]
-
-    first = lax.axis_index("c") == 0
-
-    def put(position, zero, one):
-        rows = slice(ROWS * position, ROWS * (position + 1))
-        zero, one = zero.astype(BF16), one.astype(BF16)
-        mine[:, rows, :] = jnp.where(first, zero, one).reshape(HALF, ROWS, R)
-        other[:, rows, :] = jnp.where(first, one, zero).reshape(HALF, ROWS, R)
-
-    for level, (ref, column) in enumerate([(low, 0), (middle, 0), (middle, 1), (high, 0), (high, 1)]):
-        put(level, tile(ref, 0, column), tile(ref, 1, column))
-    put(5, tile(high, 2, 1), tile(high, 4, 1))
-    put(6, tile(high, 3, 1), tile(high, 5, 1))
-    put(7, tile(high, 2, 0), tile(middle, 2, 1))
-    put(8, tile(high, 3, 0), tile(middle, 3, 1))
-    put(9, tile(high, 4, 0), tile(middle, 2, 0))
-
-
-def project(rhs, bases):
+        for acc, lefts, rights in products:
+            value = dot_t(
+                stack[lefts.start * R : lefts.stop * R, columns], stack[rights.start * R : rights.stop * R, columns]
+            )
+            if chunk == 0:
+                acc[: value.shape[0]] = value
+            else:
+                acc[: value.shape[0]] += value
+
+
+def tile(ref, row, column):
+    return ref[row * R : (row + 1) * R, column * R : (column + 1) * R]
+
+
+def rows_of(position):
+    return slice(ROWS * position, ROWS * (position + 1))
+
+
+def half_products(half, rhs, bases, stack, high, middle, low, sems, put):
+    copies = load(rhs, slice(R * half, R * (half + 1)), bases, stack, sems)
+    multiply(
+        copies,
+        stack,
+        [(high, slice(0, 5), slice(4, 6)), (middle, slice(0, 3), slice(2, 4)), (low, slice(0, 1), slice(1, 2))],
+    )
+    places = [(low, 0, 0), (middle, 0, 0), (middle, 0, 1), (high, 0, 0), (high, 0, 1)]
+    if half == 0:
+        places += [(high, 1, 1), (high, 2, 1), (high, 1, 0), (high, 2, 0), (high, 3, 0)]
+    else:
+        places += [(high, 3, 1), (high, 4, 1), (middle, 1, 1), (middle, 2, 1), (middle, 1, 0)]
+    for position, place in enumerate(places):
+        put(position, tile(*place))
+
+
+def project_kernel(rhs, bases, mine, other, stack, high, middle, low, sems):
+    core = lax.axis_index("c")
+
+    @pl.when(core == 0)
+    def _():
+        def put(position, value):
+            other[:, rows_of(position), :] = value.astype(BF16).reshape(HALF, ROWS, R)
+
+        half_products(1, rhs, bases, stack, high, middle, low, sems, put)
+        mine[...] = jnp.zeros_like(mine)
+
+    @pl.when(core == 1)
+    def _():
+        def put(position, zero, one):
+            other[:, rows_of(position), :] = zero.astype(BF16).reshape(HALF, ROWS, R)
+            mine[:, rows_of(position), :] = one.astype(BF16).reshape(HALF, ROWS, R)
+
+        copies = load(rhs, slice(0, 2 * R), bases, stack, sems)
+        multiply(
+            copies,
+            stack,
+            [(high, slice(0, 6), slice(5, 7)), (middle, slice(0, 4), slice(3, 5)), (low, slice(0, 2), slice(2, 3))],
+        )
+        for level, (ref, column) in enumerate([(low, 0), (middle, 0), (middle, 1), (high, 0), (high, 1)]):
+            put(level, tile(ref, 0, column), tile(ref, 1, column))
+        put(5, tile(high, 2, 1), tile(high, 4, 1))
+        put(6, tile(high, 3, 1), tile(high, 5, 1))
+        put(7, tile(high, 2, 0), tile(middle, 2, 1))
+        put(8, tile(high, 3, 0), tile(middle, 3, 1))
+        put(9, tile(high, 4, 0), tile(middle, 2, 0))
+
+
+def own_kernel(rhs, bases, theirs, out, stack, high, middle, low, sems):
+    def put(position, value):
+        rows = rows_of(position)
+        out[:, rows, :] = (value.reshape(HALF, ROWS, R) + theirs[:, rows, :].astype(F32)).astype(BF16)
+
+    half_products(0, rhs, bases, stack, high, middle, low, sems, put)
+
+
+def project(kernel, outputs, rhs, bases, *theirs):
     hbm = pl.BlockSpec(memory_space=pltpu.HBM)
     whole = pl.BlockSpec(memory_space=pltpu.VMEM)
     return pl.pallas_call(
-        project_kernel,
-        in_specs=[hbm, hbm],
-        out_specs=[whole, whole],
-        out_shape=[jax.ShapeDtypeStruct((HALF, 10 * ROWS, R), BF16)] * 2,
+        kernel,
+        in_specs=[hbm, hbm] + [whole] * len(theirs),
+        out_specs=[whole] * outputs,
+        out_shape=[jax.ShapeDtypeStruct((HALF, 10 * ROWS, R), BF16)] * outputs,
         scratch_shapes=[
             pltpu.VMEM((7 * R, rhs.shape[1]), BF16),
             pltpu.VMEM((6 * R, 2 * R), F32),
@@ -96,7 +146,7 @@
             pltpu.SemaphoreType.DMA((6, CHUNKS)),
         ],
         compiler_params=pltpu.CompilerParams(vmem_limit_bytes=PROJECT_VMEM_LIMIT),
-    )(rhs, bases)
+    )(rhs, bases, *theirs)
 
 
 def local_call(kernel, shapes, *arrays):
@@ -266,11 +316,13 @@
     swap = [(0, 1), (1, 0)]
     exchange = functools.partial(lax.all_to_all, split_axis=0, concat_axis=0)
 
-    mine, other = project(rhs, bases)
+    mine, other = project(project_kernel, 2, rhs, bases)
     theirs = lax.ppermute(other, "c", swap)
     (parts,) = local_call(chip_kernel, [(mine.shape, BF16)], mine, theirs)
 
-    def reduce_and_mix(core, parts, coupling):
+    def reduce_and_mix(core, rhs, bases, parts, coupling):
+        if not core:
+            (parts,) = project(own_kernel, 1, rhs, bases, parts)
         parts = exchange(parts, "y")
         couple = functools.partial(couple_kernel, core)
         (quarters,) = local_call(couple, [((4, 15 * ROWS, R), BF16)], parts, coupling)
@@ -286,6 +338,8 @@
         lax.axis_index("c") == 1,
         functools.partial(reduce_and_mix, 1),
         functools.partial(reduce_and_mix, 0),
+        rhs,
+        bases,
         parts,
         coupling,
     )

time: 99.6 us -> 97 us (0.974)
  blocking collectives: 82.6 us -> 80.4 us
    all_to_all x1, blocking collectives: 16.1 us -> 12.4 us  [reduce_and_mix(): parts = exchange(parts, 'y')]
where the time goes in v9:
time: 97 us; the launch traced here: 96.7 us
  blocking collectives  80.4 us (83%)
  starting transfers between devices  8.41 us (9%)
  Pallas kernels  6.61 us (7%)
  waiting for transfers between devices  1.23 us (1%)
    all_gather x1, blocking collectives, on_device(): mixed = lax.all_gather(mixed, group)  17.5 us
    all_to_all x1, blocking collectives, on_device(): return apply_levels(rhs, bases, mixed, exchange(corr, group))  16.3 us
    all_to_all x1, blocking collectives, on_device(): lower = exchange(lower, ('zh', 'zl'))  14.6 us
    all_to_all x1, blocking collectives, reduce_and_mix(): parts = exchange(parts, 'y')  12.4 us
    all_to_all x1, blocking collectives, reduce_and_mix(): planes = [exchange(planes[0], 'zl')]  11.3 us
    ppermute x1, starting transfers between devices, on_device(): theirs = lax.ppermute(other, 'c', swap)  8.41 us
    all_to_all x1, blocking collectives, reduce_and_mix(): quarters = exchange(quarters, 'x')  8.29 us
    pallas_call x1, Pallas kernels, project(): pl.pallas_call(kernel, in_specs=[hbm, hbm] + [whole] * len(theirs), out_s...  3.55 us
  transfers between devices with their start and end apart: 1, of which 1 were waited for; matrix products, arithmetic and copies ran while one was open for 0% of the time, Pallas kernels for 0%

profile of v9, /device:TPU:1, one launch (start us, length us, event | category | flops | bytes accessed | tf_op | source)
XLA Modules:
  0.0 96.7 jit_solution(1468910251624045703)
XLA Ops:
  0.0 0.0 copy-start.2
  0.0 0.0 copy-start.1
  0.0 3.6 %shard_map.37 = (bf16[8,160,128]{2,1,0:T(8,128)(2,1)S(1)}, bf16[8,160,128]{2,1,0:T(8,128)(2,1)S(1)}) custom-call(bf16[256,2048]{1,0:T(8,128)(2,1)} %rhs.3, bf16[5,128,2048]{2,1,0:T(8,128)(2,1)} %bases.3), custom_call_target="tpu_custom_call" | custom-call | tf_op jit(solution)/shard_map/pallas_call | solution.py:136
  3.6 8.4 %collective-permute-start = (bf16[8,160,128]{2,1,0:T(8,128)(2,1)S(1)}, bf16[8,160,128]{2,1,0:T(8,128)(2,1)S(1)}, u32[]{:S(2)}, u32[]{:S(2)}) collective-permute-start(bf16[8,160,128]{2,1,0:T(8,128)(2,1)S(1)} %get-tuple-element.30), channel_id=1, source_target_pairs={{0,1},{1,0},{2,3},{3,2},{4,5},{5,4},{6,7},{7,6},{8,9},{9,8},{10,11... | collective-permute-start | bytes 983048 | tf_op jit(solution)/shard_map/ppermute | solution.py:320
  12.0 1.2 %collective-permute-done.theirs = bf16[8,160,128]{2,1,0:T(8,128)(2,1)S(1)} collective-permute-done((bf16[8,160,128]{2,1,0:T(8,128)(2,1)S(1)}, bf16[8,160,128]{2,1,0:T(8,128)(2,1)S(1)}, u32[]{:S(2)}, u32[]{:S(2)}) %collective-permute-start) | collective-permute-done | bytes 327712 | tf_op jit(solution)/shard_map/ppermute | solution.py:320
  13.2 0.1 shard_map.38
  13.3 0.0 copy-done.2
  13.3 0.0 copy-done.1
  13.3 32.4 %conditional.1 = ((bf16[4,80,128]{2,1,0:T(8,128)(2,1)S(1)}, bf16[240,128]{1,0:T(8,128)(2,1)S(1)})) conditional(s32[]{:T(128)} %convert_element_type.3, (bf16[256,2048]{1,0:T(8,128)(2,1)S(1)}, bf16[5,128,2048]{2,1,0:T(8,128)(2,1)}, bf16[8,160,128]{2,1,0:T(8,128)(2,1)S(1)}, bf16[5,1,128,256]{3,2,1,0:T(8,128)(2,1)S(1)}) %tuple.19, ...), branch_computations={%region_0.0_spmd, %region_1.0_spmd} | conditional | bytes 1245192 | solution.py:337
  13.3 12.4 %all_to_all.32.parts = bf16[8,160,128]{2,1,0:T(8,128)(2,1)S(1)} all-to-all(bf16[8,160,128]{2,1,0:T(8,128)(2,1)S(1)} %get-tuple-element.21), channel_id=1, replica_groups=mesh['zh'=2,'zl'=4,'x'=4,'y'=8,'c'=2] {'y'}, dimensions={0} | all-to-all | bytes 655360 | tf_op jit(solution)/shard_map/cond/branch_1_fun/all_to_all | solution.py:326
  25.8 0.2 branch_1_fun.3
  25.9 8.3 %all_to_all.33.quarters = bf16[4,240,128]{2,1,0:T(8,128)(2,1)S(1)} all-to-all(bf16[4,240,128]{2,1,0:T(8,128)(2,1)S(1)} %branch_1_fun.3), channel_id=1, replica_groups=mesh['zh'=2,'zl'=4,'x'=4,'y'=8,'c'=2] {'x'}, dimensions={0} | all-to-all | bytes 491520 | tf_op jit(solution)/shard_map/cond/branch_1_fun/all_to_all | solution.py:329
  34.3 11.3 %all_to_all.34.planes_and_out_0_ = bf16[4,48,128]{2,1,0:T(8,128)(2,1)S(1)} all-to-all(bf16[4,48,128]{2,1,0:T(8,128)(2,1)S(1)} %branch_1_fun.4), channel_id=1, replica_groups=mesh['zh'=2,'zl'=4,'x'=4,'y'=8,'c'=2] {'zl'}, dimensions={0} | all-to-all | bytes 98304 | tf_op jit(solution)/shard_map/cond/branch_1_fun/all_to_all | solution.py:333
  45.6 0.1 branch_1_fun.5
  45.7 0.0 copy-start
  45.7 0.0 copy-start.3
  45.7 17.5 %all-gather = bf16[3840,128]{1,0:T(8,128)(2,1)S(1)} all-gather(bf16[240,128]{1,0:T(8,128)(2,1)S(1)} %get-tuple-element.31), channel_id=2, replica_groups=mesh['zh'=2,'zl'=4,'x'=4,'y'=8,'c'=2] {'y','c'}, dimensions={0}, use_global_device_ids=true | all-gather | bytes 1044480 | tf_op jit(solution)/shard_map/all_gather | solution.py:346
  63.2 0.6 shard_map.39
  63.8 14.6 %all_to_all.35.planes = bf16[8,48,128]{2,1,0:T(8,128)(2,1)S(1)} all-to-all(bf16[8,48,128]{2,1,0:T(8,128)(2,1)S(1)} %get-tuple-element.33), channel_id=1, replica_groups=mesh['zh'=2,'zl'=4,'x'=4,'y'=8,'c'=2] {'zh','zl'}, dimensions={0} | all-to-all | bytes 196608 | tf_op jit(solution)/shard_map/all_to_all | solution.py:354
  78.4 0.2 shard_map.40
  78.7 16.3 %all_to_all.36.corr = bf16[16,64,128]{2,1,0:T(8,128)(2,1)S(1)} all-to-all(bf16[16,64,128]{2,1,0:T(8,128)(2,1)S(1)} %shard_map.40), channel_id=1, replica_groups=mesh['zh'=2,'zl'=4,'x'=4,'y'=8,'c'=2] {'y','c'}, dimensions={0} | all-to-all | bytes 524288 | tf_op jit(solution)/shard_map/all_to_all | solution.py:356
  94.9 0.0 copy-done
  94.9 0.0 copy-done.3
  94.9 1.8 %shard_map.41 = bf16[256,2048]{1,0:T(8,128)(2,1)} custom-call(bf16[256,2048]{1,0:T(8,128)(2,1)S(1)} %copy-done.3, bf16[5,128,2048]{2,1,0:T(8,128)(2,1)S(1)} %copy-done, bf16[16,240,128]{2,1,0:T(8,128)(2,1)S(1)} %bitcast.2, bf16[16,64,128]{2,1,0:T(8,128)(2,1)S(1)} %all_to_all.36.corr), custom_call_target="tpu_custom_call" | custom-call | tf_op jit(solution)/shard_map/pallas_call | solution.py:304
  (1 shorter events, 0.0 us)
Async XLA Ops:
  0.0 13.3 %copy-start.2 = (bf16[256,2048]{1,0:T(8,128)(2,1)S(1)}, bf16[256,2048]{1,0:T(8,128)(2,1)}, u32[]{:S(2)}) copy-start(bf16[256,2048]{1,0:T(8,128)(2,1)} %rhs.3) | copy-start | bytes 3145732
  0.0 13.3 %copy-start.1 = (bf16[5,1,128,256]{3,2,1,0:T(8,128)(2,1)S(1)}, bf16[5,1,128,256]{3,2,1,0:T(8,128)(2,1)}, u32[]{:S(2)}) copy-start(bf16[5,1,128,256]{3,2,1,0:T(8,128)(2,1)} %coupling.3) | copy-start | bytes 983044
  3.6 9.7 %collective-permute-start = (bf16[8,160,128]{2,1,0:T(8,128)(2,1)S(1)}, bf16[8,160,128]{2,1,0:T(8,128)(2,1)S(1)}, u32[]{:S(2)}, u32[]{:S(2)}) collective-permute-start(bf16[8,160,128]{2,1,0:T(8,128)(2,1)S(1)} %get-tuple-element.30), channel_id=1, source_target_pairs={{0,1},{1,0},{2,3},{3,2},{4,5},{5,4},{6,7},{7,6},{8,9},{9,8},{10,11... | collective-permute-start | bytes 983048 | tf_op jit(solution)/shard_map/ppermute | solution.py:320
  45.7 49.2 %copy-start = (bf16[5,128,2048]{2,1,0:T(8,128)(2,1)S(1)}, bf16[5,128,2048]{2,1,0:T(8,128)(2,1)}, u32[]{:S(2)}) copy-start(bf16[5,128,2048]{2,1,0:T(8,128)(2,1)} %bases.3) | copy-start | bytes 7864324
  45.7 49.2 %copy-start.3 = (bf16[256,2048]{1,0:T(8,128)(2,1)S(1)}, bf16[256,2048]{1,0:T(8,128)(2,1)}, u32[]{:S(2)}) copy-start(bf16[256,2048]{1,0:T(8,128)(2,1)} %rhs.3) | copy-start | bytes 3145732

commit v10 on v9

--- a/solution.py
+++ b/solution.py
@@ -13,7 +13,7 @@
 
 ROWS = 16
 R = 128
-CHUNKS = 2
+CHUNKS = (768, 1280)
 OUT_CHUNKS = 2
 HALF = 8
 F32 = jnp.float32
@@ -31,10 +31,9 @@
 
 
 def load(rhs, rhs_rows, bases, stack, sems):
-    width = rhs.shape[1] // CHUNKS
     copies = []
-    for chunk in range(CHUNKS):
-        columns = pl.ds(chunk * width, width)
+    for chunk, width in enumerate(CHUNKS):
+        columns = pl.ds(sum(CHUNKS[:chunk]), width)
         count = rhs_rows.stop - rhs_rows.start
         source = rhs.at[pl.ds(rhs_rows.start, count), columns]
         copies.append([pltpu.make_async_copy(source, stack.at[pl.ds(0, count), columns], sems.at[0, chunk])])
@@ -51,9 +50,8 @@
 
 
 def multiply(copies, stack, products):
-    width = stack.shape[1] // CHUNKS
-    for chunk in range(CHUNKS):
-        columns = slice(chunk * width, (chunk + 1) * width)
+    for chunk, width in enumerate(CHUNKS):
+        columns = slice(sum(CHUNKS[:chunk]), sum(CHUNKS[: chunk + 1]))
         for copy in copies[chunk]:
             copy.wait()
         for acc, lefts, rights in products:
@@ -143,7 +141,7 @@
             pltpu.VMEM((6 * R, 2 * R), F32),
             pltpu.VMEM((4 * R, 2 * R), F32),
             pltpu.VMEM((2 * R, R), F32),
-            pltpu.SemaphoreType.DMA((6, CHUNKS)),
+            pltpu.SemaphoreType.DMA((6, len(CHUNKS))),
         ],
         compiler_params=pltpu.CompilerParams(vmem_limit_bytes=PROJECT_VMEM_LIMIT),
     )(rhs, bases, *theirs)
@@ -229,21 +227,22 @@
 
 
 def apart(left, right, coupling, level):
-    return dot_t(left, coupling[level, 0][:, :R]) + dot_t(right, coupling[level, 0][:, R:])
+    return dot_t(jnp.concatenate([left, right], axis=1), coupling[level, 0])
 
 
 def levels_kernel(quarters, mixed, coupling, out, keep):
     def proj(x, level):
         return quarters[x, ROWS * level : ROWS * (level + 1)]
 
+    def blocks(core, *positions):
+        return jnp.concatenate([of_core(mixed, core, *positions), of_core(mixed, core, *(p + 1 for p in positions))], axis=1)
+
     sums = []
     for node in range(2):
-        left, right = proj(2 * node, 4), proj(2 * node + 1, 4)
-        base = 4 * node
+        pair = jnp.concatenate([proj(2 * node, 4), proj(2 * node + 1, 4)], axis=1)
         updates = []
         for core in range(2):
-            both = dot_t(left, of_core(mixed, core, base, base + 2))
-            both += dot_t(right, of_core(mixed, core, base + 1, base + 3))
+            both = dot_t(pair, blocks(core, 4 * node, 4 * node + 2))
             updates += [both[:, :R], both[:, R:]]
         sums.append(
             [
@@ -252,9 +251,9 @@
             ]
         )
     left, right = sums[0][3].astype(BF16), sums[1][3].astype(BF16)
-    both = dot_t(left, of_core(mixed, 0, 8, 10)) + dot_t(right, of_core(mixed, 0, 9, 11))
-    update = dot_t(left, of_core(mixed, 0, 12)) + dot_t(right, of_core(mixed, 0, 13))
-    two = (sums[0][2] + sums[1][2] - update).astype(BF16)
+    pair = jnp.concatenate([left, right], axis=1)
+    both = dot_t(pair, blocks(0, 8, 10))
+    two = (sums[0][2] + sums[1][2] - dot_t(pair, blocks(0, 12))).astype(BF16)
     lower = dot_t(two, of_core(mixed, 1, 8, 9))
     one = (sums[0][1] + sums[1][1] - both[:, R:] - lower[:, R:]).astype(BF16)
     zero = sums[0][0] + sums[1][0] - both[:, :R] - lower[:, :R] - dot_t(one, of_core(mixed, 1, 10))

time: 97 us -> 96.8 us (level)
  no operation moved by 1% of the time
where the time goes in v10:
time: 96.8 us; the launch traced here: 96.5 us
  blocking collectives  80.3 us (83%)
  starting transfers between devices  8.48 us (9%)
  Pallas kernels  6.4 us (7%)
  waiting for transfers between devices  1.23 us (1%)
    all_gather x1, blocking collectives, on_device(): mixed = lax.all_gather(mixed, group)  17.4 us
    all_to_all x1, blocking collectives, on_device(): return apply_levels(rhs, bases, mixed, exchange(corr, group))  16.3 us
    all_to_all x1, blocking collectives, on_device(): lower = exchange(lower, ('zh', 'zl'))  14.6 us
    all_to_all x1, blocking collectives, reduce_and_mix(): parts = exchange(parts, 'y')  12.4 us
    all_to_all x1, blocking collectives, reduce_and_mix(): planes = [exchange(planes[0], 'zl')]  11.3 us
    ppermute x1, starting transfers between devices, on_device(): theirs = lax.ppermute(other, 'c', swap)  8.48 us
    all_to_all x1, blocking collectives, reduce_and_mix(): quarters = exchange(quarters, 'x')  8.22 us
    pallas_call x1, Pallas kernels, project(): pl.pallas_call(kernel, in_specs=[hbm, hbm] + [whole] * len(theirs), out_s...  3.45 us
  transfers between devices with their start and end apart: 1, of which 1 were waited for; matrix products, arithmetic and copies ran while one was open for 0% of the time, Pallas kernels for 0%

profile of v10, /device:TPU:1, one launch (start us, length us, event | category | flops | bytes accessed | tf_op | source)
XLA Modules:
  0.0 96.5 jit_solution(4167620801707328455)
XLA Ops:
  0.0 0.0 copy-start.2
  0.0 0.0 copy-start.1
  0.0 3.5 %shard_map.37 = (bf16[8,160,128]{2,1,0:T(8,128)(2,1)S(1)}, bf16[8,160,128]{2,1,0:T(8,128)(2,1)S(1)}) custom-call(bf16[256,2048]{1,0:T(8,128)(2,1)} %rhs.3, bf16[5,128,2048]{2,1,0:T(8,128)(2,1)} %bases.3), custom_call_target="tpu_custom_call" | custom-call | tf_op jit(solution)/shard_map/pallas_call | solution.py:134
  3.5 8.5 %collective-permute-start = (bf16[8,160,128]{2,1,0:T(8,128)(2,1)S(1)}, bf16[8,160,128]{2,1,0:T(8,128)(2,1)S(1)}, u32[]{:S(2)}, u32[]{:S(2)}) collective-permute-start(bf16[8,160,128]{2,1,0:T(8,128)(2,1)S(1)} %get-tuple-element.30), channel_id=1, source_target_pairs={{0,1},{1,0},{2,3},{3,2},{4,5},{5,4},{6,7},{7,6},{8,9},{9,8},{10,11... | collective-permute-start | bytes 983048 | tf_op jit(solution)/shard_map/ppermute | solution.py:319
  12.0 1.2 %collective-permute-done.theirs = bf16[8,160,128]{2,1,0:T(8,128)(2,1)S(1)} collective-permute-done((bf16[8,160,128]{2,1,0:T(8,128)(2,1)S(1)}, bf16[8,160,128]{2,1,0:T(8,128)(2,1)S(1)}, u32[]{:S(2)}, u32[]{:S(2)}) %collective-permute-start) | collective-permute-done | bytes 327712 | tf_op jit(solution)/shard_map/ppermute | solution.py:319
  13.2 0.1 shard_map.38
  13.3 0.0 copy-done.2
  13.3 0.0 copy-done.1
  13.3 32.3 %conditional.1 = ((bf16[4,80,128]{2,1,0:T(8,128)(2,1)S(1)}, bf16[240,128]{1,0:T(8,128)(2,1)S(1)})) conditional(s32[]{:T(128)} %convert_element_type.3, (bf16[256,2048]{1,0:T(8,128)(2,1)S(1)}, bf16[5,128,2048]{2,1,0:T(8,128)(2,1)}, bf16[8,160,128]{2,1,0:T(8,128)(2,1)S(1)}, bf16[5,1,128,256]{3,2,1,0:T(8,128)(2,1)S(1)}) %tuple.19, ...), branch_computations={%region_0.0_spmd, %region_1.0_spmd} | conditional | bytes 1245192 | solution.py:336
  13.3 12.4 %all_to_all.32.parts = bf16[8,160,128]{2,1,0:T(8,128)(2,1)S(1)} all-to-all(bf16[8,160,128]{2,1,0:T(8,128)(2,1)S(1)} %get-tuple-element.21), channel_id=1, replica_groups=mesh['zh'=2,'zl'=4,'x'=4,'y'=8,'c'=2] {'y'}, dimensions={0} | all-to-all | bytes 655360 | tf_op jit(solution)/shard_map/cond/branch_1_fun/all_to_all | solution.py:325
  25.7 0.2 branch_1_fun.3
  25.9 8.2 %all_to_all.33.quarters = bf16[4,240,128]{2,1,0:T(8,128)(2,1)S(1)} all-to-all(bf16[4,240,128]{2,1,0:T(8,128)(2,1)S(1)} %branch_1_fun.3), channel_id=1, replica_groups=mesh['zh'=2,'zl'=4,'x'=4,'y'=8,'c'=2] {'x'}, dimensions={0} | all-to-all | bytes 491520 | tf_op jit(solution)/shard_map/cond/branch_1_fun/all_to_all | solution.py:328
  34.2 11.3 %all_to_all.34.planes_and_out_0_ = bf16[4,48,128]{2,1,0:T(8,128)(2,1)S(1)} all-to-all(bf16[4,48,128]{2,1,0:T(8,128)(2,1)S(1)} %branch_1_fun.4), channel_id=1, replica_groups=mesh['zh'=2,'zl'=4,'x'=4,'y'=8,'c'=2] {'zl'}, dimensions={0} | all-to-all | bytes 98304 | tf_op jit(solution)/shard_map/cond/branch_1_fun/all_to_all | solution.py:332
  45.5 0.1 branch_1_fun.5
  45.6 0.0 copy-start
  45.6 0.0 copy-start.3
  45.6 17.4 %all-gather = bf16[3840,128]{1,0:T(8,128)(2,1)S(1)} all-gather(bf16[240,128]{1,0:T(8,128)(2,1)S(1)} %get-tuple-element.31), channel_id=2, replica_groups=mesh['zh'=2,'zl'=4,'x'=4,'y'=8,'c'=2] {'y','c'}, dimensions={0}, use_global_device_ids=true | all-gather | bytes 1044480 | tf_op jit(solution)/shard_map/all_gather | solution.py:345
  63.1 0.6 shard_map.39
  63.6 14.6 %all_to_all.35.planes = bf16[8,48,128]{2,1,0:T(8,128)(2,1)S(1)} all-to-all(bf16[8,48,128]{2,1,0:T(8,128)(2,1)S(1)} %get-tuple-element.33), channel_id=1, replica_groups=mesh['zh'=2,'zl'=4,'x'=4,'y'=8,'c'=2] {'zh','zl'}, dimensions={0} | all-to-all | bytes 196608 | tf_op jit(solution)/shard_map/all_to_all | solution.py:353
  78.3 0.2 shard_map.40
  78.4 16.3 %all_to_all.36.corr = bf16[16,64,128]{2,1,0:T(8,128)(2,1)S(1)} all-to-all(bf16[16,64,128]{2,1,0:T(8,128)(2,1)S(1)} %shard_map.40), channel_id=1, replica_groups=mesh['zh'=2,'zl'=4,'x'=4,'y'=8,'c'=2] {'y','c'}, dimensions={0} | all-to-all | bytes 524288 | tf_op jit(solution)/shard_map/all_to_all | solution.py:355
  94.7 0.0 copy-done
  94.7 0.0 copy-done.3
  94.7 1.8 %shard_map.41 = bf16[256,2048]{1,0:T(8,128)(2,1)} custom-call(bf16[256,2048]{1,0:T(8,128)(2,1)S(1)} %copy-done.3, bf16[5,128,2048]{2,1,0:T(8,128)(2,1)S(1)} %copy-done, bf16[16,240,128]{2,1,0:T(8,128)(2,1)S(1)} %bitcast.2, bf16[16,64,128]{2,1,0:T(8,128)(2,1)S(1)} %all_to_all.36.corr), custom_call_target="tpu_custom_call" | custom-call | tf_op jit(solution)/shard_map/pallas_call | solution.py:303
  (1 shorter events, 0.0 us)
Async XLA Ops:
  0.0 13.3 %copy-start.2 = (bf16[256,2048]{1,0:T(8,128)(2,1)S(1)}, bf16[256,2048]{1,0:T(8,128)(2,1)}, u32[]{:S(2)}) copy-start(bf16[256,2048]{1,0:T(8,128)(2,1)} %rhs.3) | copy-start | bytes 3145732
  0.0 13.3 %copy-start.1 = (bf16[5,1,128,256]{3,2,1,0:T(8,128)(2,1)S(1)}, bf16[5,1,128,256]{3,2,1,0:T(8,128)(2,1)}, u32[]{:S(2)}) copy-start(bf16[5,1,128,256]{3,2,1,0:T(8,128)(2,1)} %coupling.3) | copy-start | bytes 983044
  3.5 9.7 %collective-permute-start = (bf16[8,160,128]{2,1,0:T(8,128)(2,1)S(1)}, bf16[8,160,128]{2,1,0:T(8,128)(2,1)S(1)}, u32[]{:S(2)}, u32[]{:S(2)}) collective-permute-start(bf16[8,160,128]{2,1,0:T(8,128)(2,1)S(1)} %get-tuple-element.30), channel_id=1, source_target_pairs={{0,1},{1,0},{2,3},{3,2},{4,5},{5,4},{6,7},{7,6},{8,9},{9,8},{10,11... | collective-permute-start | bytes 983048 | tf_op jit(solution)/shard_map/ppermute | solution.py:319
  45.6 49.1 %copy-start = (bf16[5,128,2048]{2,1,0:T(8,128)(2,1)S(1)}, bf16[5,128,2048]{2,1,0:T(8,128)(2,1)}, u32[]{:S(2)}) copy-start(bf16[5,128,2048]{2,1,0:T(8,128)(2,1)} %bases.3) | copy-start | bytes 7864324
  45.6 49.1 %copy-start.3 = (bf16[256,2048]{1,0:T(8,128)(2,1)S(1)}, bf16[256,2048]{1,0:T(8,128)(2,1)}, u32[]{:S(2)}) copy-start(bf16[256,2048]{1,0:T(8,128)(2,1)} %rhs.3) | copy-start | bytes 3145732

commit v11 on v9

--- a/solution.py
+++ b/solution.py
@@ -1,5 +1,3 @@
-import functools
-
 import functools
 
 import jax
@@ -164,13 +162,13 @@
     out[...] = (mine[...].astype(F32) + theirs[...].astype(F32)).astype(BF16)
 
 
-def couple_kernel(core, parts, coupling, out):
+def couple_kernel(parts, coupling, out):
     total = parts[0].astype(F32)
     for source in range(1, HALF):
         total += parts[source].astype(F32)
     total = total.astype(BF16)
     proj, gram = total[: 5 * ROWS], total[5 * ROWS :]
-    levels = (4, 4, 2, 2, 1) if core else (4, 4, 3, 3, 3)
+    levels = (4, 4, 3, 3, 3)
     mixed = [dot(gram[ROWS * p : ROWS * (p + 1)], coupling[level, 0]) for p, level in enumerate(levels)]
     halves = [m[:, R * half : R * (half + 1)].astype(BF16) for m in mixed for half in (0, 1)]
     whole = jnp.concatenate([proj] + halves, axis=0)
@@ -178,20 +176,37 @@
         out[copy] = whole
 
 
+def couple_one_kernel(parts, coupling, first, planes):
+    total = parts[0].astype(F32)
+    for source in range(1, HALF):
+        total += parts[source].astype(F32)
+    total = total.astype(BF16)
+    gram = total[5 * ROWS :]
+    mixed = [dot(gram[ROWS * p : ROWS * (p + 1)], coupling[level, 0]) for p, level in enumerate((4, 4, 2, 2, 1))]
+    halves = [[m[:, :R].astype(BF16), m[:, R:].astype(BF16)] for m in mixed]
+    first[...] = jnp.concatenate([total[: 5 * ROWS]] + halves[0] + halves[1], axis=0)
+    for plane in range(4):
+        planes[plane] = jnp.concatenate(
+            [halves[2][plane % 2], halves[3][plane % 2], halves[4][plane // 2]], axis=0
+        )
+
+
+def join_kernel(first, planes, out):
+    pair = 2 * (lax.axis_index("zl") // 2)
+    two, one = slice(0, 2 * ROWS), slice(2 * ROWS, 3 * ROWS)
+    seconds = planes[pair, two].astype(F32) + planes[pair + 1, two].astype(F32)
+    firsts = sum((planes[plane, one].astype(F32) for plane in range(1, 4)), planes[0, one].astype(F32))
+    whole = jnp.concatenate([first[...], seconds.astype(BF16), firsts.astype(BF16)], axis=0)
+    for copy in range(4):
+        out[copy] = whole
+
+
 def quarter_sum(quarters, start, stop):
     rows = slice(ROWS * start, ROWS * stop)
     return sum((quarters[x, rows].astype(F32) for x in range(1, 4)), quarters[0, rows].astype(F32))
 
 
-def plane_kernel(quarters, out):
-    total = quarter_sum(quarters, 9, 15).astype(BF16)
-    for plane in range(4):
-        for position, block in enumerate((plane % 2, 2 + plane % 2, 4 + plane // 2)):
-            out[plane, ROWS * position : ROWS * (position + 1)] = total[ROWS * block : ROWS * (block + 1)]
-
-
-def nodes_kernel(quarters, coupling, *planes_and_out):
-    *planes, proj, out = planes_and_out
+def nodes_kernel(core, quarters, coupling, proj, out):
     proj[...] = quarters[:, : 5 * ROWS]
 
     def put(position, value):
@@ -203,12 +218,8 @@
 
     for node in range(2):
         put(4 * node, quarter(2 * node, 5, 9) + quarter(2 * node + 1, 5, 9))
-    if planes:
-        (planes,) = planes
-        pair = 2 * (lax.axis_index("zl") // 2)
-        second, first = slice(0, 2 * ROWS), slice(2 * ROWS, 3 * ROWS)
-        put(8, planes[pair, second].astype(F32) + planes[pair + 1, second].astype(F32))
-        put(10, sum((planes[plane, first].astype(F32) for plane in range(1, 4)), planes[0, first].astype(F32)))
+    if core:
+        put(8, quarter_sum(quarters, 9, 12))
         put(11, jnp.zeros((3 * ROWS, R), F32))
     else:
         put(8, quarter_sum(quarters, 9, 15))
@@ -324,15 +335,16 @@
         if not core:
             (parts,) = project(own_kernel, 1, rhs, bases, parts)
         parts = exchange(parts, "y")
-        couple = functools.partial(couple_kernel, core)
-        (quarters,) = local_call(couple, [((4, 15 * ROWS, R), BF16)], parts, coupling)
+        if core:
+            shapes = [((9 * ROWS, R), BF16), ((4, 3 * ROWS, R), BF16)]
+            first, planes = local_call(couple_one_kernel, shapes, parts, coupling)
+            planes = exchange(planes, "zl")
+            (quarters,) = local_call(join_kernel, [((4, 12 * ROWS, R), BF16)], first, planes)
+        else:
+            (quarters,) = local_call(couple_kernel, [((4, 15 * ROWS, R), BF16)], parts, coupling)
         quarters = exchange(quarters, "x")
-        planes = []
-        if core:
-            planes = local_call(plane_kernel, [((4, 3 * ROWS, R), BF16)], quarters)
-            planes = [exchange(planes[0], "zl")]
         shapes = [((4, 5 * ROWS, R), BF16), ((15 * ROWS, R), BF16)]
-        return local_call(nodes_kernel, shapes, quarters, coupling, *planes)
+        return local_call(functools.partial(nodes_kernel, core), shapes, quarters, coupling)
 
     proj, mixed = lax.cond(
         lax.axis_index("c") == 1,

time: 97 us -> 96.8 us (level)
  no operation moved by 1% of the time
where the time goes in v11:
time: 96.8 us; the launch traced here: 96.5 us
  blocking collectives  80.1 us (83%)
  starting transfers between devices  8.41 us (9%)
  Pallas kernels  6.64 us (7%)
  waiting for transfers between devices  1.23 us (1%)
    all_gather x1, blocking collectives, on_device(): mixed = lax.all_gather(mixed, group)  17.5 us
    all_to_all x1, blocking collectives, on_device(): return apply_levels(rhs, bases, mixed, exchange(corr, group))  16.3 us
    all_to_all x1, blocking collectives, on_device(): lower = exchange(lower, ('zh', 'zl'))  14.6 us
    all_to_all x1, blocking collectives, reduce_and_mix(): parts = exchange(parts, 'y')  12.4 us
    all_to_all x1, blocking collectives, reduce_and_mix(): planes = exchange(planes, 'zl')  10.4 us
    all_to_all x1, blocking collectives, reduce_and_mix(): quarters = exchange(quarters, 'x')  8.99 us
    ppermute x1, starting transfers between devices, on_device(): theirs = lax.ppermute(other, 'c', swap)  8.41 us
    pallas_call x1, Pallas kernels, project(): pl.pallas_call(kernel, in_specs=[hbm, hbm] + [whole] * len(theirs), out_s...  3.55 us
  transfers between devices with their start and end apart: 1, of which 1 were waited for; matrix products, arithmetic and copies ran while one was open for 0% of the time, Pallas kernels for 0%

profile of v11, /device:TPU:1, one launch (start us, length us, event | category | flops | bytes accessed | tf_op | source)
XLA Modules:
  0.0 96.5 jit_solution(4681349644864494615)
XLA Ops:
  0.0 0.0 copy-start.2
  0.0 0.0 copy-start.1
  0.0 3.6 %shard_map.37 = (bf16[8,160,128]{2,1,0:T(8,128)(2,1)S(1)}, bf16[8,160,128]{2,1,0:T(8,128)(2,1)S(1)}) custom-call(bf16[256,2048]{1,0:T(8,128)(2,1)} %rhs.3, bf16[5,128,2048]{2,1,0:T(8,128)(2,1)} %bases.3), custom_call_target="tpu_custom_call" | custom-call | tf_op jit(solution)/shard_map/pallas_call | solution.py:134
  3.6 8.4 %collective-permute-start = (bf16[8,160,128]{2,1,0:T(8,128)(2,1)S(1)}, bf16[8,160,128]{2,1,0:T(8,128)(2,1)S(1)}, u32[]{:S(2)}, u32[]{:S(2)}) collective-permute-start(bf16[8,160,128]{2,1,0:T(8,128)(2,1)S(1)} %get-tuple-element.32), channel_id=1, source_target_pairs={{0,1},{1,0},{2,3},{3,2},{4,5},{5,4},{6,7},{7,6},{8,9},{9,8},{10,11... | collective-permute-start | bytes 983048 | tf_op jit(solution)/shard_map/ppermute | solution.py:331
  12.0 1.2 %collective-permute-done.theirs = bf16[8,160,128]{2,1,0:T(8,128)(2,1)S(1)} collective-permute-done((bf16[8,160,128]{2,1,0:T(8,128)(2,1)S(1)}, bf16[8,160,128]{2,1,0:T(8,128)(2,1)S(1)}, u32[]{:S(2)}, u32[]{:S(2)}) %collective-permute-start) | collective-permute-done | bytes 327712 | tf_op jit(solution)/shard_map/ppermute | solution.py:331
  13.2 0.1 shard_map.38
  13.3 0.0 copy-done.2
  13.3 0.0 copy-done.1
  13.3 32.2 %conditional.1 = ((bf16[4,80,128]{2,1,0:T(8,128)(2,1)S(1)}, bf16[240,128]{1,0:T(8,128)(2,1)S(1)})) conditional(s32[]{:T(128)} %convert_element_type.3, (bf16[256,2048]{1,0:T(8,128)(2,1)S(1)}, bf16[5,128,2048]{2,1,0:T(8,128)(2,1)}, bf16[8,160,128]{2,1,0:T(8,128)(2,1)S(1)}, bf16[5,1,128,256]{3,2,1,0:T(8,128)(2,1)S(1)}) %tuple.19, ...), branch_computations={%region_0.0_spmd, %region_1.0_spmd} | conditional | bytes 1146888 | solution.py:349
  13.3 12.4 %all_to_all.32.parts = bf16[8,160,128]{2,1,0:T(8,128)(2,1)S(1)} all-to-all(bf16[8,160,128]{2,1,0:T(8,128)(2,1)S(1)} %get-tuple-element.21), channel_id=1, replica_groups=mesh['zh'=2,'zl'=4,'x'=4,'y'=8,'c'=2] {'y'}, dimensions={0} | all-to-all | bytes 655360 | tf_op jit(solution)/shard_map/cond/branch_1_fun/all_to_all | solution.py:337
  25.8 0.2 branch_1_fun.3
  25.9 10.4 %all_to_all.33.planes = bf16[4,48,128]{2,1,0:T(8,128)(2,1)S(1)} all-to-all(bf16[4,48,128]{2,1,0:T(8,128)(2,1)S(1)} %get-tuple-element.24), channel_id=1, replica_groups=mesh['zh'=2,'zl'=4,'x'=4,'y'=8,'c'=2] {'zl'}, dimensions={0} | all-to-all | bytes 98304 | tf_op jit(solution)/shard_map/cond/branch_1_fun/all_to_all | solution.py:341
  36.3 9.0 %all_to_all.34.quarters = bf16[4,192,128]{2,1,0:T(8,128)(2,1)S(1)} all-to-all(bf16[4,192,128]{2,1,0:T(8,128)(2,1)S(1)} %branch_1_fun.4), channel_id=1, replica_groups=mesh['zh'=2,'zl'=4,'x'=4,'y'=8,'c'=2] {'x'}, dimensions={0} | all-to-all | bytes 393216 | tf_op jit(solution)/shard_map/cond/branch_1_fun/all_to_all | solution.py:345
  45.3 0.2 branch_1_fun.5
  45.5 0.0 copy-start
  45.5 0.0 copy-start.3
  45.5 17.5 %all-gather = bf16[3840,128]{1,0:T(8,128)(2,1)S(1)} all-gather(bf16[240,128]{1,0:T(8,128)(2,1)S(1)} %get-tuple-element.33), channel_id=2, replica_groups=mesh['zh'=2,'zl'=4,'x'=4,'y'=8,'c'=2] {'y','c'}, dimensions={0}, use_global_device_ids=true | all-gather | bytes 1044480 | tf_op jit(solution)/shard_map/all_gather | solution.py:358
  62.9 0.6 shard_map.39
  63.6 14.6 %all_to_all.35.planes = bf16[8,48,128]{2,1,0:T(8,128)(2,1)S(1)} all-to-all(bf16[8,48,128]{2,1,0:T(8,128)(2,1)S(1)} %get-tuple-element.35), channel_id=1, replica_groups=mesh['zh'=2,'zl'=4,'x'=4,'y'=8,'c'=2] {'zh','zl'}, dimensions={0} | all-to-all | bytes 196608 | tf_op jit(solution)/shard_map/all_to_all | solution.py:366
  78.2 0.2 shard_map.40
  78.4 16.3 %all_to_all.36.corr = bf16[16,64,128]{2,1,0:T(8,128)(2,1)S(1)} all-to-all(bf16[16,64,128]{2,1,0:T(8,128)(2,1)S(1)} %shard_map.40), channel_id=1, replica_groups=mesh['zh'=2,'zl'=4,'x'=4,'y'=8,'c'=2] {'y','c'}, dimensions={0} | all-to-all | bytes 524288 | tf_op jit(solution)/shard_map/all_to_all | solution.py:368
  94.7 0.0 copy-done
  94.7 0.0 copy-done.3
  94.7 1.8 %shard_map.41 = bf16[256,2048]{1,0:T(8,128)(2,1)} custom-call(bf16[256,2048]{1,0:T(8,128)(2,1)S(1)} %copy-done.3, bf16[5,128,2048]{2,1,0:T(8,128)(2,1)S(1)} %copy-done, bf16[16,240,128]{2,1,0:T(8,128)(2,1)S(1)} %bitcast.2, bf16[16,64,128]{2,1,0:T(8,128)(2,1)S(1)} %all_to_all.36.corr), custom_call_target="tpu_custom_call" | custom-call | tf_op jit(solution)/shard_map/pallas_call | solution.py:315
  (1 shorter events, 0.0 us)
Async XLA Ops:
  0.0 13.3 %copy-start.2 = (bf16[256,2048]{1,0:T(8,128)(2,1)S(1)}, bf16[256,2048]{1,0:T(8,128)(2,1)}, u32[]{:S(2)}) copy-start(bf16[256,2048]{1,0:T(8,128)(2,1)} %rhs.3) | copy-start | bytes 3145732
  0.0 13.3 %copy-start.1 = (bf16[5,1,128,256]{3,2,1,0:T(8,128)(2,1)S(1)}, bf16[5,1,128,256]{3,2,1,0:T(8,128)(2,1)}, u32[]{:S(2)}) copy-start(bf16[5,1,128,256]{3,2,1,0:T(8,128)(2,1)} %coupling.3) | copy-start | bytes 983044
  3.6 9.7 %collective-permute-start = (bf16[8,160,128]{2,1,0:T(8,128)(2,1)S(1)}, bf16[8,160,128]{2,1,0:T(8,128)(2,1)S(1)}, u32[]{:S(2)}, u32[]{:S(2)}) collective-permute-start(bf16[8,160,128]{2,1,0:T(8,128)(2,1)S(1)} %get-tuple-element.32), channel_id=1, source_target_pairs={{0,1},{1,0},{2,3},{3,2},{4,5},{5,4},{6,7},{7,6},{8,9},{9,8},{10,11... | collective-permute-start | bytes 983048 | tf_op jit(solution)/shard_map/ppermute | solution.py:331
  45.5 49.2 %copy-start = (bf16[5,128,2048]{2,1,0:T(8,128)(2,1)S(1)}, bf16[5,128,2048]{2,1,0:T(8,128)(2,1)}, u32[]{:S(2)}) copy-start(bf16[5,128,2048]{2,1,0:T(8,128)(2,1)} %bases.3) | copy-start | bytes 7864324
  45.5 49.2 %copy-start.3 = (bf16[256,2048]{1,0:T(8,128)(2,1)S(1)}, bf16[256,2048]{1,0:T(8,128)(2,1)}, u32[]{:S(2)}) copy-start(bf16[256,2048]{1,0:T(8,128)(2,1)} %rhs.3) | copy-start | bytes 3145732
